TPU v7x, 32 devices: a whole 2x2x4 slice. The times are simulated.
32 devices in a mesh: dp: 2 (over x), expert: 16 (over z, y, core).
Axes of the slice: x: 2, y: 2, z: 4, core: 2. Of those that a mesh axis runs over, the one named last changes fastest.
Arguments:
- latent: bfloat16 [4096, 1024], P(('dp', 'expert')), may hold values from -6 to 6
- routes: int32 [4096, 8], P(('dp', 'expert')), may hold values from 0 to 15, all different within a row; in each aligned block of 128 rows (0 to 127, 128 to 255, ...) at most 80 rows name the same one
- gates: float32 [4096, 8], P(('dp', 'expert')), may hold values from 0.05 to 0.5
- grad_out: bfloat16 [4096, 4096], P(('dp', 'expert')), may hold values from -6 to 6
- w_out_t: bfloat16 [4096, 1024], P('expert'), may hold values from -0.1875 to 0.1875
- expert_up: bfloat16 [16, 1024, 2048], P('expert'), may hold values from -0.1875 to 0.1875
- expert_down: bfloat16 [16, 2048, 1024], P('expert'), may hold values from -0.125 to 0.125
Outputs:
- mixed: bfloat16 [4096, 4096], P(('dp', 'expert'))
- grad_latent: bfloat16 [4096, 1024], P(('dp', 'expert'))
- grad_w_out: float32 [4096, 1024], P('expert')
Inputs may be any that keep to these rules, and one draw needn't show every extreme that they name: `routes`: within the 128 rows of one device each row names 8 different experts, and no expert is named by more than 80 of those rows; some expert is named by exactly 80 rows of some device.
All inputs are finite; a program needn't handle non-finite values.
Results may differ from a plain program's by a relative error of at most 0.02.
Values may be sent and summed in bfloat16 or wider, within the bound.
No kernel may reach another device: no remote copies, remote signals or barrier semaphores. Data moves between devices by JAX's collectives and lax.ppermute only.
A program may use at most 128 MiB of HBM per device.

v0:
```python
import jax
import jax.numpy as jnp
from jax import lax
from jax.sharding import PartitionSpec as P


def on_device(latent, routes, gates, grad_out, w_out_t, expert_up, expert_down):
    tok_rows = latent.shape[0]
    width = latent.shape[1]
    top_count = routes.shape[1]
    members = lax.axis_size("expert")
    local_experts = expert_up.shape[0]
    all_experts = members * local_experts
    capacity = max(4, tok_rows * top_count * 5 // (4 * all_experts))
    flat = routes.reshape(-1)
    onehot = (flat[:, None] == jnp.arange(all_experts, dtype=jnp.int32)[None, :]).astype(jnp.int32)
    before = jnp.cumsum(onehot, axis=0) - onehot
    slots = jnp.sum(before * onehot, axis=1)
    target = flat * capacity + slots
    repeated = jnp.repeat(latent, top_count, axis=0)
    outgoing = jnp.zeros((all_experts * capacity, width), jnp.bfloat16).at[target].set(repeated)
    outgoing = outgoing.reshape(members, local_experts, capacity, width)
    grad_cols = lax.all_to_all(grad_out, "expert", split_axis=1, concat_axis=0, tiled=True)
    full_weight = lax.all_gather(w_out_t, "expert", axis=0, tiled=True)
    grad_combined = jnp.dot(grad_out, full_weight, preferred_element_type=jnp.float32).astype(
        jnp.bfloat16
    )
    scaled = (
        jnp.repeat(grad_combined, top_count, axis=0).astype(jnp.float32) * gates.reshape(-1, 1)
    ).astype(jnp.bfloat16)
    grad_send = jnp.zeros((all_experts * capacity, width), jnp.bfloat16).at[target].set(scaled)
    grad_send = grad_send.reshape(members, local_experts, capacity, width)
    pre = jnp.einsum(
        "secl,elh->sech",
        lax.all_to_all(outgoing, "expert", split_axis=0, concat_axis=0, tiled=True),
        expert_up,
        preferred_element_type=jnp.float32,
    )
    act = (jnp.maximum(pre, 0.0) ** 2).astype(jnp.bfloat16)
    result = jnp.einsum(
        "sech,ehl->secl", act, expert_down, preferred_element_type=jnp.float32
    ).astype(jnp.bfloat16)
    returned = lax.all_to_all(result, "expert", split_axis=0, concat_axis=0, tiled=True)
    grad_recv = lax.all_to_all(grad_send, "expert", split_axis=0, concat_axis=0, tiled=True)
    grad_act = jnp.einsum(
        "secl,ehl->sech", grad_recv, expert_down, preferred_element_type=jnp.float32
    )
    grad_pre = (grad_act * 2.0 * jnp.maximum(pre, 0.0)).astype(jnp.bfloat16)
    grad_rows = jnp.einsum(
        "sech,elh->secl", grad_pre, expert_up, preferred_element_type=jnp.float32
    ).astype(jnp.bfloat16)
    grad_back = lax.all_to_all(grad_rows, "expert", split_axis=0, concat_axis=0, tiled=True)
    picked = (
        returned.reshape(-1, width)[target].astype(jnp.float32).reshape(tok_rows, top_count, width)
    )
    combined = jnp.sum(picked * gates[:, :, None], axis=1).astype(jnp.bfloat16)
    mixed = lax.dot_general(
        combined, full_weight, (((1,), (1,)), ((), ())), preferred_element_type=jnp.float32
    ).astype(jnp.bfloat16)
    partial_grad = lax.dot_general(
        grad_cols,
        lax.all_gather(combined, "expert", axis=0, tiled=True),
        (((0,), (0,)), ((), ())),
        preferred_element_type=jnp.float32,
    )
    grad_w_out = lax.psum(partial_grad.astype(jnp.bfloat16), "dp").astype(jnp.float32)
    gathered = (
        grad_back.reshape(-1, width)[target].astype(jnp.float32).reshape(tok_rows, top_count, width)
    )
    grad_latent = jnp.sum(gathered, axis=1).astype(jnp.bfloat16)
    return (mixed, grad_latent, grad_w_out)


def solution(mesh):
    in_specs = (
        P(("dp", "expert"), None),
        P(("dp", "expert"), None),
        P(("dp", "expert"), None),
        P(("dp", "expert"), None),
        P("expert", None),
        P("expert", None, None),
        P("expert", None, None),
    )
    out_specs = (P(("dp", "expert"), None), P(("dp", "expert"), None), P("expert", None))
    return jax.shard_map(
        on_device, mesh=mesh, in_specs=in_specs, out_specs=out_specs, check_vma=False
    )
```

profile of v0, /device:TPU:15, one launch (start us, length us, event | category | flops | bytes accessed | tf_op | source)
XLA Modules:
  0.0 409.8 jit_solution(10533256520077443951)
XLA Ops:
  7.2 0.7 all-gather.3.cloned.1.call-update
  7.9 0.8 copy.33
  8.9 0.7 broadcast_multiply_fusion
  9.8 4.5 %reduce-window.6 = s32[16,8,128]{2,1,0:T(8,128)S(1)} reduce-window(s32[16,8,128]{2,1,0:T(8,128)S(1)} %fusion.33, s32[]{:T(128)} %constant.8.clone.1), window={size=1x1x128 pad=0_0x0_0x127_0}, to_apply=%region_0.0 | reduce-window | flops 2080768 | bytes 131076 | tf_op jit(solution)/shard_map/reduce-window
  14.4 0.1 copy.35
  14.8 6.1 %scatter_custom_fusion = bf16[1280,1024]{1,0:T(8,128)(2,1)S(1)} fusion(s32[1024]{0:T(1024)S(1)} %bitcast.95, bf16[]{:T(256)} %constant.6.clone.1, bf16[128,1024]{1,0:T(8,128)(2,1)S(1)} %copy-done), kind=kCustom, calls=%fused_computation.28 | custom fusion | bytes 2883586 | tf_op jit(solution)/shard_map/scatter | solution.py:21
  20.9 108.6 %all_to_all.39 = bf16[16,1,80,1024]{3,2,1,0:T(8,128)(2,1)S(1)} all-to-all(bf16[16,1,80,1024]{3,2,1,0:T(8,128)(2,1)S(1)} %bitcast.89), channel_id=1, replica_groups=mesh['dp'=2,'expert'=16] {'expert'}, dimensions={0} | all-to-all | bytes 5242880 | tf_op jit(solution)/shard_map/all_to_all | solution.py:35
  129.5 5.7 %fusion.11 = f32[16,80,2048]{2,1,0:T(8,128)S(1)} fusion(bf16[1,1024,2048]{2,1,0:T(8,128)(2,1)S(1)} %copy-done.6, bf16[16,1,80,1024]{3,2,1,0:T(8,128)(2,1)S(1)} %all_to_all.39), kind=kOutput, calls=%fused_computation.20 | convolution fusion | flops 5368709120 | bytes 17301504 | tf_op jit(solution)/shard_map/secl,elh->sech/dot_general | solution.py:33
  135.2 4.0 copy-done.8
  139.2 6.9 %convert_bitcast_fusion.1 = bf16[16,1,80,1024]{3,2,1,0:T(8,128)(2,1)} fusion(bf16[1,2048,1024]{2,1,0:T(8,128)(2,1)S(1)} %copy-done.5, f32[16,80,2048]{2,1,0:T(8,128)S(1)} %fusion.11), kind=kOutput, calls=%fused_computation.25 | convolution fusion | flops 5377884160 | bytes 17301504 | tf_op jit(solution)/shard_map/sech,ehl->secl/dot_general | solution.py:40
  146.0 5.2 %all-to-all-start.1 = ((bf16[16,1,80,1024]{3,2,1,0:T(8,128)(2,1)}), bf16[16,1,80,1024]{3,2,1,0:T(8,128)(2,1)S(1)}, u32[]{:S(2)}, u32[]{:S(2)}) async-start(bf16[16,1,80,1024]{3,2,1,0:T(8,128)(2,1)} %convert_bitcast_fusion.1), calls=%async_computation.1 | async-start | bytes 5242880 | tf_op jit(solution)/shard_map/all_to_all | solution.py:43
  151.4 5.0 %fusion.28 = f32[128,1024]{1,0:T(8,128)S(1)} fusion(bf16[128,4096]{1,0:T(8,128)(2,1)} %param.10, bf16[4096,1024]{1,0:T(8,128)(2,1)} %all-gather.3.cloned.1.call-done), kind=kOutput, calls=%fused_computation.37 | convolution fusion | flops 1074003968 | bytes 9961472 | tf_op jit(solution)/shard_map/dot_general | solution.py:25
  156.4 7.5 %scatter_custom_fusion.1 = bf16[1280,1024]{1,0:T(8,128)(2,1)} fusion(s32[1024]{0:T(1024)S(1)} %bitcast.96, f32[1024]{0:T(1024)S(1)} %mul.58, f32[128,1024]{1,0:T(8,128)S(1)} %fusion.28, bf16[]{:T(256)} %constant.6.clone.1), kind=kCustom, calls=%fused_computation.26 | custom fusion | flops 2097152 | bytes 3149826 | tf_op jit(solution)/shard_map/scatter | solution.py:31
  163.9 45.9 %all-to-all-done.1 = bf16[16,1,80,1024]{3,2,1,0:T(8,128)(2,1)S(1)} async-done(((bf16[16,1,80,1024]{3,2,1,0:T(8,128)(2,1)}), bf16[16,1,80,1024]{3,2,1,0:T(8,128)(2,1)S(1)}, u32[]{:S(2)}, u32[]{:S(2)}) %all-to-all-start.1) | async-done | bytes 2621472 | tf_op jit(solution)/shard_map/all_to_all | solution.py:43
  209.9 4.9 %all-to-all-start.2 = ((bf16[16,1,80,1024]{3,2,1,0:T(8,128)(2,1)}), bf16[16,1,80,1024]{3,2,1,0:T(8,128)(2,1)}, u32[]{:S(2)}, u32[]{:S(2)}) async-start(bf16[16,1,80,1024]{3,2,1,0:T(8,128)(2,1)} %bitcast.88), calls=%async_computation.2 | async-start | bytes 5242880 | tf_op jit(solution)/shard_map/all_to_all | solution.py:44
  214.8 5.4 %gather_fusion = bf16[1024,1024]{1,0:T(8,128)(2,1)} fusion(bf16[1280,1024]{1,0:T(8,128)(2,1)S(1)} %bitcast.87, s32[1024]{0:T(1024)S(1)} %broadcast_clamp_fusion), kind=kCustom, calls=%fused_computation | custom fusion | bytes 4198400 | tf_op jit(solution)/shard_map/gather | solution.py:54
  220.2 3.7 fusion.5
  223.9 2.3 copy.41
  226.1 72.7 %all-to-all-done.2 = bf16[16,1,80,1024]{3,2,1,0:T(8,128)(2,1)} async-done(((bf16[16,1,80,1024]{3,2,1,0:T(8,128)(2,1)}), bf16[16,1,80,1024]{3,2,1,0:T(8,128)(2,1)}, u32[]{:S(2)}, u32[]{:S(2)}) %all-to-all-start.2) | async-done | bytes 2621472 | tf_op jit(solution)/shard_map/all_to_all | solution.py:44
  298.8 4.8 %all-to-all-start.4 = ((bf16[128,16,256]{0,2,1:T(8,128)(2,1)}), bf16[128,16,256]{0,2,1:T(8,128)(2,1)S(1)}, u32[]{:S(2)}, u32[]{:S(2)}) async-start(bf16[128,16,256]{0,2,1:T(8,128)(2,1)} %bitcast.26), calls=%async_computation.4 | async-start | bytes 2097152 | tf_op jit(solution)/shard_map/all_to_all | solution.py:23
  303.6 10.8 %fusion.7 = f32[16,80,2048]{2,1,0:T(8,128)} fusion(bf16[1,2048,1024]{2,1,0:T(8,128)(2,1)} %param.13, bf16[16,1,80,1024]{3,2,1,0:T(8,128)(2,1)} %all-to-all-done.2), kind=kOutput, calls=%fused_computation.16 | convolution fusion | flops 5368709120 | bytes 17301504 | tf_op jit(solution)/shard_map/secl,ehl->sech/dot_general | solution.py:45
  314.4 14.1 %convert_bitcast_fusion = bf16[16,1,80,1024]{3,2,1,0:T(8,128)(2,1)} fusion(bf16[1,1024,2048]{2,1,0:T(8,128)(2,1)S(1)} %copy-done.7, f32[16,80,2048]{2,1,0:T(8,128)} %fusion.7, f32[16,80,2048]{2,1,0:T(8,128)} %copy-done.8), kind=kOutput, calls=%fused_computation.24 | convolution fusion | flops 5380505600 | bytes 27787264 | tf_op jit(solution)/shard_map/sech,elh->secl/dot_general | solution.py:49
  328.6 1.0 copy-done.2
  329.6 6.0 %all-to-all-start.3 = ((bf16[16,1,80,1024]{3,2,1,0:T(8,128)(2,1)}), bf16[16,1,80,1024]{3,2,1,0:T(8,128)(2,1)S(1)}, u32[]{:S(2)}, u32[]{:S(2)}) async-start(bf16[16,1,80,1024]{3,2,1,0:T(8,128)(2,1)} %convert_bitcast_fusion), calls=%async_computation.3 | async-start | bytes 5242880 | tf_op jit(solution)/shard_map/all_to_all | solution.py:52
  335.6 2.3 copy.42
  337.9 4.6 %fusion.27 = bf16[256,1024]{0,1:T(8,128)(2,1)} fusion(bf16[2048,1024]{1,0:T(8,128)(2,1)} %all-gather.5.cloned.1.call-done, bf16[2048,256]{1,0:T(8,128)(2,1)} %bitcast.91), kind=kOutput, calls=%fused_computation.35 | convolution fusion | flops 1074003968 | bytes 5767168 | tf_op jit(solution)/shard_map/dot_general | solution.py:60
  342.6 7.2 %convolution_convert_fusion = bf16[128,4096]{1,0:T(8,128)(2,1)} fusion(bf16[128,1024]{1,0:T(8,128)(2,1)S(1)} %copy-done.3, bf16[4096,1024]{1,0:T(8,128)(2,1)} %all-gather.3.cloned.1.call-done), kind=kOutput, calls=%fused_computation.11 | convolution fusion | flops 1074266112 | bytes 9699328 | tf_op jit(solution)/shard_map/dot_general | solution.py:57
  349.8 21.2 %all-reduce.2.cloned.1.call-done = bf16[256,1024]{0,1:T(8,128)(2,1)} async-done(((bf16[256,1024]{0,1:T(8,128)(2,1)}), bf16[256,1024]{0,1:T(8,128)(2,1)}) %all-reduce.2.cloned.1.call-update) | async-done | bytes 524304 | tf_op jit(solution)/shard_map/psum | solution.py:66
  370.9 2.2 copy.43
  373.2 21.1 %all-to-all-done.3 = bf16[16,1,80,1024]{3,2,1,0:T(8,128)(2,1)S(1)} async-done(((bf16[16,1,80,1024]{3,2,1,0:T(8,128)(2,1)}), bf16[16,1,80,1024]{3,2,1,0:T(8,128)(2,1)S(1)}, u32[]{:S(2)}, u32[]{:S(2)}) %all-to-all-start.3) | async-done | bytes 2621472 | tf_op jit(solution)/shard_map/all_to_all | solution.py:52
  394.2 5.3 %gather_fusion.1 = bf16[1024,1024]{1,0:T(8,128)(2,1)} fusion(bf16[1280,1024]{1,0:T(8,128)(2,1)S(1)} %bitcast.86, s32[1024]{0:T(1024)S(1)} %broadcast_clamp_fusion), kind=kCustom, calls=%fused_computation.1 | custom fusion | bytes 4198400 | tf_op jit(solution)/shard_map/gather | solution.py:68
  399.6 3.7 bitcast_reduce_fusion
  (39 shorter events, 1.1 us)
Async XLA Ops:
  7.2 7.6 %copy-start = (bf16[128,1024]{1,0:T(8,128)(2,1)S(1)}, bf16[128,1024]{1,0:T(8,128)(2,1)}, u32[]{:S(2)}) copy-start(bf16[128,1024]{1,0:T(8,128)(2,1)} %param.7) | copy-start | bytes 786436
  7.2 144.2 %all-gather.3.cloned.1.call-start = ((), (), s32[]{:S(2)}) async-start(), calls=%async_computation.5 | async-start | bytes 8912896 | tf_op jit(solution)/shard_map/all_gather | solution.py:24
  20.9 108.6 %copy-start.6 = (bf16[1,1024,2048]{2,1,0:T(8,128)(2,1)S(1)}, bf16[1,1024,2048]{2,1,0:T(8,128)(2,1)}, u32[]{:S(2)}) copy-start(bf16[1,1024,2048]{2,1,0:T(8,128)(2,1)} %param.12) | copy-start | bytes 12582916
  129.5 9.6 %copy-start.5 = (bf16[1,2048,1024]{2,1,0:T(8,128)(2,1)S(1)}, bf16[1,2048,1024]{2,1,0:T(8,128)(2,1)}, u32[]{:S(2)}) copy-start(bf16[1,2048,1024]{2,1,0:T(8,128)(2,1)} %param.13) | copy-start | bytes 12582916
  135.2 4.0 copy-start.8
  146.0 5.2 %copy-start.4 = (f32[128,8]{0,1:T(8,128)S(1)}, f32[128,8]{0,1:T(8,128)}, u32[]{:S(2)}) copy-start(f32[128,8]{0,1:T(8,128)} %param.9) | copy-start | bytes 12292
  146.0 63.8 %all-to-all-start.1 = ((bf16[16,1,80,1024]{3,2,1,0:T(8,128)(2,1)}), bf16[16,1,80,1024]{3,2,1,0:T(8,128)(2,1)S(1)}, u32[]{:S(2)}, u32[]{:S(2)}) async-start(bf16[16,1,80,1024]{3,2,1,0:T(8,128)(2,1)} %convert_bitcast_fusion.1), calls=%async_computation.1 | async-start | bytes 5242880 | tf_op jit(solution)/shard_map/all_to_all | solution.py:43
  209.9 89.0 %all-to-all-start.2 = ((bf16[16,1,80,1024]{3,2,1,0:T(8,128)(2,1)}), bf16[16,1,80,1024]{3,2,1,0:T(8,128)(2,1)}, u32[]{:S(2)}, u32[]{:S(2)}) async-start(bf16[16,1,80,1024]{3,2,1,0:T(8,128)(2,1)} %bitcast.88), calls=%async_computation.2 | async-start | bytes 5242880 | tf_op jit(solution)/shard_map/all_to_all | solution.py:44
  214.8 123.1 %all-gather.5.cloned.1.call-start = ((), (), s32[]{:S(2)}) async-start(), calls=%async_computation.6 | async-start | bytes 4456448 | tf_op jit(solution)/shard_map/all_gather | solution.py:62
  298.8 29.7 %all-to-all-start.4 = ((bf16[128,16,256]{0,2,1:T(8,128)(2,1)}), bf16[128,16,256]{0,2,1:T(8,128)(2,1)S(1)}, u32[]{:S(2)}, u32[]{:S(2)}) async-start(bf16[128,16,256]{0,2,1:T(8,128)(2,1)} %bitcast.26), calls=%async_computation.4 | async-start | bytes 2097152 | tf_op jit(solution)/shard_map/all_to_all | solution.py:23
  303.6 10.8 %copy-start.7 = (bf16[1,1024,2048]{2,1,0:T(8,128)(2,1)S(1)}, bf16[1,1024,2048]{2,1,0:T(8,128)(2,1)}, u32[]{:S(2)}) copy-start(bf16[1,1024,2048]{2,1,0:T(8,128)(2,1)} %param.12) | copy-start | bytes 12582916
  328.6 1.0 copy-start.2
  329.6 64.7 %all-to-all-start.3 = ((bf16[16,1,80,1024]{3,2,1,0:T(8,128)(2,1)}), bf16[16,1,80,1024]{3,2,1,0:T(8,128)(2,1)S(1)}, u32[]{:S(2)}, u32[]{:S(2)}) async-start(bf16[16,1,80,1024]{3,2,1,0:T(8,128)(2,1)} %convert_bitcast_fusion), calls=%async_computation.3 | async-start | bytes 5242880 | tf_op jit(solution)/shard_map/all_to_all | solution.py:52
  335.6 35.4 %all-reduce.2.cloned.1.call-start = ((), (), s32[]{:S(2)}) async-start(), calls=%async_computation.7 | async-start | bytes 1048576 | tf_op jit(solution)/shard_map/psum | solution.py:66
  337.9 4.6 %copy-start.3 = (bf16[128,1024]{1,0:T(8,128)(2,1)S(1)}, bf16[128,1024]{1,0:T(8,128)(2,1)}, u32[]{:S(2)}) copy-start(bf16[128,1024]{1,0:T(8,128)(2,1)} %fusion.5) | copy-start | bytes 786436
  394.2 9.1 %copy-start.1 = (bf16[128,1024]{1,0:T(8,128)(2,1)S(1)}, bf16[128,1024]{1,0:T(8,128)(2,1)}, u32[]{:S(2)}) copy-start(bf16[128,1024]{1,0:T(8,128)(2,1)} %param.7) | copy-start | bytes 786436
Sparse Core Ops, SparseCore 0:
  10.2 113.3 all-gather.2
  224.0 75.0 all-gather.4
  342.7 28.2 all-reduce.1
where the time goes:
time: 411 us; the launch traced here: 410 us
  waiting for transfers between devices  162 us (39%)
  blocking collectives  109 us (27%)
  matrix products  54.3 us (13%)
  local copies, waits for them, and re-layouts  30.2 us (7%)
  starting transfers between devices  21 us (5%)
  other arithmetic  20.3 us (5%)
  between operations  13.9 us (3%)
    all_to_all x1, blocking collectives, on_device(): lax.all_to_all(outgoing, 'expert', split_axis=0, concat_axis=0, tiled=True)  109 us
    all_to_all x1, waiting for transfers between devices, on_device(): lax.all_to_all(grad_send, 'expert', split_axis=0, concat_axis=0, tiled=True)  72.7 us
    all_to_all x1, waiting for transfers between devices, on_device(): lax.all_to_all(result, 'expert', split_axis=0, concat_axis=0, tiled=True)  45.9 us
    psum x1, waiting for transfers between devices, on_device(): lax.psum(partial_grad.astype(jnp.bfloat16), 'dp').astype(jnp.float32)  21.2 us
    all_to_all x1, waiting for transfers between devices, on_device(): lax.all_to_all(grad_rows, 'expert', split_axis=0, concat_axis=0, tiled=True)  21.1 us
    dot_general x1, matrix products, on_device(): jnp.einsum('sech,elh->secl', grad_pre, expert_up, preferred_element_type=...  14.1 us
    dot_general x1, matrix products, on_device(): jnp.einsum('secl,ehl->sech', grad_recv, expert_down, preferred_element_ty...  10.8 us
    unnamed x22, local copies, waits for them, and re-layouts  10.3 us
  transfers between devices with their start and end apart: 7, of which 4 were waited for; matrix products, arithmetic and copies ran while one was open for 22% of the time, Pallas kernels for 0%

commit v1 on v0

v1 whole, which is shorter than its diff:
```python
import functools

import jax
import jax.numpy as jnp
from jax import lax
from jax.experimental import pallas as pl
from jax.experimental.pallas import tpu as pltpu
from jax.sharding import PartitionSpec as P

BF16 = jnp.bfloat16
F32 = jnp.float32
LANES = 128
NN = (((1,), (0,)), ((), ()))
NT = (((1,), (1,)), ((), ()))
TN = (((0,), (0,)), ((), ()))


def dot(a, b, dims=NN):
    return lax.dot_general(a, b, dims, preferred_element_type=F32)


def cost(flops, moved):
    return pl.CostEstimate(flops=int(flops), bytes_accessed=int(moved), transcendentals=0)


def whole(shape):
    return pl.BlockSpec(shape, lambda *_: (0,) * len(shape))


SMEM = pl.BlockSpec(memory_space=pltpu.SMEM)
ANY = pl.BlockSpec(memory_space=pl.ANY)
VMEM_BYTES = 60 * 1024 * 1024


def ring_order(chips):
    return list(range(0, chips, 2)) + list(range(1, chips, 2))[::-1]


def shift(x, chips, step):
    order = ring_order(chips)
    pairs = [
        (2 * order[j] + core, 2 * order[(j + step) % chips] + core)
        for j in range(chips)
        for core in range(2)
    ]
    return lax.ppermute(x, "expert", pairs)


def swap(x, chips):
    return lax.ppermute(x, "expert", [(i, i ^ 1) for i in range(2 * chips)])


def together(*values):
    flat, tree = jax.tree.flatten(values)
    return jax.tree.unflatten(tree, lax.optimization_barrier(flat))


class View:
    def __init__(self, x, low=0, count=None):
        self.x, self.low = x, low
        self.count = x.shape[0] - low if count is None else count

    def rows(self, start, stop):
        return View(self.x, self.low + start, stop - start)

    def value(self):
        return self.x[self.low : self.low + self.count]


def cut(views, start, stop):
    found, base = [], 0
    for v in views:
        low, high = max(start, base), min(stop, base + v.count)
        if low < high:
            found.append(v.rows(low - base, high - base))
        base += v.count
    return found


def join(views):
    values = [v.value() for v in views]
    return values[0] if len(values) == 1 else jnp.concatenate(values, axis=0)


def move_group(blocks, how):
    moved, base, found = how(join([v for b in blocks for v in b])), 0, []
    for b in blocks:
        count = sum(v.count for v in b)
        found.append([View(moved, base, count)])
        base += count
    return found


def ring_step(chips, rings, beside=()):
    sent = [r.send() for r in rings]
    up, down = join([u for u, _ in sent]), join([d for _, d in sent])
    up, down, beside = together(shift(up, chips, 1), shift(down, chips, -1), beside)
    u_base = d_base = 0
    for ring, (u, d) in zip(rings, sent):
        ring.receive(View(up, u_base, u.count), View(down, d_base, d.count))
        u_base, d_base = u_base + u.count, d_base + d.count
    return beside


class Gather:
    def __init__(self, x, chips, cut_row):
        self.half, self.steps, self.cut_row = chips // 2, 0, cut_row
        self.got, self.wire = {0: [View(x)]}, (View(x), View(x))

    def send(self):
        self.steps += 1
        up, down = self.wire
        if self.steps < self.half:
            return up, down
        return up.rows(0, self.cut_row), down.rows(self.cut_row, down.count)

    def receive(self, up, down):
        self.wire = up, down
        if self.steps < self.half:
            self.got[-self.steps], self.got[self.steps] = [up], [down]
        else:
            self.got[self.steps] = [up, down]


def total(terms):
    return functools.reduce(jnp.add, [t.astype(F32) for t in terms])


class Scatter:
    def __init__(self, parts, chips):
        self.half, self.left, self.parts, self.wire = chips // 2, chips // 2, parts, None

    def send(self):
        s, self.left = self.left, self.left - 1
        if s == self.half:
            far = total(self.parts[s]).astype(BF16)
            self.cut_row = far.shape[0] // 2
            up, down = far[: self.cut_row], far[self.cut_row :]
        else:
            (up, down), at = self.wire, self.cut_row
            a, b = total(self.parts[s]), total(self.parts[-s])
            if s == self.half - 1:
                up = jnp.concatenate([a[:at] + up.astype(F32), a[at:]], axis=0)
                down = jnp.concatenate([b[:at], b[at:] + down.astype(F32)], axis=0)
            else:
                up, down = a + up.astype(F32), b + down.astype(F32)
        return View(up.astype(BF16)), View(down.astype(BF16))

    def receive(self, up, down):
        self.wire = up.value(), down.value()

    def sum(self):
        return total(list(self.parts[0]) + list(self.wire))


def local_call(kernel, name, scalars, arrays, outs, scratch, flops, moved):
    return pl.pallas_call(
        kernel,
        in_specs=[SMEM] * len(scalars) + [ANY] * len(arrays),
        out_specs=[ANY] * len(outs),
        out_shape=outs,
        scratch_shapes=scratch,
        compiler_params=pltpu.CompilerParams(vmem_limit_bytes=VMEM_BYTES),
        cost_estimate=cost(flops, moved),
        name=name,
    )(*scalars, *arrays)


class Pieces:
    def __init__(self):
        self.arrays, self.items = [], []

    def add(self, views, slot, to=0):
        for v in views:
            known = [k for k, x in enumerate(self.arrays) if x is v.x]
            if not known:
                self.arrays.append(v.x)
                known = [len(self.arrays) - 1]
            self.items.append((known[0], v.low, v.count, slot, to))
            to += v.count

    def copies(self, refs, buffer, sems, first):
        by_slot = {}
        for i, (k, low, size, slot, to) in enumerate(self.items):
            dst = buffer.at[slot, pl.ds(to, size)]
            src = refs[k].at[pl.ds(low, size), pl.ds(0, buffer.shape[2])]
            copy = pltpu.make_async_copy(src, dst, sems.at[first + i])
            by_slot.setdefault(slot, []).append(copy)
        return by_slot


def start(copies):
    for c in copies:
        c.start()


def wait(copies):
    for c in copies:
        c.wait()


def pair_gates(gate, pair, cap, tokens):
    first = gate[2 * pair * cap : (2 * pair + 1) * cap, :]
    second = gate[(2 * pair + 1) * cap : (2 * pair + 2) * cap, :]
    empty = jnp.zeros((cap, tokens), F32)
    return jnp.concatenate(
        [jnp.concatenate([first, empty], 1), jnp.concatenate([empty, second], 1)], 0
    )


def picks(gate):
    return jnp.where(gate > 0.0, 1.0, 0.0).astype(BF16)


def tile_of(i, tile):
    return pl.ds(pl.multiple_of(i * tile, tile), tile)


def weight_copies(hbm, vmem, sems, first, tile, i):
    here, count = tile_of(i, tile), hbm[0].shape[1] // tile
    return [
        pltpu.make_async_copy(hbm[0].at[:, here], vmem[0].at[:, here], sems.at[first + i]),
        pltpu.make_async_copy(hbm[1].at[here, :], vmem[1].at[here, :], sems.at[first + count + i]),
    ]


def part_copies(both, pair, tokens, part_refs, swap_ref, sems, first):
    return [
        pltpu.make_async_copy(both.at[pair, pl.ds(0, tokens)], part_refs[pair], sems.at[first + 2 * pair]),
        pltpu.make_async_copy(
            both.at[pair, pl.ds(tokens, tokens)],
            swap_ref.at[pl.ds(pair * tokens, tokens)],
            sems.at[first + 2 * pair + 1],
        ),
    ]


def forward_kernel(pairs, cap, tokens, tile, toks, exts, me_ref, *refs):
    n_tok, n_ext = len(toks.arrays), len(exts.arrays)
    tok_refs, ext_refs = refs[:n_tok], refs[n_tok : n_tok + n_ext]
    refs = refs[n_tok + n_ext :]
    n_tok, n_ext = len(toks.items), len(exts.items)
    weights_hbm, (relu_hbm, gate_hbm) = refs[:2], refs[2:4]
    part_refs, swap_ref = refs[4 : 4 + pairs], refs[4 + pairs]
    both, ext, up, down, relu, gate, rows, acc, masks, in_sem, out_sem = refs[5 + pairs :]
    count, tiles = 2 * pairs, up.shape[1] // tile

    ext_in = exts.copies(ext_refs, ext, in_sem, 0)
    tok_in = toks.copies(tok_refs, both, in_sem, n_ext)
    for copies in (*ext_in.values(), *tok_in.values()):
        start(copies)
    first = n_ext + n_tok
    for i in range(tiles):
        start(weight_copies(weights_hbm, (up, down), in_sem, first, tile, i))

    masks[...] = jnp.zeros_like(masks)
    for b in range(count):
        wait(ext_in[b])
        extra = ext[b].astype(F32)
        mine = lax.broadcasted_iota(jnp.int32, extra.shape, 0) == me_ref[0]
        line = jnp.sum(jnp.where(mine, extra, 0.0), axis=0, keepdims=True)
        masks[b : b + 1, :] = (
            line[:, :tokens] + line[:, tokens : 2 * tokens]
        ) + line[:, 2 * tokens : 3 * tokens]
    earlier = (
        lax.broadcasted_iota(jnp.int32, (tokens, tokens), 0)
        < lax.broadcasted_iota(jnp.int32, (tokens, tokens), 1)
    )
    chosen = picks(masks[...])
    slots = dot(chosen, jnp.where(earlier, 1.0, 0.0).astype(BF16)).astype(jnp.int32)
    place = lax.broadcasted_iota(jnp.int32, (cap, tokens), 0)
    for b in range(count):
        gate[b * cap : (b + 1) * cap, :] = jnp.where(
            place == slots[b : b + 1, :], masks[b : b + 1, :], 0.0
        )
    gate_out = pltpu.make_async_copy(gate, gate_hbm, out_sem.at[0])
    gate_out.start()
    for p in range(pairs):
        wait(tok_in[p])
        pick = picks(pair_gates(gate, p, cap, tokens))
        rows[2 * p * cap : (2 * p + 2) * cap, :] = dot(pick, both[p]).astype(BF16)

    def relu_copy(i):
        here = tile_of(i, tile)
        return pltpu.make_async_copy(relu.at[:, here], relu_hbm.at[:, here], out_sem.at[1 + i])

    def hidden_tile(i, begin):
        here = tile_of(i, tile)
        wait(weight_copies(weights_hbm, (up, down), in_sem, first, tile, i))
        pre = jnp.maximum(dot(rows[...], up[:, here]), 0.0)
        relu[:, here] = pre.astype(BF16)
        relu_copy(i).start()
        out = dot((pre * pre).astype(BF16), down[here, :])
        acc[...] = out if begin else acc[...] + out

    hidden_tile(0, True)
    pl.loop(1, tiles)(lambda i: hidden_tile(i, False))

    parts_out = []
    for p in range(pairs):
        scale = pair_gates(gate, p, cap, tokens)
        result = acc[2 * p * cap : (2 * p + 2) * cap, :].astype(BF16).astype(F32)
        scaled = (result * jnp.sum(scale, axis=1, keepdims=True)).astype(BF16)
        both[p] = dot(picks(scale), scaled, TN).astype(BF16)
        out = part_copies(both, p, tokens, part_refs, swap_ref, out_sem, 1 + tiles)
        start(out)
        parts_out += out
    wait(parts_out + [gate_out] + [relu_copy(i) for i in range(tiles)])


def backward_kernel(pairs, cap, tokens, tile, toks, *refs):
    tok_refs, refs = refs[: len(toks.arrays)], refs[len(toks.arrays) :]
    relu_hbm, gate_hbm, weights_hbm = refs[0], refs[1], refs[2:4]
    part_refs, swap_ref = refs[4 : 4 + pairs], refs[4 + pairs]
    both, up, down, relu, gate, rows, acc, in_sem, out_sem = refs[5 + pairs :]
    tiles = up.shape[1] // tile

    gate_in = pltpu.make_async_copy(gate_hbm, gate, in_sem.at[0])
    gate_in.start()
    tok_in = toks.copies(tok_refs, both, in_sem, 1)
    for copies in tok_in.values():
        start(copies)
    first = 1 + len(toks.items)

    def tile_copies(i):
        here = tile_of(i, tile)
        copy = pltpu.make_async_copy(relu_hbm.at[:, here], relu.at[:, here], in_sem.at[first + i])
        return weight_copies(weights_hbm, (up, down), in_sem, first + tiles, tile, i) + [copy]

    for i in range(tiles):
        start(tile_copies(i))

    gate_in.wait()
    for p in range(pairs):
        wait(tok_in[p])
        scale = pair_gates(gate, p, cap, tokens)
        rows[2 * p * cap : (2 * p + 2) * cap, :] = (
            dot(picks(scale), both[p]) * jnp.sum(scale, axis=1, keepdims=True)
        ).astype(BF16)

    def hidden_tile(i, begin):
        here = tile_of(i, tile)
        wait(tile_copies(i))
        grad_act = dot(rows[...], down[here, :], NT)
        grad_pre = (grad_act * 2.0 * relu[:, here].astype(F32)).astype(BF16)
        out = dot(grad_pre, up[:, here], NT)
        acc[...] = out if begin else acc[...] + out

    hidden_tile(0, True)
    pl.loop(1, tiles)(lambda i: hidden_tile(i, False))

    parts_out = []
    for p in range(pairs):
        pick = picks(pair_gates(gate, p, cap, tokens))
        grad_rows = acc[2 * p * cap : (2 * p + 2) * cap, :].astype(BF16)
        both[p] = dot(pick, grad_rows, TN).astype(BF16)
        out = part_copies(both, p, tokens, part_refs, swap_ref, out_sem, 0)
        start(out)
        parts_out += out
    wait(parts_out)


def part_shapes(pairs, tokens, width):
    shapes = [jax.ShapeDtypeStruct((tokens, width), BF16)] * pairs
    return shapes + [jax.ShapeDtypeStruct((pairs * tokens, width), BF16)]


def expert_forward(me, blocks, extra, up, down, cap, tokens):
    pairs, (width, hidden) = len(blocks) // 2, up.shape
    count, tile = len(blocks), min(512, hidden)
    toks, exts = Pieces(), Pieces()
    for b, block in enumerate(blocks):
        toks.add(cut(block, 0, tokens), b // 2, b % 2 * tokens)
        exts.add(cut(block, tokens, tokens + extra), b)
    outs = [
        jax.ShapeDtypeStruct((count * cap, hidden), BF16),
        jax.ShapeDtypeStruct((count * cap, tokens), F32),
    ] + part_shapes(pairs, tokens, width)
    scratch = [
        pltpu.VMEM((pairs, 2 * tokens, width), BF16),
        pltpu.VMEM((count, extra, 3 * tokens), BF16),
        pltpu.VMEM((width, hidden), BF16),
        pltpu.VMEM((hidden, width), BF16),
        pltpu.VMEM((count * cap, hidden), BF16),
        pltpu.VMEM((count * cap, tokens), F32),
        pltpu.VMEM((count * cap, width), BF16),
        pltpu.VMEM((count * cap, width), F32),
        pltpu.VMEM((-(-count // 16) * 16, tokens), F32),
        pltpu.SemaphoreType.DMA((len(toks.items) + len(exts.items) + 2 * (hidden // tile),)),
        pltpu.SemaphoreType.DMA((1 + hidden // tile + count,)),
    ]
    out = local_call(
        functools.partial(forward_kernel, pairs, cap, tokens, tile, toks, exts),
        "expert_forward", [me], [*toks.arrays, *exts.arrays, up, down], outs, scratch,
        4 * count * cap * width * hidden, 4 * width * hidden,
    )
    return out[0], out[1], list(out[2:-1]), out[-1]


def expert_backward(blocks, relu, gate, up, down, cap, tokens):
    pairs, (width, hidden) = len(blocks) // 2, up.shape
    count, tile = len(blocks), min(512, hidden)
    toks = Pieces()
    for b, block in enumerate(blocks):
        toks.add(block, b // 2, b % 2 * tokens)
    scratch = [
        pltpu.VMEM((pairs, 2 * tokens, width), BF16),
        pltpu.VMEM((width, hidden), BF16),
        pltpu.VMEM((hidden, width), BF16),
        pltpu.VMEM((count * cap, hidden), BF16),
        pltpu.VMEM((count * cap, tokens), F32),
        pltpu.VMEM((count * cap, width), BF16),
        pltpu.VMEM((count * cap, width), F32),
        pltpu.SemaphoreType.DMA((1 + len(toks.items) + 3 * (hidden // tile),)),
        pltpu.SemaphoreType.DMA((count,)),
    ]
    out = local_call(
        functools.partial(backward_kernel, pairs, cap, tokens, tile, toks),
        "expert_backward", [], [*toks.arrays, relu, gate, up, down],
        part_shapes(pairs, tokens, width), scratch,
        4 * count * cap * width * hidden, 4 * width * hidden,
    )
    return list(out[:-1]), out[-1]


def columns(offsets, k, rows):
    return pl.ds(pl.multiple_of(offsets[k] * rows, rows), rows)


def narrow_columns(x, cols, rows):
    return x.reshape(x.shape[0], -1, rows)[:, cols, :].reshape(x.shape[0], -1)


def shard_columns(grads, offsets, k, count, rows):
    return jnp.concatenate(
        [grads[0, :, columns(offsets, k, rows)], grads[0, :, columns(offsets, count + k, rows)]], 1
    )


def stacked(mine, other):
    return jnp.concatenate([join(b) for b in (*mine, *other)], axis=0)


def projection_pieces(mine, other, rows):
    pieces = Pieces()
    for k in range(len(mine)):
        pieces.add(mine[k], k, 0)
        pieces.add(other[k], k, rows)
    return pieces


def both_cores(pair, rows):
    pieces = Pieces()
    pieces.add([View(pair[0])], 0, 0)
    pieces.add([View(pair[1])], 0, rows)
    return pieces


def grad_combined_kernel(rows, acts, weights, offsets, *refs):
    n_act, n_weight = len(acts.arrays), len(weights.arrays)
    act_refs, weight_refs = refs[:n_act], refs[n_act : n_act + n_weight]
    own_ref, sib_ref, grads, weight, out, in_sem, out_sem = refs[n_act + n_weight :]
    tokens, count = own_ref.shape[0], weight.shape[0]
    act_in = acts.copies(act_refs, grads, in_sem, 0)[0]
    weight_in = weights.copies(weight_refs, weight, in_sem, len(acts.items))
    start(act_in)
    for k in range(count):
        start(weight_in[k])
    wait(act_in)
    total = jnp.zeros(out.shape, F32)
    for k in range(count):
        wait(weight_in[k])
        total += dot(shard_columns(grads, offsets, k, count, rows), weight[k])
    out[...] = total
    copies = [
        pltpu.make_async_copy(out.at[pl.ds(0, tokens)], own_ref, out_sem.at[0]),
        pltpu.make_async_copy(out.at[pl.ds(tokens, tokens)], sib_ref, out_sem.at[1]),
    ]
    start(copies)
    wait(copies)


def grad_combined_part(offsets, grads, mine, other, rows, width):
    (tokens, features), count = grads[0].shape, len(mine)
    if rows % LANES:
        weight = stacked(mine, other)
        return [dot(narrow_columns(g, offsets, rows), weight) for g in grads]
    acts, weights = both_cores(grads, tokens), projection_pieces(mine, other, rows)
    return local_call(
        functools.partial(grad_combined_kernel, rows, acts, weights),
        "grad_combined", [offsets], [*acts.arrays, *weights.arrays],
        [jax.ShapeDtypeStruct((tokens, width), F32)] * 2,
        [
            pltpu.VMEM((1, 2 * tokens, features), BF16),
            pltpu.VMEM((count, 2 * rows, width), BF16),
            pltpu.VMEM((2 * tokens, width), F32),
            pltpu.SemaphoreType.DMA((len(acts.items) + len(weights.items),)),
            pltpu.SemaphoreType.DMA((2,)),
        ],
        8 * tokens * rows * count * width, 4 * rows * count * width,
    )


def mixed_kernel(rows, acts, weights, *refs):
    n_act, n_weight = len(acts.arrays), len(weights.arrays)
    act_refs, weight_refs = refs[:n_act], refs[n_act : n_act + n_weight]
    own_ref, sib_ref, comb, weight, out, in_sem, out_sem = refs[n_act + n_weight :]
    tokens, count = own_ref.shape[0], weight.shape[0]
    act_in = acts.copies(act_refs, comb, in_sem, 0)[0]
    weight_in = weights.copies(weight_refs, weight, in_sem, len(acts.items))
    start(act_in)
    for k in range(count):
        start(weight_in[k])
    wait(act_in)
    for k in range(count):
        wait(weight_in[k])
        block = dot(comb[0], weight[k], NT).astype(BF16)
        for part in range(2):
            here = slice((part * count + k) * rows, (part * count + k + 1) * rows)
            out[:, here] = block[:, part * rows : (part + 1) * rows]
    copies = [
        pltpu.make_async_copy(out.at[pl.ds(0, tokens)], own_ref, out_sem.at[0]),
        pltpu.make_async_copy(out.at[pl.ds(tokens, tokens)], sib_ref, out_sem.at[1]),
    ]
    start(copies)
    wait(copies)


def mixed_part(combs, mine, other, rows):
    (tokens, width), count = combs[0].shape, len(mine)
    if rows % LANES:
        weight = stacked(mine, other)
        return [dot(c, weight, NT).astype(BF16) for c in combs]
    acts, weights = both_cores(combs, tokens), projection_pieces(mine, other, rows)
    return local_call(
        functools.partial(mixed_kernel, rows, acts, weights),
        "mixed", [], [*acts.arrays, *weights.arrays],
        [jax.ShapeDtypeStruct((tokens, 2 * count * rows), BF16)] * 2,
        [
            pltpu.VMEM((1, 2 * tokens, width), BF16),
            pltpu.VMEM((count, 2 * rows, width), BF16),
            pltpu.VMEM((2 * tokens, 2 * count * rows), BF16),
            pltpu.SemaphoreType.DMA((len(acts.items) + len(weights.items),)),
            pltpu.SemaphoreType.DMA((2,)),
        ],
        8 * tokens * rows * count * width, 4 * rows * count * width,
    )


def place_kernel(count, rows, offsets, own_ref, other_ref, out_ref):
    for k in range(count):
        block = slice(k * rows, (k + 1) * rows)
        out_ref[:, columns(offsets, k, rows)] = own_ref[:, block]
        out_ref[:, columns(offsets, count + k, rows)] = other_ref[:, block]


def place_columns(offsets, own, other, rows):
    count = offsets.shape[0] // 2
    if rows % LANES:
        back = jnp.zeros_like(offsets).at[offsets].set(jnp.arange(2 * count, dtype=offsets.dtype))
        return narrow_columns(jnp.concatenate([own, other], axis=1), back, rows)
    out = jax.ShapeDtypeStruct((own.shape[0], 2 * own.shape[1]), BF16)
    return pl.pallas_call(
        functools.partial(place_kernel, count, rows),
        in_specs=[SMEM, whole(own.shape), whole(other.shape)],
        out_specs=whole(out.shape),
        out_shape=out,
        grid=(1,),
        compiler_params=pltpu.CompilerParams(vmem_limit_bytes=VMEM_BYTES),
        cost_estimate=cost(0, 8 * own.size),
        name="place_columns",
    )(offsets, own, other)


def weight_grad_kernel(grads, combs, core_ref, *refs):
    n_grad, n_comb = len(grads.arrays), len(combs.arrays)
    grad_refs, comb_refs = refs[:n_grad], refs[n_grad : n_grad + n_comb]
    own_ref, sib_ref, grad, comb, out, rounded, in_sem, out_sem = refs[n_grad + n_comb :]
    rows = own_ref.shape[0]
    copies = grads.copies(grad_refs, grad, in_sem, 0)[0]
    copies += combs.copies(comb_refs, comb, in_sem, len(grads.items))[0]
    start(copies)
    wait(copies)
    out[...] = dot(grad[0], comb[0], TN)
    rounded[...] = out[...].astype(BF16)
    own = pl.ds(pl.multiple_of(core_ref[0] * rows, rows), rows)
    sib = pl.ds(pl.multiple_of((1 - core_ref[0]) * rows, rows), rows)
    copies = [
        pltpu.make_async_copy(out.at[own], own_ref, out_sem.at[0]),
        pltpu.make_async_copy(rounded.at[sib], sib_ref, out_sem.at[1]),
    ]
    start(copies)
    wait(copies)


def weight_grad(core, grads, combs):
    (tokens, features), width = grads[0].shape, combs[0][0].x.shape[1]
    grad, comb = Pieces(), Pieces()
    for k, (g, c) in enumerate(zip(grads, combs)):
        grad.add([View(g)], 0, k * tokens)
        comb.add(c, 0, k * tokens)
    count, rows = len(grads), features // 2
    return local_call(
        functools.partial(weight_grad_kernel, grad, comb),
        "weight_grad", [core], [*grad.arrays, *comb.arrays],
        [jax.ShapeDtypeStruct((rows, width), F32), jax.ShapeDtypeStruct((rows, width), BF16)],
        [
            pltpu.VMEM((1, count * tokens, features), BF16),
            pltpu.VMEM((1, count * tokens, width), BF16),
            pltpu.VMEM((features, width), F32),
            pltpu.VMEM((features, width), BF16),
            pltpu.SemaphoreType.DMA((len(grad.items) + len(comb.items),)),
            pltpu.SemaphoreType.DMA((2,)),
        ],
        2 * count * tokens * features * width, 2 * count * tokens * (features + width),
    )


def gate_rows(routes, gates, experts, width):
    chosen = routes.T[None] == jnp.arange(experts, dtype=jnp.int32)[:, None, None]
    gate = jnp.sum(jnp.where(chosen, gates.T[None], 0.0), axis=1)
    high = lax.reduce_precision(gate, 8, 7)
    middle = lax.reduce_precision(gate - high, 8, 7)
    low = gate - high - middle
    terms = jnp.concatenate([high, middle, low], axis=1).astype(BF16)
    return jnp.pad(terms, ((0, 0), (0, width - terms.shape[1])))


def on_device(latent, routes, gates, grad_out, w_out_t, expert_up, expert_down):
    tokens, width = latent.shape
    members = lax.axis_size("expert")
    chips = members // 2
    half = chips // 2
    capacity = max(4, tokens * routes.shape[1] * 5 // (4 * members))
    cap = -(-capacity // 16) * 16
    up_weight, down_weight = expert_up[0], expert_down[0]

    me = lax.axis_index("expert").astype(jnp.int32)
    chip, core = me // 2, me % 2
    position = jnp.where(chip % 2 == 0, chip // 2, chips - 1 - chip // 2)
    dists = [0] + [d for s in range(1, half) for d in (-s, s)] + [half]
    there = (position + jnp.array(dists, jnp.int32)) % chips
    chip_there = jnp.where(there < half, 2 * there, 2 * (chips - 1 - there) + 1)
    own_cols, sib_cols = 2 * chip_there + core, 2 * chip_there + 1 - core
    me, core = me.reshape(1), core.reshape(1)
    groups = [[0, -1, 1]] + [[-s, s] for s in range(2, half)] + [[half]]

    dp, replica = lax.axis_size("dp"), lax.axis_index("dp").astype(jnp.int32)
    shard = w_out_t.shape[0]
    piece = shard // dp
    own_parts = jnp.concatenate([own_cols * 2 + replica, own_cols * 2 + 1 - replica])
    sib_parts = jnp.concatenate([sib_cols * 2 + replica, sib_cols * 2 + 1 - replica])

    def partner(x):
        return lax.ppermute(x, "dp", [(i, (i + 1) % dp) for i in range(dp)])

    def half_rows(which):
        return lax.dynamic_slice_in_dim(w_out_t, which * piece, piece, 0)

    def core_swap(gathered, group, size):
        own = [cut(gathered.got[d], 0, size) for d in group]
        other = move_group(own, lambda x: swap(x, chips))
        return [side for pair in zip(own, other) for side in pair]

    def share_out(group, parts, other, into):
        swapped = swap(other, chips)
        for i, d in enumerate(group):
            into[d] = [parts[i], swapped[i * tokens : (i + 1) * tokens]]

    extra = members
    begin, end = tokens + extra, tokens + extra + piece
    block = jnp.concatenate(
        [latent, gate_rows(routes, gates, members, width), half_rows(replica)], axis=0
    )
    ring = Gather(block, chips, tokens)
    other_half = {0: half_rows(1 - replica)}
    forward, backward, kept = {}, {}, []

    def run_forward(i):
        pairs = core_swap(ring, groups[i], tokens + extra)
        return expert_forward(me, pairs, extra, up_weight, down_weight, cap, tokens)

    def keep_forward(i, out):
        kept.append(out[:2])
        share_out(groups[i], *out[2:], forward)

    def exchange(ds):
        return partner(join([v for d in ds for v in cut(ring.got[d], begin, end)]))

    def keep_half(ds, got):
        for i, d in enumerate(ds):
            other_half[d] = got[i * piece : (i + 1) * piece]

    grads = (grad_out, ring_step(chips, [ring], swap(grad_out, chips)))
    for s in range(2, half + 1):
        ds = [1 - s, s - 1]
        out, got = ring_step(chips, [ring], (run_forward(s - 2), exchange(ds)))
        keep_forward(s - 2, out)
        keep_half(ds, got)

    def column_block(d):
        chip_at = chip_there[dists.index(d)]
        return lax.dynamic_slice_in_dim(grad_out, chip_at * 2 * shard, 2 * shard, 1)

    def send_columns(ds):
        return [shift(column_block(half if d == half else -d), chips, -d) for d in ds]

    ordered = dists[:0:-1]
    first, second = len(ordered) * 3 // 7, len(ordered) * 5 // 7
    col_blocks = {0: column_block(0)}

    out, got, cols = together(
        run_forward(half - 1), exchange([half]), send_columns(ordered[:first])
    )
    keep_forward(half - 1, out)
    keep_half([half], got)
    col_blocks.update(zip(ordered[:first], cols))

    mine = [cut(ring.got[d], begin, end) for d in dists]
    others = [[View(other_half[d])] for d in dists]
    comb = Scatter(forward, chips)
    gc_own, gc_swap = grad_combined_part(own_parts, grads, mine, others, piece, width)
    gc_other, cols = ring_step(
        chips, [comb], (swap(gc_swap, chips), send_columns(ordered[first:second]))
    )
    col_blocks.update(zip(ordered[first:second], cols))
    grad_ring = Gather((gc_own + gc_other).astype(BF16), chips, tokens // 2)

    def run_backward(i):
        pairs = core_swap(grad_ring, groups[i], tokens)
        return expert_backward(pairs, *kept[i], up_weight, down_weight, cap, tokens)

    ring_step(chips, [comb, grad_ring])
    for s in range(2, half):
        out = ring_step(chips, [comb, grad_ring], run_backward(s - 2))
        share_out(groups[s - 2], *out, backward)
    combined = comb.sum().astype(BF16)
    comb_ring = Gather(combined, chips, tokens // 2)
    out = ring_step(chips, [grad_ring, comb_ring], run_backward(half - 2))
    share_out(groups[half - 2], *out, backward)
    out, cols, comb_other = ring_step(
        chips,
        [comb_ring],
        (run_backward(half - 1), send_columns(ordered[second:]), swap(combined, chips)),
    )
    share_out(groups[half - 1], *out, backward)
    col_blocks.update(zip(ordered[second:], cols))

    back = Scatter(backward, chips)
    mixed = mixed_part((combined, comb_other), mine, others, piece)
    mixed = ring_step(chips, [comb_ring, back], mixed)
    beside = swap(mixed[1], chips)
    for _ in range(4, half + 1):
        beside = ring_step(chips, [comb_ring, back], beside)
    places = jnp.concatenate([own_parts, sib_parts])
    mixed = place_columns(places, mixed[0], beside, piece)
    grad_own, grad_sib = weight_grad(
        core, [col_blocks[d] for d in dists], [comb_ring.got[d] for d in dists]
    )
    mixed, grad_own, grad_sib = ring_step(chips, [back], (mixed, grad_own, grad_sib))
    partial = (grad_own + swap(grad_sib, chips).astype(F32)).astype(BF16)
    partial, other = ring_step(chips, [back], (partial, partner(partial)))
    grad_w_out = partial.astype(F32) + other.astype(F32)
    grad_latent = back.sum().astype(BF16)
    return (mixed, grad_latent, grad_w_out)


def solution(mesh):
    rows_split = P(("dp", "expert"), None)
    experts = P("expert", None, None)
    in_specs = (rows_split, rows_split, rows_split, rows_split, P("expert", None), experts, experts)
    out_specs = (rows_split, rows_split, P("expert", None))
    return jax.shard_map(
        on_device, mesh=mesh, in_specs=in_specs, out_specs=out_specs, check_vma=False
    )
```

time: 411 us -> 235 us (0.57)
  the two profiles are of different devices: /device:TPU:15 before, /device:TPU:0 now
where the time goes in v1:
time: 235 us
  Pallas kernels  77.7 us (33%)
  waiting for transfers between devices  74.5 us (32%)
  starting transfers between devices  51 us (22%)
  other arithmetic  12.7 us (5%)
  local copies, waits for them, and re-layouts  11.7 us (5%)
  between operations  6.94 us (3%)
    pallas_call x11, Pallas kernels, local_call(): pl.pallas_call(kernel, in_specs=[SMEM] * len(scalars) + [ANY] * len(array...  75.3 us
    ppermute x35, waiting for transfers between devices, shift(): return lax.ppermute(x, 'expert', pairs)  63.5 us
    ppermute x35, starting transfers between devices, shift(): return lax.ppermute(x, 'expert', pairs)  41.5 us
    ppermute x5, waiting for transfers between devices, partner(): return lax.ppermute(x, 'dp', [(i, (i + 1) % dp) for i in range(dp)])  8.08 us
    ppermute x5, starting transfers between devices, partner(): return lax.ppermute(x, 'dp', [(i, (i + 1) % dp) for i in range(dp)])  5.82 us
  transfers between devices with their start and end apart: 61, of which 25 were waited for; matrix products, arithmetic and copies ran while one was open for 7% of the time, Pallas kernels for 33%

profile of v1, /device:TPU:0, one launch (start us, length us, event | category | flops | bytes accessed | tf_op | source)
XLA Modules:
  0.0 234.5 jit_solution(12082410713155566193)
XLA Ops:
  1.9 1.8 constant_dynamic-slice_fusion.5
  4.7 2.6 %collective-permute-start = (bf16[272,1024]{1,0:T(8,128)(2,1)S(1)}, bf16[272,1024]{1,0:T(8,128)(2,1)S(1)}, u32[]{:S(2)}, u32[]{:S(2)}) collective-permute-start(bf16[272,1024]{1,0:T(8,128)(2,1)S(1)} %pad_maximum_fusion.8.refs_0_.refs_4_.refs_2_), channel_id=1, source_target_pairs={{0,4},{1,5},{4,8},{5,9},{8,12},{9,13},{12,14},{13,15},{14,10},{15,... | collective-permute-start | bytes 1671176 | tf_op jit(solution)/shard_map/ppermute | solution.py:46
  7.4 13.2 %collective-permute-done.refs_2_.refs_6_.refs_4_ = bf16[272,1024]{1,0:T(8,128)(2,1)S(1)} collective-permute-done((bf16[272,1024]{1,0:T(8,128)(2,1)S(1)}, bf16[272,1024]{1,0:T(8,128)(2,1)S(1)}, u32[]{:S(2)}, u32[]{:S(2)}) %collective-permute-start) | collective-permute-done | bytes 557088 | tf_op jit(solution)/shard_map/ppermute | solution.py:46
  26.9 8.8 %expert_forward.4 = (bf16[480,2048]{1,0:T(8,128)(2,1)}, f32[480,128]{1,0:T(8,128)}, bf16[128,1024]{1,0:T(8,128)(2,1)}, bf16[128,1024]{1,0:T(8,128)(2,1)}, bf16[1...) custom-call(s32[1]{0:T(128)} %bitcast.2.me_ref, bf16[272,1024]{1,0:T(8,128)(2,1)} %copy-done.4, ...), custom_call_target="tpu_custom_call" | custom-call | flops 4026531840 | bytes 8388608 | tf_op jit(solution)/shard_map/expert_forward/pallas_call | solution.py:157
  35.7 3.5 %collective-permute-done.6 = bf16[256,1024]{1,0:T(8,128)(2,1)S(1)} collective-permute-done((bf16[256,1024]{1,0:T(8,128)(2,1)S(1)}, bf16[256,1024]{1,0:T(8,128)(2,1)S(1)}, u32[]{:S(2)}, u32[]{:S(2)}) %collective-permute-start.6) | collective-permute-done | bytes 524320 | tf_op jit(solution)/shard_map/ppermute | solution.py:655
  51.6 3.1 %collective-permute-start.20 = (bf16[128,512]{1,0:T(8,128)(2,1)}, bf16[128,512]{1,0:T(8,128)(2,1)S(1)}, u32[]{:S(2)}, u32[]{:S(2)}) collective-permute-start(bf16[128,512]{1,0:T(8,128)(2,1)} %get-tuple-element.251), channel_id=1, source_target_pairs={{0,14},{1,15},{4,10},{5,11},{8,6},{9,7},{12,2},{13,3},{14,0},{15,1... | collective-permute-start | bytes 393224 | tf_op jit(solution)/shard_map/ppermute | solution.py:46
  54.7 7.3 %expert_forward.5 = (bf16[320,2048]{1,0:T(8,128)(2,1)}, f32[320,128]{1,0:T(8,128)}, bf16[128,1024]{1,0:T(8,128)(2,1)}, bf16[128,1024]{1,0:T(8,128)(2,1)}, bf16[256,1024]{1,0:T(8,128)(2,1)}) custom-call(s32[1]{0:T(128)} %bitcast.2.me_ref, bf16[272,1024]{1,0:T(8,128)(2,1)} %copy-done.2, bf16[288,1024]{1,0:T(8,128)(2,1)} %collective-permute-done.10.refs_1_.refs_4_, ...), custom_call_target="tpu_custom_call" | custom-call | flops 2684354560 | bytes 8388608 | tf_op jit(solution)/shard_map/expert_forward/pallas_call | solution.py:157
  63.9 2.0 collective-permute-start.14
  67.3 7.3 %expert_forward.6 = (bf16[320,2048]{1,0:T(8,128)(2,1)}, f32[320,128]{1,0:T(8,128)}, bf16[128,1024]{1,0:T(8,128)(2,1)}, bf16[128,1024]{1,0:T(8,128)(2,1)}, bf16[256,1024]{1,0:T(8,128)(2,1)}) custom-call(s32[1]{0:T(128)} %bitcast.2.me_ref, bf16[272,1024]{1,0:T(8,128)(2,1)} %copy-done.1, bf16[288,1024]{1,0:T(8,128)(2,1)} %copy-done.14, ...), custom_call_target="tpu_custom_call" | custom-call | flops 2684354560 | bytes 8388608 | tf_op jit(solution)/shard_map/expert_forward/pallas_call | solution.py:157
  74.7 3.1 %collective-permute-start.22 = (bf16[128,512]{1,0:T(8,128)(2,1)}, bf16[128,512]{1,0:T(8,128)(2,1)S(1)}, u32[]{:S(2)}, u32[]{:S(2)}) collective-permute-start(bf16[128,512]{1,0:T(8,128)(2,1)} %get-tuple-element.249), channel_id=1, source_target_pairs={{0,12},{1,13},{4,14},{5,15},{8,10},{9,11},{12,6},{13,7},{14,2},{15... | collective-permute-start | bytes 393224 | tf_op jit(solution)/shard_map/ppermute | solution.py:46
  81.0 1.9 fusion.14
  83.7 5.7 %expert_forward.7 = (bf16[160,2048]{1,0:T(8,128)(2,1)}, f32[160,128]{1,0:T(8,128)}, bf16[128,1024]{1,0:T(8,128)(2,1)}, bf16[128,1024]{1,0:T(8,128)(2,1)}) custom-call(s32[1]{0:T(128)} %bitcast.2.me_ref, bf16[128,1024]{1,0:T(8,128)(2,1)} %copy-done.26, bf16[144,1024]{1,0:T(8,128)(2,1)} %copy-done.18, bf16[144,1024]{1,0:T(8,128)(2,1)} %copy-done.7, ...), custom_call_target="tpu_custom_call" | custom-call | flops 1342177280 | bytes 8388608 | tf_op jit(solution)/shard_map/expert_forward/pallas_call | solution.py:157
  89.4 2.5 %collective-permute-start.28 = (bf16[128,512]{1,0:T(8,128)(2,1)S(1)}, bf16[128,512]{1,0:T(8,128)(2,1)S(1)}, u32[]{:S(2)}, u32[]{:S(2)}) collective-permute-start(bf16[128,512]{1,0:T(8,128)(2,1)S(1)} %copy-done.60), channel_id=1, source_target_pairs={{0,8},{1,9},{4,12},{5,13},{8,14},{9,15},{12,10},{13,11},{14,6},{15... | collective-permute-start | bytes 393224 | tf_op jit(solution)/shard_map/ppermute | solution.py:46
  93.3 5.4 %grad_combined.1 = (f32[128,1024]{1,0:T(8,128)}, f32[128,1024]{1,0:T(8,128)}) custom-call(s32[16]{0:T(128)} %pad_add_fusion.offsets, bf16[128,4096]{1,0:T(8,128)(2,1)} %refs_0_.1, bf16[128,4096]{1,0:T(8,128)(2,1)} %collective-permute-done.2.refs_1_, bf16[272,1024]{1,0:T(8,128)(2,1)} %copy-done.4, bf16[128,1024]{1,0:T(8,128)(2,1)} %get-tuple-element.275.refs_3_, ...), custom_call_target="tpu_custom_call" | custom-call | flops 1073741824 | bytes 4194304 | tf_op jit(solution)/shard_map/grad_combined/pallas_call | solution.py:157
  99.0 2.0 collective-permute-start.25
  101.3 3.6 %collective-permute-done.24 = bf16[64,1024]{1,0:T(8,128)(2,1)S(1)} collective-permute-done((bf16[64,1024]{1,0:T(8,128)(2,1)S(1)}, bf16[64,1024]{1,0:T(8,128)(2,1)S(1)}, u32[]{:S(2)}, u32[]{:S(2)}) %collective-permute-start.24) | collective-permute-done | bytes 131104 | tf_op jit(solution)/shard_map/ppermute | solution.py:46
  107.3 11.5 %collective-permute-done.29.refs_2_ = bf16[256,1024]{1,0:T(8,128)(2,1)S(1)} collective-permute-done((bf16[256,1024]{1,0:T(8,128)(2,1)S(1)}, bf16[256,1024]{1,0:T(8,128)(2,1)S(1)}, u32[]{:S(2)}, u32[]{:S(2)}) %collective-permute-start.29) | collective-permute-done | bytes 524320 | tf_op jit(solution)/shard_map/ppermute | solution.py:46
  120.5 1.7 collective-permute-start.32
  122.2 8.9 %expert_backward.4 = (bf16[128,1024]{1,0:T(8,128)(2,1)}, bf16[128,1024]{1,0:T(8,128)(2,1)}, bf16[128,1024]{1,0:T(8,128)(2,1)}, bf16[384,1024]{1,0:T(8,128)(2,1)}) custom-call(bf16[128,1024]{1,0:T(8,128)(2,1)} %copy-done.15, bf16[384,1024]{1,0:T(8,128)(2,1)} %collective-permute-done.33.refs_1_, bf16[256,1024]{1,0:T(8,128)(2,1)} %copy-done.34, ...), custom_call_target="tpu_custom_call" | custom-call | flops 4026531840 | bytes 8388608 | tf_op jit(solution)/shard_map/expert_backward/pallas_call | solution.py:157
  131.1 2.8 %collective-permute-done.31.refs_0_ = bf16[256,1024]{1,0:T(8,128)(2,1)S(1)} collective-permute-done((bf16[256,1024]{1,0:T(8,128)(2,1)S(1)}, bf16[256,1024]{1,0:T(8,128)(2,1)S(1)}, u32[]{:S(2)}, u32[]{:S(2)}) %collective-permute-start.31) | collective-permute-done | bytes 524320 | tf_op jit(solution)/shard_map/ppermute | solution.py:46
  138.1 7.3 %expert_backward.5 = (bf16[128,1024]{1,0:T(8,128)(2,1)}, bf16[128,1024]{1,0:T(8,128)(2,1)}, bf16[256,1024]{1,0:T(8,128)(2,1)}) custom-call(bf16[256,1024]{1,0:T(8,128)(2,1)} %copy-done.16, bf16[256,1024]{1,0:T(8,128)(2,1)} %copy-done.30, bf16[256,1024]{1,0:T(8,128)(2,1)} %copy-done.17, bf16[320,2048]{1,0:T(8,128)(2,1)} %get-tuple-element.182.refs_3_, ...), custom_call_target="tpu_custom_call" | custom-call | flops 2684354560 | bytes 8388608 | tf_op jit(solution)/shard_map/expert_backward/pallas_call | solution.py:157
  145.4 4.1 %collective-permute-done.34.refs_0_ = bf16[256,1024]{1,0:T(8,128)(2,1)S(1)} collective-permute-done((bf16[256,1024]{1,0:T(8,128)(2,1)S(1)}, bf16[256,1024]{1,0:T(8,128)(2,1)S(1)}, u32[]{:S(2)}, u32[]{:S(2)}) %collective-permute-start.34) | collective-permute-done | bytes 524320 | tf_op jit(solution)/shard_map/ppermute | solution.py:46
  154.3 7.3 %expert_backward.6 = (bf16[128,1024]{1,0:T(8,128)(2,1)}, bf16[128,1024]{1,0:T(8,128)(2,1)}, bf16[256,1024]{1,0:T(8,128)(2,1)}) custom-call(bf16[256,1024]{1,0:T(8,128)(2,1)} %copy-done.12, bf16[256,1024]{1,0:T(8,128)(2,1)} %copy-done.29, bf16[256,1024]{1,0:T(8,128)(2,1)} %copy-done.13, bf16[320,2048]{1,0:T(8,128)(2,1)} %get-tuple-element.192.refs_3_, ...), custom_call_target="tpu_custom_call" | custom-call | flops 2684354560 | bytes 8388608 | tf_op jit(solution)/shard_map/expert_backward/pallas_call | solution.py:157
  168.3 6.7 %expert_backward.7 = (bf16[128,1024]{1,0:T(8,128)(2,1)}, bf16[128,1024]{1,0:T(8,128)(2,1)}) custom-call(bf16[192,1024]{1,0:T(8,128)(2,1)} %copy-done.10, bf16[192,1024]{1,0:T(8,128)(2,1)} %copy-done.11, bf16[128,1024]{1,0:T(8,128)(2,1)} %copy-done.39, bf16[160,2048]{1,0:T(8,128)(2,1)} %get-tuple-element.199.refs_3_, f32[160,128]{1,0:T(8,128)} %get-tuple-element.200.refs_4_, ...), custom_call_target="tpu_custom_call" | custom-call | flops 1342177280 | bytes 8388608 | tf_op jit(solution)/shard_map/expert_backward/pallas_call | solution.py:157
  179.3 1.8 collective-permute-start.48
  181.5 6.0 %mixed.1 = (bf16[128,2048]{1,0:T(8,128)(2,1)}, bf16[128,2048]{1,0:T(8,128)(2,1)}) custom-call(bf16[128,1024]{1,0:T(8,128)(2,1)} %copy-done.9, bf16[128,1024]{1,0:T(8,128)(2,1)} %copy-done.52, bf16[272,1024]{1,0:T(8,128)(2,1)} %copy-done.4, bf16[128,1024]{1,0:T(8,128)(2,1)} %get-tuple-element.275.refs_3_, bf16[272,1024]{1,0:T(8,128)(2,1)} %copy-done.5, ...), custom_call_target="tpu_custom_call" | custom-call | flops 1073741824 | bytes 4194304 | tf_op jit(solution)/shard_map/mixed/pallas_call | solution.py:157
  187.7 2.7 %collective-permute-done.48.refs_13_ = bf16[192,1024]{1,0:T(8,128)(2,1)S(1)} collective-permute-done((bf16[192,1024]{1,0:T(8,128)(2,1)S(1)}, bf16[192,1024]{1,0:T(8,128)(2,1)S(1)}, u32[]{:S(2)}, u32[]{:S(2)}) %collective-permute-start.48) | collective-permute-done | bytes 393248 | tf_op jit(solution)/shard_map/ppermute | solution.py:46
  194.4 9.4 %collective-permute-done.51.refs_15_ = bf16[192,1024]{1,0:T(8,128)(2,1)S(1)} collective-permute-done((bf16[192,1024]{1,0:T(8,128)(2,1)S(1)}, bf16[192,1024]{1,0:T(8,128)(2,1)S(1)}, u32[]{:S(2)}, u32[]{:S(2)}) %collective-permute-start.51) | collective-permute-done | bytes 393248 | tf_op jit(solution)/shard_map/ppermute | solution.py:46
  207.8 2.4 %place_columns.1 = bf16[128,4096]{1,0:T(8,128)(2,1)} custom-call(s32[32]{0:T(128)} %pad_add_fusion.1.offsets, bf16[128,2048]{1,0:T(8,128)(2,1)} %get-tuple-element.219.own_ref, bf16[128,2048]{1,0:T(8,128)(2,1)} %copy-done.28), custom_call_target="tpu_custom_call" | custom-call | bytes 2097152 | tf_op jit(solution)/shard_map/place_columns/pallas_call | solution.py:563
  210.3 4.6 %weight_grad.1 = (f32[256,1024]{1,0:T(8,128)}, bf16[256,1024]{1,0:T(8,128)(2,1)}) custom-call(s32[1]{0:T(128)} %bitcast.12.core_ref, bf16[128,512]{1,0:T(8,128)(2,1)} %get-tuple-element.245.refs_0_, bf16[128,512]{1,0:T(8,128)(2,1)} %copy-done.63, bf16[128,512]{1,0:T(8,128)(2,1)} %copy-done.62, bf16[128,512]{1,0:T(8,128)(2,1)} %copy-done.57, ...), custom_call_target="tpu_custom_call" | custom-call | flops 1073741824 | bytes 3145728 | tf_op jit(solution)/shard_map/weight_grad/pallas_call | solution.py:157
  221.4 6.0 %collective-permute-done.57 = bf16[128,1024]{1,0:T(8,128)(2,1)S(1)} collective-permute-done((bf16[128,1024]{1,0:T(8,128)(2,1)S(1)}, bf16[128,1024]{1,0:T(8,128)(2,1)S(1)}, u32[]{:S(2)}, u32[]{:S(2)}) %collective-permute-start.57) | collective-permute-done | bytes 262176 | tf_op jit(solution)/shard_map/ppermute | solution.py:46
  227.9 4.6 %collective-permute-done.60 = bf16[256,1024]{1,0:T(8,128)(2,1)S(1)} collective-permute-done((bf16[256,1024]{1,0:T(8,128)(2,1)S(1)}, bf16[256,1024]{1,0:T(8,128)(2,1)S(1)}, u32[]{:S(2)}, u32[]{:S(2)}) %collective-permute-start.60) | collective-permute-done | bytes 524320 | tf_op jit(solution)/shard_map/ppermute | solution.py:655
  (321 shorter events, 65.9 us)
Async XLA Ops:
  0.6 21.5 %collective-permute-start.2 = (bf16[128,4096]{1,0:T(8,128)(2,1)}, bf16[128,4096]{1,0:T(8,128)(2,1)}, u32[]{:S(2)}, u32[]{:S(2)}) collective-permute-start(bf16[128,4096]{1,0:T(8,128)(2,1)} %refs_0_.1), channel_id=1, source_target_pairs={{0,1},{1,0},{2,3},{3,2},{4,5},{5,4},{6,7},{7,6},{8,9},{9,8},{10,11... | collective-permute-start | bytes 3145736 | tf_op jit(solution)/shard_map/ppermute | solution.py:50
  4.7 15.9 %collective-permute-start = (bf16[272,1024]{1,0:T(8,128)(2,1)S(1)}, bf16[272,1024]{1,0:T(8,128)(2,1)S(1)}, u32[]{:S(2)}, u32[]{:S(2)}) collective-permute-start(bf16[272,1024]{1,0:T(8,128)(2,1)S(1)} %pad_maximum_fusion.8.refs_0_.refs_4_.refs_2_), channel_id=1, source_target_pairs={{0,4},{1,5},{4,8},{5,9},{8,12},{9,13},{12,14},{13,15},{14,10},{15,... | collective-permute-start | bytes 1671176 | tf_op jit(solution)/shard_map/ppermute | solution.py:46
  7.4 14.7 %collective-permute-start.1 = (bf16[272,1024]{1,0:T(8,128)(2,1)S(1)}, bf16[272,1024]{1,0:T(8,128)(2,1)S(1)}, u32[]{:S(2)}, u32[]{:S(2)}) collective-permute-start(bf16[272,1024]{1,0:T(8,128)(2,1)S(1)} %pad_maximum_fusion.8.refs_0_.refs_4_.refs_2_), channel_id=1, source_target_pairs={{0,2},{1,3},{4,0},{5,1},{8,4},{9,5},{12,8},{13,9},{14,12},{15,13},... | collective-permute-start | bytes 1671176 | tf_op jit(solution)/shard_map/ppermute | solution.py:46
  23.2 16.0 %collective-permute-start.3 = (bf16[272,1024]{1,0:T(8,128)(2,1)S(1)}, bf16[272,1024]{1,0:T(8,128)(2,1)S(1)}, u32[]{:S(2)}, u32[]{:S(2)}) collective-permute-start(bf16[272,1024]{1,0:T(8,128)(2,1)S(1)} %collective-permute-done.refs_2_.refs_6_.refs_4_), channel_id=1, source_target_pairs={{0,4},{1,5},{4,8},{5,9},{8,12},{9,13},{12,14},{13,15},{14,10},{15,... | collective-permute-start | bytes 1671176 | tf_op jit(solution)/shard_map/ppermute | solution.py:46
  24.8 14.8 %collective-permute-start.4 = (bf16[272,1024]{1,0:T(8,128)(2,1)S(1)}, bf16[272,1024]{1,0:T(8,128)(2,1)S(1)}, u32[]{:S(2)}, u32[]{:S(2)}) collective-permute-start(bf16[272,1024]{1,0:T(8,128)(2,1)S(1)} %collective-permute-done.1.refs_3_.refs_7_.refs_6_), channel_id=1, source_target_pairs={{0,2},{1,3},{4,0},{5,1},{8,4},{9,5},{12,8},{13,9},{14,12},{15,13},... | collective-permute-start | bytes 1671176 | tf_op jit(solution)/shard_map/ppermute | solution.py:46
  25.4 13.8 %collective-permute-start.6 = (bf16[256,1024]{1,0:T(8,128)(2,1)S(1)}, bf16[256,1024]{1,0:T(8,128)(2,1)S(1)}, u32[]{:S(2)}, u32[]{:S(2)}) collective-permute-start(bf16[256,1024]{1,0:T(8,128)(2,1)S(1)} %pad_maximum_fusion.9), channel_id=1, source_target_pairs={{0,16},{16,0},{1,17},{17,1},{2,18},{18,2},{3,19},{19,3},{4,20},{20... | collective-permute-start | bytes 1572872 | tf_op jit(solution)/shard_map/ppermute | solution.py:655
  39.6 22.6 %collective-permute-start.9 = (bf16[272,1024]{1,0:T(8,128)(2,1)S(1)}, bf16[272,1024]{1,0:T(8,128)(2,1)S(1)}, u32[]{:S(2)}, u32[]{:S(2)}) collective-permute-start(bf16[272,1024]{1,0:T(8,128)(2,1)S(1)} %collective-permute-done.4.refs_2_.refs_5_.refs_10_), channel_id=1, source_target_pairs={{0,2},{1,3},{4,0},{5,1},{8,4},{9,5},{12,8},{13,9},{14,12},{15,13},... | collective-permute-start | bytes 1671176 | tf_op jit(solution)/shard_map/ppermute | solution.py:46
  40.1 22.0 %collective-permute-start.8 = (bf16[272,1024]{1,0:T(8,128)(2,1)S(1)}, bf16[272,1024]{1,0:T(8,128)(2,1)S(1)}, u32[]{:S(2)}, u32[]{:S(2)}) collective-permute-start(bf16[272,1024]{1,0:T(8,128)(2,1)S(1)} %collective-permute-done.3.refs_0_.refs_3_.refs_8_), channel_id=1, source_target_pairs={{0,4},{1,5},{4,8},{5,9},{8,12},{9,13},{12,14},{13,15},{14,10},{15,... | collective-permute-start | bytes 1671176 | tf_op jit(solution)/shard_map/ppermute | solution.py:46
  42.7 12.1 %collective-permute-start.10 = (bf16[288,1024]{1,0:T(8,128)(2,1)}, bf16[288,1024]{1,0:T(8,128)(2,1)}, u32[]{:S(2)}, u32[]{:S(2)}) collective-permute-start(bf16[288,1024]{1,0:T(8,128)(2,1)} %pad_maximum_fusion.6), channel_id=1, source_target_pairs={{0,1},{1,0},{2,3},{3,2},{4,5},{5,4},{6,7},{7,6},{8,9},{9,8},{10,11... | collective-permute-start | bytes 1769480 | tf_op jit(solution)/shard_map/ppermute | solution.py:50
  43.5 18.6 %collective-permute-start.11 = (bf16[256,1024]{1,0:T(8,128)(2,1)}, bf16[256,1024]{1,0:T(8,128)(2,1)}, u32[]{:S(2)}, u32[]{:S(2)}) collective-permute-start(bf16[256,1024]{1,0:T(8,128)(2,1)} %pad_maximum_fusion.10), channel_id=1, source_target_pairs={{0,16},{16,0},{1,17},{17,1},{2,18},{18,2},{3,19},{19,3},{4,20},{20... | collective-permute-start | bytes 1572872 | tf_op jit(solution)/shard_map/ppermute | solution.py:655
  51.6 37.8 %collective-permute-start.20 = (bf16[128,512]{1,0:T(8,128)(2,1)}, bf16[128,512]{1,0:T(8,128)(2,1)S(1)}, u32[]{:S(2)}, u32[]{:S(2)}) collective-permute-start(bf16[128,512]{1,0:T(8,128)(2,1)} %get-tuple-element.251), channel_id=1, source_target_pairs={{0,14},{1,15},{4,10},{5,11},{8,6},{9,7},{12,2},{13,3},{14,0},{15,1... | collective-permute-start | bytes 393224 | tf_op jit(solution)/shard_map/ppermute | solution.py:46
  63.2 15.3 %collective-permute-start.16 = (bf16[256,1024]{1,0:T(8,128)(2,1)S(1)}, bf16[256,1024]{1,0:T(8,128)(2,1)S(1)}, u32[]{:S(2)}, u32[]{:S(2)}) collective-permute-start(bf16[256,1024]{1,0:T(8,128)(2,1)S(1)} %pad_maximum_fusion.11), channel_id=1, source_target_pairs={{0,16},{16,0},{1,17},{17,1},{2,18},{18,2},{3,19},{19,3},{4,20},{20... | collective-permute-start | bytes 1572872 | tf_op jit(solution)/shard_map/ppermute | solution.py:655
  63.9 14.7 %collective-permute-start.14 = (bf16[144,1024]{1,0:T(8,128)(2,1)S(1)}, bf16[144,1024]{1,0:T(8,128)(2,1)S(1)}, u32[]{:S(2)}, u32[]{:S(2)}) collective-permute-start(bf16[144,1024]{1,0:T(8,128)(2,1)S(1)} %get-tuple-element.260), channel_id=1, source_target_pairs={{0,2},{1,3},{4,0},{5,1},{8,4},{9,5},{12,8},{13,9},{14,12},{15,13},... | collective-permute-start | bytes 884744 | tf_op jit(solution)/shard_map/ppermute | solution.py:46
  66.5 25.3 %collective-permute-start.21 = (bf16[128,512]{1,0:T(8,128)(2,1)}, bf16[128,512]{1,0:T(8,128)(2,1)S(1)}, u32[]{:S(2)}, u32[]{:S(2)}) collective-permute-start(bf16[128,512]{1,0:T(8,128)(2,1)} %get-tuple-element.250), channel_id=1, source_target_pairs={{0,10},{1,11},{4,6},{5,7},{8,2},{9,3},{12,0},{13,1},{14,4},{15,5},... | collective-permute-start | bytes 393224 | tf_op jit(solution)/shard_map/ppermute | solution.py:46
  74.7 17.2 %collective-permute-start.22 = (bf16[128,512]{1,0:T(8,128)(2,1)}, bf16[128,512]{1,0:T(8,128)(2,1)S(1)}, u32[]{:S(2)}, u32[]{:S(2)}) collective-permute-start(bf16[128,512]{1,0:T(8,128)(2,1)} %get-tuple-element.249), channel_id=1, source_target_pairs={{0,12},{1,13},{4,14},{5,15},{8,10},{9,11},{12,6},{13,7},{14,2},{15... | collective-permute-start | bytes 393224 | tf_op jit(solution)/shard_map/ppermute | solution.py:46
  79.5 12.4 %collective-permute-start.19 = (bf16[128,1024]{1,0:T(8,128)(2,1)S(1)}, bf16[128,1024]{1,0:T(8,128)(2,1)S(1)}, u32[]{:S(2)}, u32[]{:S(2)}) collective-permute-start(bf16[128,1024]{1,0:T(8,128)(2,1)S(1)} %slice.269), channel_id=1, source_target_pairs={{0,16},{16,0},{1,17},{17,1},{2,18},{18,2},{3,19},{19,3},{4,20},{20... | collective-permute-start | bytes 786440 | tf_op jit(solution)/shard_map/ppermute | solution.py:655
  82.9 18.3 %collective-permute-start.27 = (bf16[128,512]{1,0:T(8,128)(2,1)S(1)}, bf16[128,512]{1,0:T(8,128)(2,1)S(1)}, u32[]{:S(2)}, u32[]{:S(2)}) collective-permute-start(bf16[128,512]{1,0:T(8,128)(2,1)S(1)} %copy-done.61), channel_id=1, source_target_pairs={{0,6},{1,7},{4,2},{5,3},{8,0},{9,1},{12,4},{13,5},{14,8},{15,9},{1... | collective-permute-start | bytes 393224 | tf_op jit(solution)/shard_map/ppermute | solution.py:46
  89.4 11.9 %collective-permute-start.28 = (bf16[128,512]{1,0:T(8,128)(2,1)S(1)}, bf16[128,512]{1,0:T(8,128)(2,1)S(1)}, u32[]{:S(2)}, u32[]{:S(2)}) collective-permute-start(bf16[128,512]{1,0:T(8,128)(2,1)S(1)} %copy-done.60), channel_id=1, source_target_pairs={{0,8},{1,9},{4,12},{5,13},{8,14},{9,15},{12,10},{13,11},{14,6},{15... | collective-permute-start | bytes 393224 | tf_op jit(solution)/shard_map/ppermute | solution.py:46
  105.2 13.6 %collective-permute-start.29 = (bf16[256,1024]{1,0:T(8,128)(2,1)S(1)}, bf16[256,1024]{1,0:T(8,128)(2,1)S(1)}, u32[]{:S(2)}, u32[]{:S(2)}) collective-permute-start(bf16[256,1024]{1,0:T(8,128)(2,1)S(1)} %get-tuple-element.285), channel_id=1, source_target_pairs={{0,4},{1,5},{4,8},{5,9},{8,12},{9,13},{12,14},{13,15},{14,10},{15,... | collective-permute-start | bytes 1572872 | tf_op jit(solution)/shard_map/ppermute | solution.py:46
  105.6 13.4 %collective-permute-start.30 = (bf16[256,1024]{1,0:T(8,128)(2,1)S(1)}, bf16[256,1024]{1,0:T(8,128)(2,1)S(1)}, u32[]{:S(2)}, u32[]{:S(2)}) collective-permute-start(bf16[256,1024]{1,0:T(8,128)(2,1)S(1)} %get-tuple-element.284), channel_id=1, source_target_pairs={{0,2},{1,3},{4,0},{5,1},{8,4},{9,5},{12,8},{13,9},{14,12},{15,13},... | collective-permute-start | bytes 1572872 | tf_op jit(solution)/shard_map/ppermute | solution.py:46
  107.3 12.3 %collective-permute-start.12 = (bf16[256,1024]{1,0:T(8,128)(2,1)S(1)}, bf16[256,1024]{1,0:T(8,128)(2,1)S(1)}, u32[]{:S(2)}, u32[]{:S(2)}) collective-permute-start(bf16[256,1024]{1,0:T(8,128)(2,1)S(1)} %copy-done.66), channel_id=1, source_target_pairs={{0,1},{1,0},{2,3},{3,2},{4,5},{5,4},{6,7},{7,6},{8,9},{9,8},{10,11... | collective-permute-start | bytes 1572872 | tf_op jit(solution)/shard_map/ppermute | solution.py:50
  119.2 15.0 %collective-permute-start.7 = (bf16[384,1024]{1,0:T(8,128)(2,1)}, bf16[384,1024]{1,0:T(8,128)(2,1)S(1)}, u32[]{:S(2)}, u32[]{:S(2)}) collective-permute-start(bf16[384,1024]{1,0:T(8,128)(2,1)} %get-tuple-element.132), channel_id=1, source_target_pairs={{0,1},{1,0},{2,3},{3,2},{4,5},{5,4},{6,7},{7,6},{8,9},{9,8},{10,11... | collective-permute-start | bytes 2359304 | tf_op jit(solution)/shard_map/ppermute | solution.py:50
  120.0 14.0 %collective-permute-start.31 = (bf16[256,1024]{1,0:T(8,128)(2,1)S(1)}, bf16[256,1024]{1,0:T(8,128)(2,1)S(1)}, u32[]{:S(2)}, u32[]{:S(2)}) collective-permute-start(bf16[256,1024]{1,0:T(8,128)(2,1)S(1)} %pad_maximum_fusion.12), channel_id=1, source_target_pairs={{0,4},{1,5},{4,8},{5,9},{8,12},{9,13},{12,14},{13,15},{14,10},{15,... | collective-permute-start | bytes 1572872 | tf_op jit(solution)/shard_map/ppermute | solution.py:46
  120.5 13.7 %collective-permute-start.32 = (bf16[256,1024]{1,0:T(8,128)(2,1)S(1)}, bf16[256,1024]{1,0:T(8,128)(2,1)S(1)}, u32[]{:S(2)}, u32[]{:S(2)}) collective-permute-start(bf16[256,1024]{1,0:T(8,128)(2,1)S(1)} %pad_maximum_fusion.13), channel_id=1, source_target_pairs={{0,2},{1,3},{4,0},{5,1},{8,4},{9,5},{12,8},{13,9},{14,12},{15,13},... | collective-permute-start | bytes 1572872 | tf_op jit(solution)/shard_map/ppermute | solution.py:46
  135.2 14.3 %collective-permute-start.34 = (bf16[256,1024]{1,0:T(8,128)(2,1)S(1)}, bf16[256,1024]{1,0:T(8,128)(2,1)S(1)}, u32[]{:S(2)}, u32[]{:S(2)}) collective-permute-start(bf16[256,1024]{1,0:T(8,128)(2,1)S(1)} %get-tuple-element.282), channel_id=1, source_target_pairs={{0,4},{1,5},{4,8},{5,9},{8,12},{9,13},{12,14},{13,15},{14,10},{15,... | collective-permute-start | bytes 1572872 | tf_op jit(solution)/shard_map/ppermute | solution.py:46
  136.5 14.0 %collective-permute-start.35 = (bf16[256,1024]{1,0:T(8,128)(2,1)S(1)}, bf16[256,1024]{1,0:T(8,128)(2,1)S(1)}, u32[]{:S(2)}, u32[]{:S(2)}) collective-permute-start(bf16[256,1024]{1,0:T(8,128)(2,1)S(1)} %get-tuple-element.283), channel_id=1, source_target_pairs={{0,2},{1,3},{4,0},{5,1},{8,4},{9,5},{12,8},{13,9},{14,12},{15,13},... | collective-permute-start | bytes 1572872 | tf_op jit(solution)/shard_map/ppermute | solution.py:46
  163.6 12.7 %collective-permute-start.46 = (bf16[128,1024]{1,0:T(8,128)(2,1)S(1)}, bf16[128,1024]{1,0:T(8,128)(2,1)S(1)}, u32[]{:S(2)}, u32[]{:S(2)}) collective-permute-start(bf16[128,1024]{1,0:T(8,128)(2,1)S(1)} %add_convert_fusion.7.refs_0_.refs_8_), channel_id=1, source_target_pairs={{0,1},{1,0},{2,3},{3,2},{4,5},{5,4},{6,7},{7,6},{8,9},{9,8},{10,11... | collective-permute-start | bytes 786440 | tf_op jit(solution)/shard_map/ppermute | solution.py:50
  164.1 12.2 %collective-permute-start.41 = (bf16[128,1024]{1,0:T(8,128)(2,1)S(1)}, bf16[128,1024]{1,0:T(8,128)(2,1)S(1)}, u32[]{:S(2)}, u32[]{:S(2)}) collective-permute-start(bf16[128,1024]{1,0:T(8,128)(2,1)S(1)} %slice.305), channel_id=1, source_target_pairs={{0,4},{1,5},{4,8},{5,9},{8,12},{9,13},{12,14},{13,15},{14,10},{15,... | collective-permute-start | bytes 786440 | tf_op jit(solution)/shard_map/ppermute | solution.py:46
  181.4 23.4 %collective-permute-start.37 = (bf16[256,1024]{1,0:T(8,128)(2,1)}, bf16[256,1024]{1,0:T(8,128)(2,1)S(1)}, u32[]{:S(2)}, u32[]{:S(2)}) collective-permute-start(bf16[256,1024]{1,0:T(8,128)(2,1)} %get-tuple-element.188), channel_id=1, source_target_pairs={{0,1},{1,0},{2,3},{3,2},{4,5},{5,4},{6,7},{7,6},{8,9},{9,8},{10,11... | collective-permute-start | bytes 1572872 | tf_op jit(solution)/shard_map/ppermute | solution.py:50
  192.1 12.7 %collective-permute-start.53 = (bf16[128,2048]{1,0:T(8,128)(2,1)S(1)}, bf16[128,2048]{1,0:T(8,128)(2,1)S(1)}, u32[]{:S(2)}, u32[]{:S(2)}) collective-permute-start(bf16[128,2048]{1,0:T(8,128)(2,1)S(1)} %copy-done.67), channel_id=1, source_target_pairs={{0,1},{1,0},{2,3},{3,2},{4,5},{5,4},{6,7},{7,6},{8,9},{9,8},{10,11... | collective-permute-start | bytes 1572872 | tf_op jit(solution)/shard_map/ppermute | solution.py:50
  192.2 11.6 %collective-permute-start.51 = (bf16[192,1024]{1,0:T(8,128)(2,1)S(1)}, bf16[192,1024]{1,0:T(8,128)(2,1)S(1)}, u32[]{:S(2)}, u32[]{:S(2)}) collective-permute-start(bf16[192,1024]{1,0:T(8,128)(2,1)S(1)} %pad_maximum_fusion.20), channel_id=1, source_target_pairs={{0,4},{1,5},{4,8},{5,9},{8,12},{9,13},{12,14},{13,15},{14,10},{15,... | collective-permute-start | bytes 1179656 | tf_op jit(solution)/shard_map/ppermute | solution.py:46
  218.5 14.0 %collective-permute-start.60 = (bf16[256,1024]{1,0:T(8,128)(2,1)S(1)}, bf16[256,1024]{1,0:T(8,128)(2,1)S(1)}, u32[]{:S(2)}, u32[]{:S(2)}) collective-permute-start(bf16[256,1024]{1,0:T(8,128)(2,1)S(1)} %add_convert_fusion), channel_id=1, source_target_pairs={{0,16},{16,0},{1,17},{17,1},{2,18},{18,2},{3,19},{19,3},{4,20},{20... | collective-permute-start | bytes 1572872 | tf_op jit(solution)/shard_map/ppermute | solution.py:655
  (97 other events, 625.2 us)

commit v2 on v1

--- a/solution.py
+++ b/solution.py
@@ -547,6 +547,34 @@
     )
 
 
+def column_blocks_kernel(chip_ref, grad_ref, *refs):
+    outs, (grad, in_sem, out_sem) = refs[:-3], refs[-3:]
+    fetch = pltpu.make_async_copy(grad_ref, grad, in_sem.at[0])
+    fetch.start()
+    fetch.wait()
+    copies = []
+    for k, out in enumerate(outs):
+        size = out.shape[1]
+        here = pl.ds(pl.multiple_of(chip_ref[k] * size, size), size)
+        copies.append(pltpu.make_async_copy(grad.at[:, here], out, out_sem.at[k]))
+    start(copies)
+    wait(copies)
+
+
+def column_blocks(chip_there, grad_out, size):
+    count = chip_there.shape[0]
+    return local_call(
+        column_blocks_kernel, "column_blocks", [chip_there], [grad_out],
+        [jax.ShapeDtypeStruct((grad_out.shape[0], size), BF16)] * count,
+        [
+            pltpu.VMEM(grad_out.shape, BF16),
+            pltpu.SemaphoreType.DMA((1,)),
+            pltpu.SemaphoreType.DMA((count,)),
+        ],
+        0, 4 * grad_out.size,
+    )
+
+
 def place_kernel(count, rows, offsets, own_ref, other_ref, out_ref):
     for k in range(count):
         block = slice(k * rows, (k + 1) * rows)
@@ -654,11 +682,13 @@
     def partner(x):
         return lax.ppermute(x, "dp", [(i, (i + 1) % dp) for i in range(dp)])
 
-    def half_rows(which):
-        return lax.dynamic_slice_in_dim(w_out_t, which * piece, piece, 0)
+    def half_rows(shard_rows, which):
+        if dp == 2:
+            return jnp.where(which == 0, shard_rows[:piece], shard_rows[piece:])
+        return lax.dynamic_slice_in_dim(shard_rows, which * piece, piece, 0)
 
     def core_swap(gathered, group, size):
-        own = [cut(gathered.got[d], 0, size) for d in group]
+        own = [cut(gathered.got[d], 0, size) for d in group if d]
         other = move_group(own, lambda x: swap(x, chips))
         return [side for pair in zip(own, other) for side in pair]
 
@@ -670,14 +700,15 @@
     extra = members
     begin, end = tokens + extra, tokens + extra + piece
     block = jnp.concatenate(
-        [latent, gate_rows(routes, gates, members, width), half_rows(replica)], axis=0
+        [latent, gate_rows(routes, gates, members, width), half_rows(w_out_t, replica)], axis=0
     )
     ring = Gather(block, chips, tokens)
-    other_half = {0: half_rows(1 - replica)}
     forward, backward, kept = {}, {}, []
 
     def run_forward(i):
         pairs = core_swap(ring, groups[i], tokens + extra)
+        if i == 0:
+            pairs = [[View(block)], [View(block_sib)]] + pairs
         return expert_forward(me, pairs, extra, up_weight, down_weight, cap, tokens)
 
     def keep_forward(i, out):
@@ -691,23 +722,26 @@
         for i, d in enumerate(ds):
             other_half[d] = got[i * piece : (i + 1) * piece]
 
-    grads = (grad_out, ring_step(chips, [ring], swap(grad_out, chips)))
+    blocks = column_blocks(chip_there, grad_out, 2 * shard)
+    grad_sib, block_sib, blocks, shard_rows = ring_step(
+        chips,
+        [ring],
+        (swap(grad_out, chips), swap(block[: tokens + extra], chips), blocks, w_out_t),
+    )
+    grads = (grad_out, grad_sib)
+    other_half = {0: half_rows(shard_rows, 1 - replica)}
     for s in range(2, half + 1):
         ds = [1 - s, s - 1]
         out, got = ring_step(chips, [ring], (run_forward(s - 2), exchange(ds)))
         keep_forward(s - 2, out)
         keep_half(ds, got)
 
-    def column_block(d):
-        chip_at = chip_there[dists.index(d)]
-        return lax.dynamic_slice_in_dim(grad_out, chip_at * 2 * shard, 2 * shard, 1)
-
     def send_columns(ds):
-        return [shift(column_block(half if d == half else -d), chips, -d) for d in ds]
+        return [shift(blocks[dists.index(half if d == half else -d)], chips, -d) for d in ds]
 
     ordered = dists[:0:-1]
     first, second = len(ordered) * 3 // 7, len(ordered) * 5 // 7
-    col_blocks = {0: column_block(0)}
+    col_blocks = {0: blocks[0]}
 
     out, got, cols = together(
         run_forward(half - 1), exchange([half]), send_columns(ordered[:first])
@@ -724,13 +758,16 @@
         chips, [comb], (swap(gc_swap, chips), send_columns(ordered[first:second]))
     )
     col_blocks.update(zip(ordered[first:second], cols))
-    grad_ring = Gather((gc_own + gc_other).astype(BF16), chips, tokens // 2)
+    grad_combined = (gc_own + gc_other).astype(BF16)
+    grad_ring = Gather(grad_combined, chips, tokens // 2)
 
     def run_backward(i):
         pairs = core_swap(grad_ring, groups[i], tokens)
+        if i == 0:
+            pairs = [[View(grad_combined)], [View(grad_combined_sib)]] + pairs
         return expert_backward(pairs, *kept[i], up_weight, down_weight, cap, tokens)
 
-    ring_step(chips, [comb, grad_ring])
+    grad_combined_sib = ring_step(chips, [comb, grad_ring], swap(grad_combined, chips))
     for s in range(2, half):
         out = ring_step(chips, [comb, grad_ring], run_backward(s - 2))
         share_out(groups[s - 2], *out, backward)
@@ -753,13 +790,13 @@
     for _ in range(4, half + 1):
         beside = ring_step(chips, [comb_ring, back], beside)
     places = jnp.concatenate([own_parts, sib_parts])
-    mixed = place_columns(places, mixed[0], beside, piece)
     grad_own, grad_sib = weight_grad(
         core, [col_blocks[d] for d in dists], [comb_ring.got[d] for d in dists]
     )
-    mixed, grad_own, grad_sib = ring_step(chips, [back], (mixed, grad_own, grad_sib))
+    grad_own, grad_sib, mixed_sib = ring_step(chips, [back], (grad_own, grad_sib, beside))
     partial = (grad_own + swap(grad_sib, chips).astype(F32)).astype(BF16)
-    partial, other = ring_step(chips, [back], (partial, partner(partial)))
+    mixed = place_columns(places, mixed[0], mixed_sib, piece)
+    partial, other, mixed = ring_step(chips, [back], (partial, partner(partial), mixed))
     grad_w_out = partial.astype(F32) + other.astype(F32)
     grad_latent = back.sum().astype(BF16)
     return (mixed, grad_latent, grad_w_out)

time: 235 us -> 235 us (level)
  between operations: 6.94 us -> 2.05 us
  starting transfers between devices: 51 us -> 54.3 us
  waiting for transfers between devices: 74.5 us -> 71.2 us
  Pallas kernels: 77.7 us -> 80.6 us
    ppermute x35, waiting for transfers between devices: 63.5 us -> 55.5 us  [shift(): return lax.ppermute(x, 'expert', pairs)]
    unnamed x136 -> x152, local copies, waits for them, and re-layouts: 4.09 us -> 8.1 us
    pallas_call x11 -> x12, Pallas kernels: 75.3 us -> 78.2 us  [local_call(): pl.pallas_call(kernel, in_specs=[SMEM] * len(scalars) + [ANY] * len(array...]
    dynamic_slice x2 -> x0, local copies, waits for them, and re-layouts: 2.81 us -> none  [the longest x1 1.81 us: half_rows(): return lax.dynamic_slice_in_dim(w_out_t, which * piece, piece, 0)]
    ppermute x21 -> x23, waiting for transfers between devices: 2.89 us -> 5.35 us  [swap(): return lax.ppermute(x, 'expert', [(i, i ^ 1) for i in range(2 * chips)])]
  transfers between devices with their start and end apart: 61 -> 63, of which waited for: 25 -> 30; matrix products, arithmetic and copies ran while one was open for 7% -> 6% of each run, Pallas kernels for 33% -> 34%
where the time goes in v2:
time: 235 us
  Pallas kernels  80.6 us (34%)
  waiting for transfers between devices  71.2 us (30%)
  starting transfers between devices  54.3 us (23%)
  other arithmetic  13.9 us (6%)
  local copies, waits for them, and re-layouts  12.7 us (5%)
    pallas_call x12, Pallas kernels, local_call(): pl.pallas_call(kernel, in_specs=[SMEM] * len(scalars) + [ANY] * len(array...  78.2 us
    ppermute x35, waiting for transfers between devices, shift(): return lax.ppermute(x, 'expert', pairs)  55.5 us
    ppermute x35, starting transfers between devices, shift(): return lax.ppermute(x, 'expert', pairs)  43.5 us
    ppermute x5, waiting for transfers between devices, partner(): return lax.ppermute(x, 'dp', [(i, (i + 1) % dp) for i in range(dp)])  10.3 us
    unnamed x152, local copies, waits for them, and re-layouts  8.1 us
    ppermute x5, starting transfers between devices, partner(): return lax.ppermute(x, 'dp', [(i, (i + 1) % dp) for i in range(dp)])  6.74 us
    ppermute x23, waiting for transfers between devices, swap(): return lax.ppermute(x, 'expert', [(i, i ^ 1) for i in range(2 * chips)])  5.35 us
  transfers between devices with their start and end apart: 63, of which 30 were waited for; matrix products, arithmetic and copies ran while one was open for 6% of the time, Pallas kernels for 34%

profile of v2, /device:TPU:0, one launch (start us, length us, event | category | flops | bytes accessed | tf_op | source)
XLA Modules:
  0.0 234.7 jit_solution(9017547741346721223)
XLA Ops:
  4.0 2.6 %collective-permute-start = (bf16[272,1024]{1,0:T(8,128)(2,1)S(1)}, bf16[272,1024]{1,0:T(8,128)(2,1)S(1)}, u32[]{:S(2)}, u32[]{:S(2)}) collective-permute-start(bf16[272,1024]{1,0:T(8,128)(2,1)S(1)} %pad_maximum_fusion.9.refs_0_.refs_5_.refs_2_), channel_id=1, source_target_pairs={{0,4},{1,5},{4,8},{5,9},{8,12},{9,13},{12,14},{13,15},{14,10},{15,... | collective-permute-start | bytes 1671176 | tf_op jit(solution)/shard_map/ppermute | solution.py:46
  8.2 2.9 %column_blocks.1 = (bf16[128,512]{1,0:T(8,128)(2,1)}, bf16[128,512]{1,0:T(8,128)(2,1)}, bf16[128,512]{1,0:T(8,128)(2,1)}, bf16[128,512]{1,0:T(8,128)(2,1)}, bf16...) custom-call(s32[8]{0:T(128)} %get-tuple-element.284.chip_ref, ...), custom_call_target="tpu_custom_call" | custom-call | bytes 2097152 | tf_op jit(solution)/shard_map/column_blocks/pallas_call | solution.py:157
  11.1 8.8 %collective-permute-done.refs_2_.refs_7_.refs_4_ = bf16[272,1024]{1,0:T(8,128)(2,1)S(1)} collective-permute-done((bf16[272,1024]{1,0:T(8,128)(2,1)S(1)}, bf16[272,1024]{1,0:T(8,128)(2,1)S(1)}, u32[]{:S(2)}, u32[]{:S(2)}) %collective-permute-start) | collective-permute-done | bytes 557088 | tf_op jit(solution)/shard_map/ppermute | solution.py:46
  22.7 1.6 collective-permute-start.4
  27.2 8.8 %expert_forward.4 = (bf16[480,2048]{1,0:T(8,128)(2,1)}, f32[480,128]{1,0:T(8,128)}, bf16[128,1024]{1,0:T(8,128)(2,1)}, bf16[128,1024]{1,0:T(8,128)(2,1)}, bf16[1...) custom-call(s32[1]{0:T(128)} %bitcast.2.me_ref, bf16[272,1024]{1,0:T(8,128)(2,1)} %copy-done.4, ...), custom_call_target="tpu_custom_call" | custom-call | flops 4026531840 | bytes 8388608 | tf_op jit(solution)/shard_map/expert_forward/pallas_call | solution.py:157
  36.0 2.6 %collective-permute-done.7 = bf16[256,1024]{1,0:T(8,128)(2,1)S(1)} collective-permute-done((bf16[256,1024]{1,0:T(8,128)(2,1)S(1)}, bf16[256,1024]{1,0:T(8,128)(2,1)S(1)}, u32[]{:S(2)}, u32[]{:S(2)}) %collective-permute-start.7) | collective-permute-done | bytes 524320 | tf_op jit(solution)/shard_map/ppermute | solution.py:683
  44.1 7.3 %expert_forward.5 = (bf16[320,2048]{1,0:T(8,128)(2,1)}, f32[320,128]{1,0:T(8,128)}, bf16[128,1024]{1,0:T(8,128)(2,1)}, bf16[128,1024]{1,0:T(8,128)(2,1)}, bf16[256,1024]{1,0:T(8,128)(2,1)}) custom-call(s32[1]{0:T(128)} %bitcast.2.me_ref, bf16[272,1024]{1,0:T(8,128)(2,1)} %copy-done.2, bf16[288,1024]{1,0:T(8,128)(2,1)} %copy-done.14, ...), custom_call_target="tpu_custom_call" | custom-call | flops 2684354560 | bytes 8388608 | tf_op jit(solution)/shard_map/expert_forward/pallas_call | solution.py:157
  51.4 4.0 %collective-permute-done.11 = bf16[256,1024]{1,0:T(8,128)(2,1)S(1)} collective-permute-done((bf16[256,1024]{1,0:T(8,128)(2,1)S(1)}, bf16[256,1024]{1,0:T(8,128)(2,1)S(1)}, u32[]{:S(2)}, u32[]{:S(2)}) %collective-permute-start.11) | collective-permute-done | bytes 524320 | tf_op jit(solution)/shard_map/ppermute | solution.py:683
  60.5 3.0 %collective-permute-start.20 = (bf16[128,512]{1,0:T(8,128)(2,1)}, bf16[128,512]{1,0:T(8,128)(2,1)S(1)}, u32[]{:S(2)}, u32[]{:S(2)}) collective-permute-start(bf16[128,512]{1,0:T(8,128)(2,1)} %get-tuple-element.184), channel_id=1, source_target_pairs={{0,14},{1,15},{4,10},{5,11},{8,6},{9,7},{12,2},{13,3},{14,0},{15,1... | collective-permute-start | bytes 393224 | tf_op jit(solution)/shard_map/ppermute | solution.py:46
  67.2 7.3 %expert_forward.6 = (bf16[320,2048]{1,0:T(8,128)(2,1)}, f32[320,128]{1,0:T(8,128)}, bf16[128,1024]{1,0:T(8,128)(2,1)}, bf16[128,1024]{1,0:T(8,128)(2,1)}, bf16[256,1024]{1,0:T(8,128)(2,1)}) custom-call(s32[1]{0:T(128)} %bitcast.2.me_ref, bf16[272,1024]{1,0:T(8,128)(2,1)} %copy-done.1, bf16[288,1024]{1,0:T(8,128)(2,1)} %copy-done.13, ...), custom_call_target="tpu_custom_call" | custom-call | flops 2684354560 | bytes 8388608 | tf_op jit(solution)/shard_map/expert_forward/pallas_call | solution.py:157
  74.8 2.8 %collective-permute-start.22 = (bf16[128,512]{1,0:T(8,128)(2,1)}, bf16[128,512]{1,0:T(8,128)(2,1)S(1)}, u32[]{:S(2)}, u32[]{:S(2)}) collective-permute-start(bf16[128,512]{1,0:T(8,128)(2,1)} %get-tuple-element.186), channel_id=1, source_target_pairs={{0,12},{1,13},{4,14},{5,15},{8,10},{9,11},{12,6},{13,7},{14,2},{15... | collective-permute-start | bytes 393224 | tf_op jit(solution)/shard_map/ppermute | solution.py:46
  80.1 3.3 %collective-permute-start.27 = (bf16[128,512]{1,0:T(8,128)(2,1)S(1)}, bf16[128,512]{1,0:T(8,128)(2,1)S(1)}, u32[]{:S(2)}, u32[]{:S(2)}) collective-permute-start(bf16[128,512]{1,0:T(8,128)(2,1)S(1)} %copy-done.75), channel_id=1, source_target_pairs={{0,6},{1,7},{4,2},{5,3},{8,0},{9,1},{12,4},{13,5},{14,8},{15,9},{1... | collective-permute-start | bytes 393224 | tf_op jit(solution)/shard_map/ppermute | solution.py:46
  83.3 5.6 %expert_forward.7 = (bf16[160,2048]{1,0:T(8,128)(2,1)}, f32[160,128]{1,0:T(8,128)}, bf16[128,1024]{1,0:T(8,128)(2,1)}, bf16[128,1024]{1,0:T(8,128)(2,1)}) custom-call(s32[1]{0:T(128)} %bitcast.2.me_ref, bf16[128,1024]{1,0:T(8,128)(2,1)} %copy-done.28, bf16[144,1024]{1,0:T(8,128)(2,1)} %copy-done.18, bf16[144,1024]{1,0:T(8,128)(2,1)} %copy-done.7, ...), custom_call_target="tpu_custom_call" | custom-call | flops 1342177280 | bytes 8388608 | tf_op jit(solution)/shard_map/expert_forward/pallas_call | solution.py:157
  90.6 5.4 %grad_combined.1 = (f32[128,1024]{1,0:T(8,128)}, f32[128,1024]{1,0:T(8,128)}) custom-call(s32[16]{0:T(128)} %pad_add_fusion.offsets, bf16[128,4096]{1,0:T(8,128)(2,1)} %refs_0_.1, bf16[128,4096]{1,0:T(8,128)(2,1)} %copy-done.23, bf16[272,1024]{1,0:T(8,128)(2,1)} %copy-done.4, bf16[128,1024]{1,0:T(8,128)(2,1)} %slice_select_fusion.refs_3_, ...), custom_call_target="tpu_custom_call" | custom-call | flops 1073741824 | bytes 4194304 | tf_op jit(solution)/shard_map/grad_combined/pallas_call | solution.py:157
  96.3 2.9 %collective-permute-start.24 = (bf16[64,1024]{1,0:T(8,128)(2,1)S(1)}, bf16[64,1024]{1,0:T(8,128)(2,1)S(1)}, u32[]{:S(2)}, u32[]{:S(2)}) collective-permute-start(bf16[64,1024]{1,0:T(8,128)(2,1)S(1)} %get-tuple-element.320), channel_id=1, source_target_pairs={{0,4},{1,5},{4,8},{5,9},{8,12},{9,13},{12,14},{13,15},{14,10},{15,... | collective-permute-start | bytes 393224 | tf_op jit(solution)/shard_map/ppermute | solution.py:46
  100.5 3.8 %collective-permute-done.24 = bf16[64,1024]{1,0:T(8,128)(2,1)S(1)} collective-permute-done((bf16[64,1024]{1,0:T(8,128)(2,1)S(1)}, bf16[64,1024]{1,0:T(8,128)(2,1)S(1)}, u32[]{:S(2)}, u32[]{:S(2)}) %collective-permute-start.24) | collective-permute-done | bytes 131104 | tf_op jit(solution)/shard_map/ppermute | solution.py:46
  107.7 1.8 collective-permute-done.31.refs_1_
  109.5 8.9 %collective-permute-done.29.refs_2_ = bf16[256,1024]{1,0:T(8,128)(2,1)S(1)} collective-permute-done((bf16[256,1024]{1,0:T(8,128)(2,1)S(1)}, bf16[256,1024]{1,0:T(8,128)(2,1)S(1)}, u32[]{:S(2)}, u32[]{:S(2)}) %collective-permute-start.29) | collective-permute-done | bytes 524320 | tf_op jit(solution)/shard_map/ppermute | solution.py:46
  123.6 8.9 %expert_backward.4 = (bf16[128,1024]{1,0:T(8,128)(2,1)}, bf16[128,1024]{1,0:T(8,128)(2,1)}, bf16[128,1024]{1,0:T(8,128)(2,1)}, bf16[384,1024]{1,0:T(8,128)(2,1)}) custom-call(bf16[128,1024]{1,0:T(8,128)(2,1)} %copy-done.26, bf16[128,1024]{1,0:T(8,128)(2,1)} %copy-done.71, bf16[256,1024]{1,0:T(8,128)(2,1)} %copy-done.36, ...), custom_call_target="tpu_custom_call" | custom-call | flops 4026531840 | bytes 8388608 | tf_op jit(solution)/shard_map/expert_backward/pallas_call | solution.py:157
  132.5 3.4 %collective-permute-done.32.refs_0_ = bf16[256,1024]{1,0:T(8,128)(2,1)S(1)} collective-permute-done((bf16[256,1024]{1,0:T(8,128)(2,1)S(1)}, bf16[256,1024]{1,0:T(8,128)(2,1)S(1)}, u32[]{:S(2)}, u32[]{:S(2)}) %collective-permute-start.32) | collective-permute-done | bytes 524320 | tf_op jit(solution)/shard_map/ppermute | solution.py:46
  141.0 7.3 %expert_backward.5 = (bf16[128,1024]{1,0:T(8,128)(2,1)}, bf16[128,1024]{1,0:T(8,128)(2,1)}, bf16[256,1024]{1,0:T(8,128)(2,1)}) custom-call(bf16[256,1024]{1,0:T(8,128)(2,1)} %copy-done.16, bf16[256,1024]{1,0:T(8,128)(2,1)} %copy-done.32, bf16[256,1024]{1,0:T(8,128)(2,1)} %copy-done.17, bf16[320,2048]{1,0:T(8,128)(2,1)} %get-tuple-element.220.refs_3_, ...), custom_call_target="tpu_custom_call" | custom-call | flops 2684354560 | bytes 8388608 | tf_op jit(solution)/shard_map/expert_backward/pallas_call | solution.py:157
  148.3 4.1 %collective-permute-done.37.refs_0_ = bf16[256,1024]{1,0:T(8,128)(2,1)S(1)} collective-permute-done((bf16[256,1024]{1,0:T(8,128)(2,1)S(1)}, bf16[256,1024]{1,0:T(8,128)(2,1)S(1)}, u32[]{:S(2)}, u32[]{:S(2)}) %collective-permute-start.37) | collective-permute-done | bytes 524320 | tf_op jit(solution)/shard_map/ppermute | solution.py:46
  157.1 7.3 %expert_backward.6 = (bf16[128,1024]{1,0:T(8,128)(2,1)}, bf16[128,1024]{1,0:T(8,128)(2,1)}, bf16[256,1024]{1,0:T(8,128)(2,1)}) custom-call(bf16[256,1024]{1,0:T(8,128)(2,1)} %copy-done.11, bf16[256,1024]{1,0:T(8,128)(2,1)} %copy-done.31, bf16[256,1024]{1,0:T(8,128)(2,1)} %copy-done.12, bf16[320,2048]{1,0:T(8,128)(2,1)} %get-tuple-element.230.refs_3_, ...), custom_call_target="tpu_custom_call" | custom-call | flops 2684354560 | bytes 8388608 | tf_op jit(solution)/shard_map/expert_backward/pallas_call | solution.py:157
  170.8 6.7 %expert_backward.7 = (bf16[128,1024]{1,0:T(8,128)(2,1)}, bf16[128,1024]{1,0:T(8,128)(2,1)}) custom-call(bf16[192,1024]{1,0:T(8,128)(2,1)} %copy-done.9, bf16[192,1024]{1,0:T(8,128)(2,1)} %copy-done.10, bf16[128,1024]{1,0:T(8,128)(2,1)} %copy-done.41, bf16[160,2048]{1,0:T(8,128)(2,1)} %get-tuple-element.237.refs_3_, f32[160,128]{1,0:T(8,128)} %get-tuple-element.238.refs_4_, ...), custom_call_target="tpu_custom_call" | custom-call | flops 1342177280 | bytes 8388608 | tf_op jit(solution)/shard_map/expert_backward/pallas_call | solution.py:157
  183.4 6.0 %mixed.1 = (bf16[128,2048]{1,0:T(8,128)(2,1)}, bf16[128,2048]{1,0:T(8,128)(2,1)}) custom-call(bf16[128,1024]{1,0:T(8,128)(2,1)} %copy-done.8, bf16[128,1024]{1,0:T(8,128)(2,1)} %copy-done.54, bf16[272,1024]{1,0:T(8,128)(2,1)} %copy-done.4, bf16[128,1024]{1,0:T(8,128)(2,1)} %slice_select_fusion.refs_3_, bf16[272,1024]{1,0:T(8,128)(2,1)} %copy-done.5, ...), custom_call_target="tpu_custom_call" | custom-call | flops 1073741824 | bytes 4194304 | tf_op jit(solution)/shard_map/mixed/pallas_call | solution.py:157
  189.7 2.7 %collective-permute-done.52.refs_14_ = bf16[192,1024]{1,0:T(8,128)(2,1)S(1)} collective-permute-done((bf16[192,1024]{1,0:T(8,128)(2,1)S(1)}, bf16[192,1024]{1,0:T(8,128)(2,1)S(1)}, u32[]{:S(2)}, u32[]{:S(2)}) %collective-permute-start.52) | collective-permute-done | bytes 393248 | tf_op jit(solution)/shard_map/ppermute | solution.py:46
  196.5 9.0 %collective-permute-done.55.refs_16_ = bf16[192,1024]{1,0:T(8,128)(2,1)S(1)} collective-permute-done((bf16[192,1024]{1,0:T(8,128)(2,1)S(1)}, bf16[192,1024]{1,0:T(8,128)(2,1)S(1)}, u32[]{:S(2)}, u32[]{:S(2)}) %collective-permute-start.55) | collective-permute-done | bytes 393248 | tf_op jit(solution)/shard_map/ppermute | solution.py:46
  208.3 4.6 %weight_grad.1 = (f32[256,1024]{1,0:T(8,128)}, bf16[256,1024]{1,0:T(8,128)(2,1)}) custom-call(s32[1]{0:T(128)} %bitcast.5.core_ref, bf16[128,512]{1,0:T(8,128)(2,1)} %get-tuple-element.259.refs_0_, bf16[128,512]{1,0:T(8,128)(2,1)} %copy-done.61, bf16[128,512]{1,0:T(8,128)(2,1)} %copy-done.60, bf16[128,512]{1,0:T(8,128)(2,1)} %copy-done.59, ...), custom_call_target="tpu_custom_call" | custom-call | flops 1073741824 | bytes 3145728 | tf_op jit(solution)/shard_map/weight_grad/pallas_call | solution.py:157
  215.0 2.3 collective-permute-done.61
  223.1 2.4 %place_columns.1 = bf16[128,4096]{1,0:T(8,128)(2,1)} custom-call(s32[32]{0:T(128)} %pad_add_fusion.1.offsets, bf16[128,2048]{1,0:T(8,128)(2,1)} %get-tuple-element.275.own_ref, bf16[128,2048]{1,0:T(8,128)(2,1)} %copy-done.30), custom_call_target="tpu_custom_call" | custom-call | bytes 2097152 | tf_op jit(solution)/shard_map/place_columns/pallas_call | solution.py:591
  225.6 3.0 %collective-permute-done.59 = bf16[128,1024]{1,0:T(8,128)(2,1)S(1)} collective-permute-done((bf16[128,1024]{1,0:T(8,128)(2,1)S(1)}, bf16[128,1024]{1,0:T(8,128)(2,1)S(1)}, u32[]{:S(2)}, u32[]{:S(2)}) %collective-permute-start.59) | collective-permute-done | bytes 262176 | tf_op jit(solution)/shard_map/ppermute | solution.py:46
  229.0 3.7 %collective-permute-done.62 = bf16[256,1024]{1,0:T(8,128)(2,1)S(1)} collective-permute-done((bf16[256,1024]{1,0:T(8,128)(2,1)S(1)}, bf16[256,1024]{1,0:T(8,128)(2,1)S(1)}, u32[]{:S(2)}, u32[]{:S(2)}) %collective-permute-start.62) | collective-permute-done | bytes 524320 | tf_op jit(solution)/shard_map/ppermute | solution.py:683
  (340 shorter events, 77.7 us)
Async XLA Ops:
  0.6 20.8 %collective-permute-start.2 = (bf16[128,4096]{1,0:T(8,128)(2,1)}, bf16[128,4096]{1,0:T(8,128)(2,1)S(1)}, u32[]{:S(2)}, u32[]{:S(2)}) collective-permute-start(bf16[128,4096]{1,0:T(8,128)(2,1)} %refs_0_.1), channel_id=1, source_target_pairs={{0,1},{1,0},{2,3},{3,2},{4,5},{5,4},{6,7},{7,6},{8,9},{9,8},{10,11... | collective-permute-start | bytes 3145736 | tf_op jit(solution)/shard_map/ppermute | solution.py:50
  4.0 15.9 %collective-permute-start = (bf16[272,1024]{1,0:T(8,128)(2,1)S(1)}, bf16[272,1024]{1,0:T(8,128)(2,1)S(1)}, u32[]{:S(2)}, u32[]{:S(2)}) collective-permute-start(bf16[272,1024]{1,0:T(8,128)(2,1)S(1)} %pad_maximum_fusion.9.refs_0_.refs_5_.refs_2_), channel_id=1, source_target_pairs={{0,4},{1,5},{4,8},{5,9},{8,12},{9,13},{12,14},{13,15},{14,10},{15,... | collective-permute-start | bytes 1671176 | tf_op jit(solution)/shard_map/ppermute | solution.py:46
  6.6 14.7 %collective-permute-start.1 = (bf16[272,1024]{1,0:T(8,128)(2,1)S(1)}, bf16[272,1024]{1,0:T(8,128)(2,1)S(1)}, u32[]{:S(2)}, u32[]{:S(2)}) collective-permute-start(bf16[272,1024]{1,0:T(8,128)(2,1)S(1)} %pad_maximum_fusion.9.refs_0_.refs_5_.refs_2_), channel_id=1, source_target_pairs={{0,2},{1,3},{4,0},{5,1},{8,4},{9,5},{12,8},{13,9},{14,12},{15,13},... | collective-permute-start | bytes 1671176 | tf_op jit(solution)/shard_map/ppermute | solution.py:46
  22.7 15.9 %collective-permute-start.4 = (bf16[272,1024]{1,0:T(8,128)(2,1)S(1)}, bf16[272,1024]{1,0:T(8,128)(2,1)S(1)}, u32[]{:S(2)}, u32[]{:S(2)}) collective-permute-start(bf16[272,1024]{1,0:T(8,128)(2,1)S(1)} %collective-permute-done.refs_2_.refs_7_.refs_4_), channel_id=1, source_target_pairs={{0,4},{1,5},{4,8},{5,9},{8,12},{9,13},{12,14},{13,15},{14,10},{15,... | collective-permute-start | bytes 1671176 | tf_op jit(solution)/shard_map/ppermute | solution.py:46
  24.3 14.7 %collective-permute-start.5 = (bf16[272,1024]{1,0:T(8,128)(2,1)S(1)}, bf16[272,1024]{1,0:T(8,128)(2,1)S(1)}, u32[]{:S(2)}, u32[]{:S(2)}) collective-permute-start(bf16[272,1024]{1,0:T(8,128)(2,1)S(1)} %collective-permute-done.1.refs_4_.refs_9_.refs_6_), channel_id=1, source_target_pairs={{0,2},{1,3},{4,0},{5,1},{8,4},{9,5},{12,8},{13,9},{14,12},{15,13},... | collective-permute-start | bytes 1671176 | tf_op jit(solution)/shard_map/ppermute | solution.py:46
  24.8 13.8 %collective-permute-start.7 = (bf16[256,1024]{1,0:T(8,128)(2,1)S(1)}, bf16[256,1024]{1,0:T(8,128)(2,1)S(1)}, u32[]{:S(2)}, u32[]{:S(2)}) collective-permute-start(bf16[256,1024]{1,0:T(8,128)(2,1)S(1)} %pad_maximum_fusion.10), channel_id=1, source_target_pairs={{0,16},{16,0},{1,17},{17,1},{2,18},{18,2},{3,19},{19,3},{4,20},{20... | collective-permute-start | bytes 1572872 | tf_op jit(solution)/shard_map/ppermute | solution.py:683
  39.6 15.8 %collective-permute-start.8 = (bf16[272,1024]{1,0:T(8,128)(2,1)S(1)}, bf16[272,1024]{1,0:T(8,128)(2,1)S(1)}, u32[]{:S(2)}, u32[]{:S(2)}) collective-permute-start(bf16[272,1024]{1,0:T(8,128)(2,1)S(1)} %collective-permute-done.4.refs_0_.refs_3_.refs_8_), channel_id=1, source_target_pairs={{0,4},{1,5},{4,8},{5,9},{8,12},{9,13},{12,14},{13,15},{14,10},{15,... | collective-permute-start | bytes 1671176 | tf_op jit(solution)/shard_map/ppermute | solution.py:46
  41.2 14.7 %collective-permute-start.9 = (bf16[272,1024]{1,0:T(8,128)(2,1)S(1)}, bf16[272,1024]{1,0:T(8,128)(2,1)S(1)}, u32[]{:S(2)}, u32[]{:S(2)}) collective-permute-start(bf16[272,1024]{1,0:T(8,128)(2,1)S(1)} %collective-permute-done.5.refs_2_.refs_5_.refs_10_), channel_id=1, source_target_pairs={{0,2},{1,3},{4,0},{5,1},{8,4},{9,5},{12,8},{13,9},{14,12},{15,13},... | collective-permute-start | bytes 1671176 | tf_op jit(solution)/shard_map/ppermute | solution.py:46
  41.7 13.8 %collective-permute-start.11 = (bf16[256,1024]{1,0:T(8,128)(2,1)S(1)}, bf16[256,1024]{1,0:T(8,128)(2,1)S(1)}, u32[]{:S(2)}, u32[]{:S(2)}) collective-permute-start(bf16[256,1024]{1,0:T(8,128)(2,1)S(1)} %pad_maximum_fusion.11), channel_id=1, source_target_pairs={{0,16},{16,0},{1,17},{17,1},{2,18},{18,2},{3,19},{19,3},{4,20},{20... | collective-permute-start | bytes 1572872 | tf_op jit(solution)/shard_map/ppermute | solution.py:683
  58.5 19.1 %collective-permute-start.16 = (bf16[256,1024]{1,0:T(8,128)(2,1)}, bf16[256,1024]{1,0:T(8,128)(2,1)S(1)}, u32[]{:S(2)}, u32[]{:S(2)}) collective-permute-start(bf16[256,1024]{1,0:T(8,128)(2,1)} %pad_maximum_fusion.12), channel_id=1, source_target_pairs={{0,16},{16,0},{1,17},{17,1},{2,18},{18,2},{3,19},{19,3},{4,20},{20... | collective-permute-start | bytes 1572872 | tf_op jit(solution)/shard_map/ppermute | solution.py:683
  60.5 28.5 %collective-permute-start.20 = (bf16[128,512]{1,0:T(8,128)(2,1)}, bf16[128,512]{1,0:T(8,128)(2,1)S(1)}, u32[]{:S(2)}, u32[]{:S(2)}) collective-permute-start(bf16[128,512]{1,0:T(8,128)(2,1)} %get-tuple-element.184), channel_id=1, source_target_pairs={{0,14},{1,15},{4,10},{5,11},{8,6},{9,7},{12,2},{13,3},{14,0},{15,1... | collective-permute-start | bytes 393224 | tf_op jit(solution)/shard_map/ppermute | solution.py:46
  63.6 14.0 %collective-permute-start.14 = (bf16[144,1024]{1,0:T(8,128)(2,1)}, bf16[144,1024]{1,0:T(8,128)(2,1)S(1)}, u32[]{:S(2)}, u32[]{:S(2)}) collective-permute-start(bf16[144,1024]{1,0:T(8,128)(2,1)} %get-tuple-element.292), channel_id=1, source_target_pairs={{0,2},{1,3},{4,0},{5,1},{8,4},{9,5},{12,8},{13,9},{14,12},{15,13},... | collective-permute-start | bytes 884744 | tf_op jit(solution)/shard_map/ppermute | solution.py:46
  66.3 22.8 %collective-permute-start.21 = (bf16[128,512]{1,0:T(8,128)(2,1)}, bf16[128,512]{1,0:T(8,128)(2,1)S(1)}, u32[]{:S(2)}, u32[]{:S(2)}) collective-permute-start(bf16[128,512]{1,0:T(8,128)(2,1)} %get-tuple-element.185), channel_id=1, source_target_pairs={{0,10},{1,11},{4,6},{5,7},{8,2},{9,3},{12,0},{13,1},{14,4},{15,5},... | collective-permute-start | bytes 393224 | tf_op jit(solution)/shard_map/ppermute | solution.py:46
  74.8 14.4 %collective-permute-start.22 = (bf16[128,512]{1,0:T(8,128)(2,1)}, bf16[128,512]{1,0:T(8,128)(2,1)S(1)}, u32[]{:S(2)}, u32[]{:S(2)}) collective-permute-start(bf16[128,512]{1,0:T(8,128)(2,1)} %get-tuple-element.186), channel_id=1, source_target_pairs={{0,12},{1,13},{4,14},{5,15},{8,10},{9,11},{12,6},{13,7},{14,2},{15... | collective-permute-start | bytes 393224 | tf_op jit(solution)/shard_map/ppermute | solution.py:46
  80.1 20.4 %collective-permute-start.27 = (bf16[128,512]{1,0:T(8,128)(2,1)S(1)}, bf16[128,512]{1,0:T(8,128)(2,1)S(1)}, u32[]{:S(2)}, u32[]{:S(2)}) collective-permute-start(bf16[128,512]{1,0:T(8,128)(2,1)S(1)} %copy-done.75), channel_id=1, source_target_pairs={{0,6},{1,7},{4,2},{5,3},{8,0},{9,1},{12,4},{13,5},{14,8},{15,9},{1... | collective-permute-start | bytes 393224 | tf_op jit(solution)/shard_map/ppermute | solution.py:46
  89.0 11.4 %collective-permute-start.28 = (bf16[128,512]{1,0:T(8,128)(2,1)S(1)}, bf16[128,512]{1,0:T(8,128)(2,1)S(1)}, u32[]{:S(2)}, u32[]{:S(2)}) collective-permute-start(bf16[128,512]{1,0:T(8,128)(2,1)S(1)} %copy-done.74), channel_id=1, source_target_pairs={{0,8},{1,9},{4,12},{5,13},{8,14},{9,15},{12,10},{13,11},{14,6},{15... | collective-permute-start | bytes 393224 | tf_op jit(solution)/shard_map/ppermute | solution.py:46
  105.1 13.3 %collective-permute-start.29 = (bf16[256,1024]{1,0:T(8,128)(2,1)S(1)}, bf16[256,1024]{1,0:T(8,128)(2,1)S(1)}, u32[]{:S(2)}, u32[]{:S(2)}) collective-permute-start(bf16[256,1024]{1,0:T(8,128)(2,1)S(1)} %get-tuple-element.318), channel_id=1, source_target_pairs={{0,4},{1,5},{4,8},{5,9},{8,12},{9,13},{12,14},{13,15},{14,10},{15,... | collective-permute-start | bytes 1572872 | tf_op jit(solution)/shard_map/ppermute | solution.py:46
  106.4 13.2 %collective-permute-start.30 = (bf16[256,1024]{1,0:T(8,128)(2,1)S(1)}, bf16[256,1024]{1,0:T(8,128)(2,1)S(1)}, u32[]{:S(2)}, u32[]{:S(2)}) collective-permute-start(bf16[256,1024]{1,0:T(8,128)(2,1)S(1)} %get-tuple-element.317), channel_id=1, source_target_pairs={{0,2},{1,3},{4,0},{5,1},{8,4},{9,5},{12,8},{13,9},{14,12},{15,13},... | collective-permute-start | bytes 1572872 | tf_op jit(solution)/shard_map/ppermute | solution.py:46
  107.2 12.5 %collective-permute-start.12 = (bf16[256,1024]{1,0:T(8,128)(2,1)S(1)}, bf16[256,1024]{1,0:T(8,128)(2,1)S(1)}, u32[]{:S(2)}, u32[]{:S(2)}) collective-permute-start(bf16[256,1024]{1,0:T(8,128)(2,1)S(1)} %copy-done.67), channel_id=1, source_target_pairs={{0,1},{1,0},{2,3},{3,2},{4,5},{5,4},{6,7},{7,6},{8,9},{9,8},{10,11... | collective-permute-start | bytes 1572872 | tf_op jit(solution)/shard_map/ppermute | solution.py:50
  121.6 15.5 %collective-permute-start.36 = (bf16[384,1024]{1,0:T(8,128)(2,1)S(1)}, bf16[384,1024]{1,0:T(8,128)(2,1)S(1)}, u32[]{:S(2)}, u32[]{:S(2)}) collective-permute-start(bf16[384,1024]{1,0:T(8,128)(2,1)S(1)} %copy-done.64), channel_id=1, source_target_pairs={{0,1},{1,0},{2,3},{3,2},{4,5},{5,4},{6,7},{7,6},{8,9},{9,8},{10,11... | collective-permute-start | bytes 2359304 | tf_op jit(solution)/shard_map/ppermute | solution.py:50
  121.6 14.3 %collective-permute-start.32 = (bf16[256,1024]{1,0:T(8,128)(2,1)S(1)}, bf16[256,1024]{1,0:T(8,128)(2,1)S(1)}, u32[]{:S(2)}, u32[]{:S(2)}) collective-permute-start(bf16[256,1024]{1,0:T(8,128)(2,1)S(1)} %get-tuple-element.315), channel_id=1, source_target_pairs={{0,4},{1,5},{4,8},{5,9},{8,12},{9,13},{12,14},{13,15},{14,10},{15,... | collective-permute-start | bytes 1572872 | tf_op jit(solution)/shard_map/ppermute | solution.py:46
  123.0 14.1 %collective-permute-start.33 = (bf16[256,1024]{1,0:T(8,128)(2,1)S(1)}, bf16[256,1024]{1,0:T(8,128)(2,1)S(1)}, u32[]{:S(2)}, u32[]{:S(2)}) collective-permute-start(bf16[256,1024]{1,0:T(8,128)(2,1)S(1)} %get-tuple-element.316), channel_id=1, source_target_pairs={{0,2},{1,3},{4,0},{5,1},{8,4},{9,5},{12,8},{13,9},{14,12},{15,13},... | collective-permute-start | bytes 1572872 | tf_op jit(solution)/shard_map/ppermute | solution.py:46
  138.1 14.3 %collective-permute-start.37 = (bf16[256,1024]{1,0:T(8,128)(2,1)S(1)}, bf16[256,1024]{1,0:T(8,128)(2,1)S(1)}, u32[]{:S(2)}, u32[]{:S(2)}) collective-permute-start(bf16[256,1024]{1,0:T(8,128)(2,1)S(1)} %get-tuple-element.312), channel_id=1, source_target_pairs={{0,4},{1,5},{4,8},{5,9},{8,12},{9,13},{12,14},{13,15},{14,10},{15,... | collective-permute-start | bytes 1572872 | tf_op jit(solution)/shard_map/ppermute | solution.py:46
  138.8 14.0 %collective-permute-start.38 = (bf16[256,1024]{1,0:T(8,128)(2,1)S(1)}, bf16[256,1024]{1,0:T(8,128)(2,1)S(1)}, u32[]{:S(2)}, u32[]{:S(2)}) collective-permute-start(bf16[256,1024]{1,0:T(8,128)(2,1)S(1)} %get-tuple-element.313), channel_id=1, source_target_pairs={{0,2},{1,3},{4,0},{5,1},{8,4},{9,5},{12,8},{13,9},{14,12},{15,13},... | collective-permute-start | bytes 1572872 | tf_op jit(solution)/shard_map/ppermute | solution.py:46
  166.1 12.1 %collective-permute-start.49 = (bf16[128,1024]{1,0:T(8,128)(2,1)S(1)}, bf16[128,1024]{1,0:T(8,128)(2,1)S(1)}, u32[]{:S(2)}, u32[]{:S(2)}) collective-permute-start(bf16[128,1024]{1,0:T(8,128)(2,1)S(1)} %add_convert_fusion.7.refs_0_.refs_8_), channel_id=1, source_target_pairs={{0,1},{1,0},{2,3},{3,2},{4,5},{5,4},{6,7},{7,6},{8,9},{9,8},{10,11... | collective-permute-start | bytes 786440 | tf_op jit(solution)/shard_map/ppermute | solution.py:50
  166.7 11.6 %collective-permute-start.44 = (bf16[128,1024]{1,0:T(8,128)(2,1)S(1)}, bf16[128,1024]{1,0:T(8,128)(2,1)S(1)}, u32[]{:S(2)}, u32[]{:S(2)}) collective-permute-start(bf16[128,1024]{1,0:T(8,128)(2,1)S(1)} %slice.293), channel_id=1, source_target_pairs={{0,4},{1,5},{4,8},{5,9},{8,12},{9,13},{12,14},{13,15},{14,10},{15,... | collective-permute-start | bytes 786440 | tf_op jit(solution)/shard_map/ppermute | solution.py:46
  178.4 11.0 %collective-permute-start.53 = (bf16[256,1024]{1,0:T(8,128)(2,1)}, bf16[256,1024]{1,0:T(8,128)(2,1)S(1)}, u32[]{:S(2)}, u32[]{:S(2)}) collective-permute-start(bf16[256,1024]{1,0:T(8,128)(2,1)} %get-tuple-element.252), channel_id=1, source_target_pairs={{0,1},{1,0},{2,3},{3,2},{4,5},{5,4},{6,7},{7,6},{8,9},{9,8},{10,11... | collective-permute-start | bytes 1572872 | tf_op jit(solution)/shard_map/ppermute | solution.py:50
  181.2 11.2 %collective-permute-start.52 = (bf16[192,1024]{1,0:T(8,128)(2,1)S(1)}, bf16[192,1024]{1,0:T(8,128)(2,1)S(1)}, u32[]{:S(2)}, u32[]{:S(2)}) collective-permute-start(bf16[192,1024]{1,0:T(8,128)(2,1)S(1)} %pad_maximum_fusion.19), channel_id=1, source_target_pairs={{0,2},{1,3},{4,0},{5,1},{8,4},{9,5},{12,8},{13,9},{14,12},{15,13},... | collective-permute-start | bytes 1179656 | tf_op jit(solution)/shard_map/ppermute | solution.py:46
  183.4 22.5 %collective-permute-start.40 = (bf16[256,1024]{1,0:T(8,128)(2,1)}, bf16[256,1024]{1,0:T(8,128)(2,1)S(1)}, u32[]{:S(2)}, u32[]{:S(2)}) collective-permute-start(bf16[256,1024]{1,0:T(8,128)(2,1)} %get-tuple-element.226), channel_id=1, source_target_pairs={{0,1},{1,0},{2,3},{3,2},{4,5},{5,4},{6,7},{7,6},{8,9},{9,8},{10,11... | collective-permute-start | bytes 1572872 | tf_op jit(solution)/shard_map/ppermute | solution.py:50
  193.7 12.2 %collective-permute-start.56 = (bf16[128,2048]{1,0:T(8,128)(2,1)S(1)}, bf16[128,2048]{1,0:T(8,128)(2,1)S(1)}, u32[]{:S(2)}, u32[]{:S(2)}) collective-permute-start(bf16[128,2048]{1,0:T(8,128)(2,1)S(1)} %copy-done.69), channel_id=1, source_target_pairs={{0,1},{1,0},{2,3},{3,2},{4,5},{5,4},{6,7},{7,6},{8,9},{9,8},{10,11... | collective-permute-start | bytes 1572872 | tf_op jit(solution)/shard_map/ppermute | solution.py:50
  194.4 11.1 %collective-permute-start.55 = (bf16[192,1024]{1,0:T(8,128)(2,1)S(1)}, bf16[192,1024]{1,0:T(8,128)(2,1)S(1)}, u32[]{:S(2)}, u32[]{:S(2)}) collective-permute-start(bf16[192,1024]{1,0:T(8,128)(2,1)S(1)} %pad_maximum_fusion.21), channel_id=1, source_target_pairs={{0,2},{1,3},{4,0},{5,1},{8,4},{9,5},{12,8},{13,9},{14,12},{15,13},... | collective-permute-start | bytes 1179656 | tf_op jit(solution)/shard_map/ppermute | solution.py:46
  218.6 14.0 %collective-permute-start.62 = (bf16[256,1024]{1,0:T(8,128)(2,1)S(1)}, bf16[256,1024]{1,0:T(8,128)(2,1)S(1)}, u32[]{:S(2)}, u32[]{:S(2)}) collective-permute-start(bf16[256,1024]{1,0:T(8,128)(2,1)S(1)} %add_convert_fusion), channel_id=1, source_target_pairs={{0,16},{16,0},{1,17},{17,1},{2,18},{18,2},{3,19},{19,3},{4,20},{20... | collective-permute-start | bytes 1572872 | tf_op jit(solution)/shard_map/ppermute | solution.py:683
  (107 other events, 589.5 us)

commit v3 on v2

--- a/solution.py
+++ b/solution.py
@@ -698,11 +698,8 @@
             into[d] = [parts[i], swapped[i * tokens : (i + 1) * tokens]]
 
     extra = members
-    begin, end = tokens + extra, tokens + extra + piece
-    block = jnp.concatenate(
-        [latent, gate_rows(routes, gates, members, width), half_rows(w_out_t, replica)], axis=0
-    )
-    ring = Gather(block, chips, tokens)
+    block = jnp.concatenate([latent, gate_rows(routes, gates, members, width)], axis=0)
+    ring = Gather(block, chips, tokens // 2)
     forward, backward, kept = {}, {}, []
 
     def run_forward(i):
@@ -716,7 +713,7 @@
         share_out(groups[i], *out[2:], forward)
 
     def exchange(ds):
-        return partner(join([v for d in ds for v in cut(ring.got[d], begin, end)]))
+        return partner(join([v for d in ds for v in proj.got[d]]))
 
     def keep_half(ds, got):
         for i, d in enumerate(ds):
@@ -726,13 +723,16 @@
     grad_sib, block_sib, blocks, shard_rows = ring_step(
         chips,
         [ring],
-        (swap(grad_out, chips), swap(block[: tokens + extra], chips), blocks, w_out_t),
+        (swap(grad_out, chips), swap(block, chips), blocks, w_out_t),
     )
     grads = (grad_out, grad_sib)
+    proj = Gather(half_rows(shard_rows, replica), chips, piece // 32 * 16)
     other_half = {0: half_rows(shard_rows, 1 - replica)}
     for s in range(2, half + 1):
-        ds = [1 - s, s - 1]
-        out, got = ring_step(chips, [ring], (run_forward(s - 2), exchange(ds)))
+        ds = [2 - s, s - 2] if s > 2 else []
+        out, got = ring_step(
+            chips, [ring, proj], (run_forward(s - 2), exchange(ds) if ds else None)
+        )
         keep_forward(s - 2, out)
         keep_half(ds, got)
 
@@ -743,21 +743,23 @@
     first, second = len(ordered) * 3 // 7, len(ordered) * 5 // 7
     col_blocks = {0: blocks[0]}
 
-    out, got, cols = together(
-        run_forward(half - 1), exchange([half]), send_columns(ordered[:first])
+    ds = [1 - half, half - 1]
+    out, got, cols = ring_step(
+        chips, [proj], (run_forward(half - 1), exchange(ds), send_columns(ordered[:first]))
     )
     keep_forward(half - 1, out)
+    keep_half(ds, got)
+    col_blocks.update(zip(ordered[:first], cols))
+    comb = Scatter(forward, chips)
+    got, cols = ring_step(
+        chips, [comb], (exchange([half]), send_columns(ordered[first:second]))
+    )
     keep_half([half], got)
-    col_blocks.update(zip(ordered[:first], cols))
-
-    mine = [cut(ring.got[d], begin, end) for d in dists]
+    col_blocks.update(zip(ordered[first:second], cols))
+    mine = [proj.got[d] for d in dists]
     others = [[View(other_half[d])] for d in dists]
-    comb = Scatter(forward, chips)
     gc_own, gc_swap = grad_combined_part(own_parts, grads, mine, others, piece, width)
-    gc_other, cols = ring_step(
-        chips, [comb], (swap(gc_swap, chips), send_columns(ordered[first:second]))
-    )
-    col_blocks.update(zip(ordered[first:second], cols))
+    gc_other = swap(gc_swap, chips)
     grad_combined = (gc_own + gc_other).astype(BF16)
     grad_ring = Gather(grad_combined, chips, tokens // 2)
 

time: 235 us -> 233 us (level)
    ppermute x35 -> x37, waiting for transfers between devices: 55.5 us -> 52.3 us  [shift(): return lax.ppermute(x, 'expert', pairs)]
    unnamed x152 -> x148, local copies, waits for them, and re-layouts: 8.1 us -> 7.35 us
    ppermute x35 -> x37, starting transfers between devices: 43.5 us -> 44 us  [shift(): return lax.ppermute(x, 'expert', pairs)]
  transfers between devices with their start and end apart: 63 -> 65, of which waited for: 30 -> 32; matrix products, arithmetic and copies ran while one was open for 6% -> 6% of each run, Pallas kernels for 34% -> 35%
where the time goes in v3:
time: 233 us
  Pallas kernels  80.6 us (35%)
  waiting for transfers between devices  69.5 us (30%)
  starting transfers between devices  54.8 us (24%)
  other arithmetic  14.7 us (6%)
  local copies, waits for them, and re-layouts  11.1 us (5%)
    pallas_call x12, Pallas kernels, local_call(): pl.pallas_call(kernel, in_specs=[SMEM] * len(scalars) + [ANY] * len(array...  78.2 us
    ppermute x37, waiting for transfers between devices, shift(): return lax.ppermute(x, 'expert', pairs)  52.3 us
    ppermute x37, starting transfers between devices, shift(): return lax.ppermute(x, 'expert', pairs)  44 us
    ppermute x5, waiting for transfers between devices, partner(): return lax.ppermute(x, 'dp', [(i, (i + 1) % dp) for i in range(dp)])  10.1 us
    unnamed x148, local copies, waits for them, and re-layouts  7.35 us
    ppermute x23, waiting for transfers between devices, swap(): return lax.ppermute(x, 'expert', [(i, i ^ 1) for i in range(2 * chips)])  7.12 us
    ppermute x5, starting transfers between devices, partner(): return lax.ppermute(x, 'dp', [(i, (i + 1) % dp) for i in range(dp)])  6.83 us
  transfers between devices with their start and end apart: 65, of which 32 were waited for; matrix products, arithmetic and copies ran while one was open for 6% of the time, Pallas kernels for 35%

profile of v3, /device:TPU:0, one launch (start us, length us, event | category | flops | bytes accessed | tf_op | source)
XLA Modules:
  0.0 232.7 jit_solution(13884837908365834527)
XLA Ops:
  3.0 3.0 %collective-permute-start.1 = (bf16[144,1024]{1,0:T(8,128)(2,1)S(1)}, bf16[144,1024]{1,0:T(8,128)(2,1)S(1)}, u32[]{:S(2)}, u32[]{:S(2)}) collective-permute-start(bf16[144,1024]{1,0:T(8,128)(2,1)S(1)} %pad_maximum_fusion.24.refs_0_.refs_5_), channel_id=1, source_target_pairs={{0,2},{1,3},{4,0},{5,1},{8,4},{9,5},{12,8},{13,9},{14,12},{15,13},... | collective-permute-start | bytes 884744 | tf_op jit(solution)/shard_map/ppermute | solution.py:46
  7.3 3.0 %column_blocks.1 = (bf16[128,512]{1,0:T(8,128)(2,1)}, bf16[128,512]{1,0:T(8,128)(2,1)}, bf16[128,512]{1,0:T(8,128)(2,1)}, bf16[128,512]{1,0:T(8,128)(2,1)}, bf16...) custom-call(s32[8]{0:T(128)} %get-tuple-element.286.chip_ref, ...), custom_call_target="tpu_custom_call" | custom-call | bytes 2097152 | tf_op jit(solution)/shard_map/column_blocks/pallas_call | solution.py:157
  10.3 3.0 %collective-permute-done.1.refs_4_.refs_9_ = bf16[144,1024]{1,0:T(8,128)(2,1)S(1)} collective-permute-done((bf16[144,1024]{1,0:T(8,128)(2,1)S(1)}, bf16[144,1024]{1,0:T(8,128)(2,1)S(1)}, u32[]{:S(2)}, u32[]{:S(2)}) %collective-permute-start.1) | collective-permute-done | bytes 294944 | tf_op jit(solution)/shard_map/ppermute | solution.py:46
  19.4 8.8 %expert_forward.4 = (bf16[480,2048]{1,0:T(8,128)(2,1)}, f32[480,128]{1,0:T(8,128)}, bf16[128,1024]{1,0:T(8,128)(2,1)}, bf16[128,1024]{1,0:T(8,128)(2,1)}, bf16[1...) custom-call(s32[1]{0:T(128)} %bitcast.2.me_ref, bf16[144,1024]{1,0:T(8,128)(2,1)} %copy-done.37, ...), custom_call_target="tpu_custom_call" | custom-call | flops 4026531840 | bytes 8388608 | tf_op jit(solution)/shard_map/expert_forward/pallas_call | solution.py:157
  28.3 4.4 %collective-permute-done.5.refs_2_.refs_5_.refs_6_ = bf16[272,1024]{1,0:T(8,128)(2,1)S(1)} collective-permute-done((bf16[272,1024]{1,0:T(8,128)(2,1)}, bf16[272,1024]{1,0:T(8,128)(2,1)S(1)}, u32[]{:S(2)}, u32[]{:S(2)}) %collective-permute-start.5) | collective-permute-done | bytes 557088 | tf_op jit(solution)/shard_map/ppermute | solution.py:46
  39.0 7.3 %expert_forward.5 = (bf16[320,2048]{1,0:T(8,128)(2,1)}, f32[320,128]{1,0:T(8,128)}, bf16[128,1024]{1,0:T(8,128)(2,1)}, bf16[128,1024]{1,0:T(8,128)(2,1)}, bf16[256,1024]{1,0:T(8,128)(2,1)}) custom-call(s32[1]{0:T(128)} %bitcast.2.me_ref, bf16[272,1024]{1,0:T(8,128)(2,1)} %copy-done.3, bf16[288,1024]{1,0:T(8,128)(2,1)} %copy-done.13, ...), custom_call_target="tpu_custom_call" | custom-call | flops 2684354560 | bytes 8388608 | tf_op jit(solution)/shard_map/expert_forward/pallas_call | solution.py:157
  46.4 3.6 %collective-permute-done.10 = bf16[256,1024]{1,0:T(8,128)(2,1)S(1)} collective-permute-done((bf16[256,1024]{1,0:T(8,128)(2,1)S(1)}, bf16[256,1024]{1,0:T(8,128)(2,1)S(1)}, u32[]{:S(2)}, u32[]{:S(2)}) %collective-permute-start.10) | collective-permute-done | bytes 524320 | tf_op jit(solution)/shard_map/ppermute | solution.py:683
  54.7 2.8 %collective-permute-start.21 = (bf16[128,512]{1,0:T(8,128)(2,1)}, bf16[128,512]{1,0:T(8,128)(2,1)S(1)}, u32[]{:S(2)}, u32[]{:S(2)}) collective-permute-start(bf16[128,512]{1,0:T(8,128)(2,1)} %get-tuple-element.186), channel_id=1, source_target_pairs={{0,14},{1,15},{4,10},{5,11},{8,6},{9,7},{12,2},{13,3},{14,0},{15,1... | collective-permute-start | bytes 393224 | tf_op jit(solution)/shard_map/ppermute | solution.py:46
  58.3 7.3 %expert_forward.6 = (bf16[320,2048]{1,0:T(8,128)(2,1)}, f32[320,128]{1,0:T(8,128)}, bf16[128,1024]{1,0:T(8,128)(2,1)}, bf16[128,1024]{1,0:T(8,128)(2,1)}, bf16[256,1024]{1,0:T(8,128)(2,1)}) custom-call(s32[1]{0:T(128)} %bitcast.2.me_ref, bf16[272,1024]{1,0:T(8,128)(2,1)} %copy-done.1, bf16[288,1024]{1,0:T(8,128)(2,1)} %copy-done.12, ...), custom_call_target="tpu_custom_call" | custom-call | flops 2684354560 | bytes 8388608 | tf_op jit(solution)/shard_map/expert_forward/pallas_call | solution.py:157
  67.9 4.6 %collective-permute-start.22 = (bf16[128,512]{1,0:T(8,128)(2,1)}, bf16[128,512]{1,0:T(8,128)(2,1)S(1)}, u32[]{:S(2)}, u32[]{:S(2)}) collective-permute-start(bf16[128,512]{1,0:T(8,128)(2,1)} %get-tuple-element.187), channel_id=1, source_target_pairs={{0,10},{1,11},{4,6},{5,7},{8,2},{9,3},{12,0},{13,1},{14,4},{15,5},... | collective-permute-start | bytes 393224 | tf_op jit(solution)/shard_map/ppermute | solution.py:46
  75.4 5.7 %expert_forward.7 = (bf16[160,2048]{1,0:T(8,128)(2,1)}, f32[160,128]{1,0:T(8,128)}, bf16[128,1024]{1,0:T(8,128)(2,1)}, bf16[128,1024]{1,0:T(8,128)(2,1)}) custom-call(s32[1]{0:T(128)} %bitcast.2.me_ref, bf16[192,1024]{1,0:T(8,128)(2,1)} %copy-done.5, bf16[208,1024]{1,0:T(8,128)(2,1)} %copy-done.4, bf16[144,1024]{1,0:T(8,128)(2,1)} %copy-done.18, ...), custom_call_target="tpu_custom_call" | custom-call | flops 1342177280 | bytes 8388608 | tf_op jit(solution)/shard_map/expert_forward/pallas_call | solution.py:157
  81.2 3.0 %collective-permute-start.28 = (bf16[128,512]{1,0:T(8,128)(2,1)S(1)}, bf16[128,512]{1,0:T(8,128)(2,1)S(1)}, u32[]{:S(2)}, u32[]{:S(2)}) collective-permute-start(bf16[128,512]{1,0:T(8,128)(2,1)S(1)} %copy-done.72), channel_id=1, source_target_pairs={{0,6},{1,7},{4,2},{5,3},{8,0},{9,1},{12,4},{13,5},{14,8},{15,9},{1... | collective-permute-start | bytes 393224 | tf_op jit(solution)/shard_map/ppermute | solution.py:46
  90.8 3.2 %collective-permute-done.27.refs_18_ = bf16[128,1024]{1,0:T(8,128)(2,1)S(1)} collective-permute-done((bf16[128,1024]{1,0:T(8,128)(2,1)S(1)}, bf16[128,1024]{1,0:T(8,128)(2,1)S(1)}, u32[]{:S(2)}, u32[]{:S(2)}) %collective-permute-start.27) | collective-permute-done | bytes 262176 | tf_op jit(solution)/shard_map/ppermute | solution.py:683
  94.8 5.4 %grad_combined.1 = (f32[128,1024]{1,0:T(8,128)}, f32[128,1024]{1,0:T(8,128)}) custom-call(s32[16]{0:T(128)} %pad_add_fusion.offsets, bf16[128,4096]{1,0:T(8,128)(2,1)} %refs_0_.1, bf16[128,4096]{1,0:T(8,128)(2,1)} %copy-done.25, bf16[128,1024]{1,0:T(8,128)(2,1)} %copy-done.6, bf16[128,1024]{1,0:T(8,128)(2,1)} %get-tuple-element.305.refs_3_, ...), custom_call_target="tpu_custom_call" | custom-call | flops 1073741824 | bytes 4194304 | tf_op jit(solution)/shard_map/grad_combined/pallas_call | solution.py:157
  100.6 1.8 collective-permute-done.30
  105.2 1.8 collective-permute-done.33.refs_1_
  106.9 9.6 %collective-permute-done.32.refs_4_ = bf16[256,1024]{1,0:T(8,128)(2,1)S(1)} collective-permute-done((bf16[256,1024]{1,0:T(8,128)(2,1)S(1)}, bf16[256,1024]{1,0:T(8,128)(2,1)S(1)}, u32[]{:S(2)}, u32[]{:S(2)}) %collective-permute-start.32) | collective-permute-done | bytes 524320 | tf_op jit(solution)/shard_map/ppermute | solution.py:46
  121.9 8.9 %expert_backward.4 = (bf16[128,1024]{1,0:T(8,128)(2,1)}, bf16[128,1024]{1,0:T(8,128)(2,1)}, bf16[128,1024]{1,0:T(8,128)(2,1)}, bf16[384,1024]{1,0:T(8,128)(2,1)}) custom-call(bf16[128,1024]{1,0:T(8,128)(2,1)} %copy-done.29, bf16[128,1024]{1,0:T(8,128)(2,1)} %copy-done.68, bf16[256,1024]{1,0:T(8,128)(2,1)} %copy-done.36, ...), custom_call_target="tpu_custom_call" | custom-call | flops 4026531840 | bytes 8388608 | tf_op jit(solution)/shard_map/expert_backward/pallas_call | solution.py:157
  130.8 3.4 %collective-permute-done.34.refs_0_ = bf16[256,1024]{1,0:T(8,128)(2,1)S(1)} collective-permute-done((bf16[256,1024]{1,0:T(8,128)(2,1)S(1)}, bf16[256,1024]{1,0:T(8,128)(2,1)S(1)}, u32[]{:S(2)}, u32[]{:S(2)}) %collective-permute-start.34) | collective-permute-done | bytes 524320 | tf_op jit(solution)/shard_map/ppermute | solution.py:46
  135.9 1.8 collective-permute-start.39
  138.8 7.3 %expert_backward.5 = (bf16[128,1024]{1,0:T(8,128)(2,1)}, bf16[128,1024]{1,0:T(8,128)(2,1)}, bf16[256,1024]{1,0:T(8,128)(2,1)}) custom-call(bf16[256,1024]{1,0:T(8,128)(2,1)} %copy-done.14, bf16[256,1024]{1,0:T(8,128)(2,1)} %copy-done.32, bf16[256,1024]{1,0:T(8,128)(2,1)} %copy-done.15, bf16[320,2048]{1,0:T(8,128)(2,1)} %get-tuple-element.222.refs_3_, ...), custom_call_target="tpu_custom_call" | custom-call | flops 2684354560 | bytes 8388608 | tf_op jit(solution)/shard_map/expert_backward/pallas_call | solution.py:157
  146.1 4.2 %collective-permute-done.39.refs_0_ = bf16[256,1024]{1,0:T(8,128)(2,1)S(1)} collective-permute-done((bf16[256,1024]{1,0:T(8,128)(2,1)S(1)}, bf16[256,1024]{1,0:T(8,128)(2,1)S(1)}, u32[]{:S(2)}, u32[]{:S(2)}) %collective-permute-start.39) | collective-permute-done | bytes 524320 | tf_op jit(solution)/shard_map/ppermute | solution.py:46
  156.0 7.3 %expert_backward.6 = (bf16[128,1024]{1,0:T(8,128)(2,1)}, bf16[128,1024]{1,0:T(8,128)(2,1)}, bf16[256,1024]{1,0:T(8,128)(2,1)}) custom-call(bf16[256,1024]{1,0:T(8,128)(2,1)} %copy-done.10, bf16[256,1024]{1,0:T(8,128)(2,1)} %copy-done.31, bf16[256,1024]{1,0:T(8,128)(2,1)} %copy-done.11, bf16[320,2048]{1,0:T(8,128)(2,1)} %get-tuple-element.232.refs_3_, ...), custom_call_target="tpu_custom_call" | custom-call | flops 2684354560 | bytes 8388608 | tf_op jit(solution)/shard_map/expert_backward/pallas_call | solution.py:157
  168.9 6.7 %expert_backward.7 = (bf16[128,1024]{1,0:T(8,128)(2,1)}, bf16[128,1024]{1,0:T(8,128)(2,1)}) custom-call(bf16[192,1024]{1,0:T(8,128)(2,1)} %copy-done.9, bf16[192,1024]{1,0:T(8,128)(2,1)} %copy-done.8, bf16[128,1024]{1,0:T(8,128)(2,1)} %copy-done.42, bf16[160,2048]{1,0:T(8,128)(2,1)} %get-tuple-element.239.refs_3_, f32[160,128]{1,0:T(8,128)} %get-tuple-element.240.refs_4_, ...), custom_call_target="tpu_custom_call" | custom-call | flops 1342177280 | bytes 8388608 | tf_op jit(solution)/shard_map/expert_backward/pallas_call | solution.py:157
  181.8 6.0 %mixed.1 = (bf16[128,2048]{1,0:T(8,128)(2,1)}, bf16[128,2048]{1,0:T(8,128)(2,1)}) custom-call(bf16[128,1024]{1,0:T(8,128)(2,1)} %copy-done.7, bf16[128,1024]{1,0:T(8,128)(2,1)} %copy-done.40, bf16[128,1024]{1,0:T(8,128)(2,1)} %copy-done.6, bf16[128,1024]{1,0:T(8,128)(2,1)} %get-tuple-element.305.refs_3_, bf16[272,1024]{1,0:T(8,128)(2,1)} %copy-done.3, ...), custom_call_target="tpu_custom_call" | custom-call | flops 1073741824 | bytes 4194304 | tf_op jit(solution)/shard_map/mixed/pallas_call | solution.py:157
  188.1 2.7 %collective-permute-done.53.refs_13_ = bf16[192,1024]{1,0:T(8,128)(2,1)S(1)} collective-permute-done((bf16[192,1024]{1,0:T(8,128)(2,1)S(1)}, bf16[192,1024]{1,0:T(8,128)(2,1)S(1)}, u32[]{:S(2)}, u32[]{:S(2)}) %collective-permute-start.53) | collective-permute-done | bytes 393248 | tf_op jit(solution)/shard_map/ppermute | solution.py:46
  194.5 9.0 %collective-permute-done.56.refs_15_ = bf16[192,1024]{1,0:T(8,128)(2,1)S(1)} collective-permute-done((bf16[192,1024]{1,0:T(8,128)(2,1)S(1)}, bf16[192,1024]{1,0:T(8,128)(2,1)S(1)}, u32[]{:S(2)}, u32[]{:S(2)}) %collective-permute-start.56) | collective-permute-done | bytes 393248 | tf_op jit(solution)/shard_map/ppermute | solution.py:46
  207.3 4.6 %weight_grad.1 = (f32[256,1024]{1,0:T(8,128)}, bf16[256,1024]{1,0:T(8,128)(2,1)}) custom-call(s32[1]{0:T(128)} %bitcast.5.core_ref, bf16[128,512]{1,0:T(8,128)(2,1)} %get-tuple-element.261.refs_0_, bf16[128,512]{1,0:T(8,128)(2,1)} %copy-done.61, bf16[128,512]{1,0:T(8,128)(2,1)} %copy-done.60, bf16[128,512]{1,0:T(8,128)(2,1)} %copy-done.59, ...), custom_call_target="tpu_custom_call" | custom-call | flops 1073741824 | bytes 3145728 | tf_op jit(solution)/shard_map/weight_grad/pallas_call | solution.py:157
  213.0 2.3 collective-permute-done.63
  221.2 2.4 %place_columns.1 = bf16[128,4096]{1,0:T(8,128)(2,1)} custom-call(s32[32]{0:T(128)} %pad_add_fusion.1.offsets, bf16[128,2048]{1,0:T(8,128)(2,1)} %get-tuple-element.277.own_ref, bf16[128,2048]{1,0:T(8,128)(2,1)} %copy-done.30), custom_call_target="tpu_custom_call" | custom-call | bytes 2097152 | tf_op jit(solution)/shard_map/place_columns/pallas_call | solution.py:591
  223.6 3.0 %collective-permute-done.62 = bf16[128,1024]{1,0:T(8,128)(2,1)S(1)} collective-permute-done((bf16[128,1024]{1,0:T(8,128)(2,1)S(1)}, bf16[128,1024]{1,0:T(8,128)(2,1)S(1)}, u32[]{:S(2)}, u32[]{:S(2)}) %collective-permute-start.62) | collective-permute-done | bytes 262176 | tf_op jit(solution)/shard_map/ppermute | solution.py:46
  227.4 3.3 %collective-permute-done.64 = bf16[256,1024]{1,0:T(8,128)(2,1)S(1)} collective-permute-done((bf16[256,1024]{1,0:T(8,128)(2,1)S(1)}, bf16[256,1024]{1,0:T(8,128)(2,1)S(1)}, u32[]{:S(2)}, u32[]{:S(2)}) %collective-permute-start.64) | collective-permute-done | bytes 524320 | tf_op jit(solution)/shard_map/ppermute | solution.py:683
  (342 shorter events, 79.8 us)
Async XLA Ops:
  0.6 14.1 %collective-permute-start.2 = (bf16[128,4096]{1,0:T(8,128)(2,1)}, bf16[128,4096]{1,0:T(8,128)(2,1)S(1)}, u32[]{:S(2)}, u32[]{:S(2)}) collective-permute-start(bf16[128,4096]{1,0:T(8,128)(2,1)} %refs_0_.1), channel_id=1, source_target_pairs={{0,1},{1,0},{2,3},{3,2},{4,5},{5,4},{6,7},{7,6},{8,9},{9,8},{10,11... | collective-permute-start | bytes 3145736 | tf_op jit(solution)/shard_map/ppermute | solution.py:50
  17.4 15.3 %collective-permute-start.5 = (bf16[272,1024]{1,0:T(8,128)(2,1)}, bf16[272,1024]{1,0:T(8,128)(2,1)S(1)}, u32[]{:S(2)}, u32[]{:S(2)}) collective-permute-start(bf16[272,1024]{1,0:T(8,128)(2,1)} %get-tuple-element.323), channel_id=1, source_target_pairs={{0,2},{1,3},{4,0},{5,1},{8,4},{9,5},{12,8},{13,9},{14,12},{15,13},... | collective-permute-start | bytes 1671176 | tf_op jit(solution)/shard_map/ppermute | solution.py:46
  19.0 14.8 %collective-permute-start.4 = (bf16[272,1024]{1,0:T(8,128)(2,1)S(1)}, bf16[272,1024]{1,0:T(8,128)(2,1)S(1)}, u32[]{:S(2)}, u32[]{:S(2)}) collective-permute-start(bf16[272,1024]{1,0:T(8,128)(2,1)S(1)} %get-tuple-element.324), channel_id=1, source_target_pairs={{0,4},{1,5},{4,8},{5,9},{8,12},{9,13},{12,14},{13,15},{14,10},{15,... | collective-permute-start | bytes 1671176 | tf_op jit(solution)/shard_map/ppermute | solution.py:46
  34.6 15.3 %collective-permute-start.7 = (bf16[272,1024]{1,0:T(8,128)(2,1)S(1)}, bf16[272,1024]{1,0:T(8,128)(2,1)S(1)}, u32[]{:S(2)}, u32[]{:S(2)}) collective-permute-start(bf16[272,1024]{1,0:T(8,128)(2,1)S(1)} %collective-permute-done.4.refs_0_.refs_3_.refs_4_), channel_id=1, source_target_pairs={{0,4},{1,5},{4,8},{5,9},{8,12},{9,13},{12,14},{13,15},{14,10},{15,... | collective-permute-start | bytes 1671176 | tf_op jit(solution)/shard_map/ppermute | solution.py:46
  35.0 14.9 %collective-permute-start.8 = (bf16[272,1024]{1,0:T(8,128)(2,1)S(1)}, bf16[272,1024]{1,0:T(8,128)(2,1)S(1)}, u32[]{:S(2)}, u32[]{:S(2)}) collective-permute-start(bf16[272,1024]{1,0:T(8,128)(2,1)S(1)} %collective-permute-done.5.refs_2_.refs_5_.refs_6_), channel_id=1, source_target_pairs={{0,2},{1,3},{4,0},{5,1},{8,4},{9,5},{12,8},{13,9},{14,12},{15,13},... | collective-permute-start | bytes 1671176 | tf_op jit(solution)/shard_map/ppermute | solution.py:46
  36.7 13.3 %collective-permute-start.10 = (bf16[256,1024]{1,0:T(8,128)(2,1)S(1)}, bf16[256,1024]{1,0:T(8,128)(2,1)S(1)}, u32[]{:S(2)}, u32[]{:S(2)}) collective-permute-start(bf16[256,1024]{1,0:T(8,128)(2,1)S(1)} %pad_maximum_fusion.11), channel_id=1, source_target_pairs={{0,16},{16,0},{1,17},{17,1},{2,18},{18,2},{3,19},{19,3},{4,20},{20... | collective-permute-start | bytes 1572872 | tf_op jit(solution)/shard_map/ppermute | solution.py:683
  50.2 15.4 %collective-permute-start.15 = (bf16[256,1024]{1,0:T(8,128)(2,1)S(1)}, bf16[256,1024]{1,0:T(8,128)(2,1)S(1)}, u32[]{:S(2)}, u32[]{:S(2)}) collective-permute-start(bf16[256,1024]{1,0:T(8,128)(2,1)S(1)} %pad_maximum_fusion.12), channel_id=1, source_target_pairs={{0,16},{16,0},{1,17},{17,1},{2,18},{18,2},{3,19},{19,3},{4,20},{20... | collective-permute-start | bytes 1572872 | tf_op jit(solution)/shard_map/ppermute | solution.py:683
  51.9 13.8 %collective-permute-start.13 = (bf16[208,1024]{1,0:T(8,128)(2,1)S(1)}, bf16[208,1024]{1,0:T(8,128)(2,1)S(1)}, u32[]{:S(2)}, u32[]{:S(2)}) collective-permute-start(bf16[208,1024]{1,0:T(8,128)(2,1)S(1)} %concatenate.120), channel_id=1, source_target_pairs={{0,2},{1,3},{4,0},{5,1},{8,4},{9,5},{12,8},{13,9},{14,12},{15,13},... | collective-permute-start | bytes 1277960 | tf_op jit(solution)/shard_map/ppermute | solution.py:46
  54.2 11.4 %collective-permute-start.12 = (bf16[192,1024]{1,0:T(8,128)(2,1)}, bf16[192,1024]{1,0:T(8,128)(2,1)S(1)}, u32[]{:S(2)}, u32[]{:S(2)}) collective-permute-start(bf16[192,1024]{1,0:T(8,128)(2,1)} %pad_maximum_fusion.19), channel_id=1, source_target_pairs={{0,4},{1,5},{4,8},{5,9},{8,12},{9,13},{12,14},{13,15},{14,10},{15,... | collective-permute-start | bytes 1179656 | tf_op jit(solution)/shard_map/ppermute | solution.py:46
  54.7 17.8 %collective-permute-start.21 = (bf16[128,512]{1,0:T(8,128)(2,1)}, bf16[128,512]{1,0:T(8,128)(2,1)S(1)}, u32[]{:S(2)}, u32[]{:S(2)}) collective-permute-start(bf16[128,512]{1,0:T(8,128)(2,1)} %get-tuple-element.186), channel_id=1, source_target_pairs={{0,14},{1,15},{4,10},{5,11},{8,6},{9,7},{12,2},{13,3},{14,0},{15,1... | collective-permute-start | bytes 393224 | tf_op jit(solution)/shard_map/ppermute | solution.py:46
  66.6 17.7 %collective-permute-start.20 = (bf16[256,1024]{1,0:T(8,128)(2,1)S(1)}, bf16[256,1024]{1,0:T(8,128)(2,1)S(1)}, u32[]{:S(2)}, u32[]{:S(2)}) collective-permute-start(bf16[256,1024]{1,0:T(8,128)(2,1)S(1)} %pad_maximum_fusion.13), channel_id=1, source_target_pairs={{0,16},{16,0},{1,17},{17,1},{2,18},{18,2},{3,19},{19,3},{4,20},{20... | collective-permute-start | bytes 1572872 | tf_op jit(solution)/shard_map/ppermute | solution.py:683
  67.9 13.3 %collective-permute-start.22 = (bf16[128,512]{1,0:T(8,128)(2,1)}, bf16[128,512]{1,0:T(8,128)(2,1)S(1)}, u32[]{:S(2)}, u32[]{:S(2)}) collective-permute-start(bf16[128,512]{1,0:T(8,128)(2,1)} %get-tuple-element.187), channel_id=1, source_target_pairs={{0,10},{1,11},{4,6},{5,7},{8,2},{9,3},{12,0},{13,1},{14,4},{15,5},... | collective-permute-start | bytes 393224 | tf_op jit(solution)/shard_map/ppermute | solution.py:46
  72.4 11.7 %collective-permute-start.23 = (bf16[128,512]{1,0:T(8,128)(2,1)S(1)}, bf16[128,512]{1,0:T(8,128)(2,1)S(1)}, u32[]{:S(2)}, u32[]{:S(2)}) collective-permute-start(bf16[128,512]{1,0:T(8,128)(2,1)S(1)} %copy-done.73), channel_id=1, source_target_pairs={{0,12},{1,13},{4,14},{5,15},{8,10},{9,11},{12,6},{13,7},{14,2},{15... | collective-permute-start | bytes 393224 | tf_op jit(solution)/shard_map/ppermute | solution.py:46
  72.5 11.7 %collective-permute-start.18 = (bf16[64,1024]{1,0:T(8,128)(2,1)S(1)}, bf16[64,1024]{1,0:T(8,128)(2,1)S(1)}, u32[]{:S(2)}, u32[]{:S(2)}) collective-permute-start(bf16[64,1024]{1,0:T(8,128)(2,1)S(1)} %slice.254), channel_id=1, source_target_pairs={{0,2},{1,3},{4,0},{5,1},{8,4},{9,5},{12,8},{13,9},{14,12},{15,13},... | collective-permute-start | bytes 393224 | tf_op jit(solution)/shard_map/ppermute | solution.py:46
  84.2 16.0 %collective-permute-start.16 = (bf16[256,1024]{1,0:T(8,128)(2,1)}, bf16[256,1024]{1,0:T(8,128)(2,1)S(1)}, u32[]{:S(2)}, u32[]{:S(2)}) collective-permute-start(bf16[256,1024]{1,0:T(8,128)(2,1)} %get-tuple-element.179), channel_id=1, source_target_pairs={{0,1},{1,0},{2,3},{3,2},{4,5},{5,4},{6,7},{7,6},{8,9},{9,8},{10,11... | collective-permute-start | bytes 1572872 | tf_op jit(solution)/shard_map/ppermute | solution.py:50
  102.6 14.0 %collective-permute-start.32 = (bf16[256,1024]{1,0:T(8,128)(2,1)S(1)}, bf16[256,1024]{1,0:T(8,128)(2,1)S(1)}, u32[]{:S(2)}, u32[]{:S(2)}) collective-permute-start(bf16[256,1024]{1,0:T(8,128)(2,1)S(1)} %get-tuple-element.319), channel_id=1, source_target_pairs={{0,2},{1,3},{4,0},{5,1},{8,4},{9,5},{12,8},{13,9},{14,12},{15,13},... | collective-permute-start | bytes 1572872 | tf_op jit(solution)/shard_map/ppermute | solution.py:46
  104.2 13.7 %collective-permute-start.31 = (bf16[256,1024]{1,0:T(8,128)(2,1)S(1)}, bf16[256,1024]{1,0:T(8,128)(2,1)S(1)}, u32[]{:S(2)}, u32[]{:S(2)}) collective-permute-start(bf16[256,1024]{1,0:T(8,128)(2,1)S(1)} %get-tuple-element.320), channel_id=1, source_target_pairs={{0,4},{1,5},{4,8},{5,9},{8,12},{9,13},{12,14},{13,15},{14,10},{15,... | collective-permute-start | bytes 1572872 | tf_op jit(solution)/shard_map/ppermute | solution.py:46
  104.6 13.4 %collective-permute-start.11 = (bf16[256,1024]{1,0:T(8,128)(2,1)S(1)}, bf16[256,1024]{1,0:T(8,128)(2,1)S(1)}, u32[]{:S(2)}, u32[]{:S(2)}) collective-permute-start(bf16[256,1024]{1,0:T(8,128)(2,1)S(1)} %copy-done.65), channel_id=1, source_target_pairs={{0,1},{1,0},{2,3},{3,2},{4,5},{5,4},{6,7},{7,6},{8,9},{9,8},{10,11... | collective-permute-start | bytes 1572872 | tf_op jit(solution)/shard_map/ppermute | solution.py:50
  119.9 15.1 %collective-permute-start.38 = (bf16[384,1024]{1,0:T(8,128)(2,1)S(1)}, bf16[384,1024]{1,0:T(8,128)(2,1)S(1)}, u32[]{:S(2)}, u32[]{:S(2)}) collective-permute-start(bf16[384,1024]{1,0:T(8,128)(2,1)S(1)} %copy-done.63), channel_id=1, source_target_pairs={{0,1},{1,0},{2,3},{3,2},{4,5},{5,4},{6,7},{7,6},{8,9},{9,8},{10,11... | collective-permute-start | bytes 2359304 | tf_op jit(solution)/shard_map/ppermute | solution.py:50
  119.9 14.3 %collective-permute-start.34 = (bf16[256,1024]{1,0:T(8,128)(2,1)S(1)}, bf16[256,1024]{1,0:T(8,128)(2,1)S(1)}, u32[]{:S(2)}, u32[]{:S(2)}) collective-permute-start(bf16[256,1024]{1,0:T(8,128)(2,1)S(1)} %get-tuple-element.317), channel_id=1, source_target_pairs={{0,4},{1,5},{4,8},{5,9},{8,12},{9,13},{12,14},{13,15},{14,10},{15,... | collective-permute-start | bytes 1572872 | tf_op jit(solution)/shard_map/ppermute | solution.py:46
  120.8 14.1 %collective-permute-start.35 = (bf16[256,1024]{1,0:T(8,128)(2,1)S(1)}, bf16[256,1024]{1,0:T(8,128)(2,1)S(1)}, u32[]{:S(2)}, u32[]{:S(2)}) collective-permute-start(bf16[256,1024]{1,0:T(8,128)(2,1)S(1)} %get-tuple-element.318), channel_id=1, source_target_pairs={{0,2},{1,3},{4,0},{5,1},{8,4},{9,5},{12,8},{13,9},{14,12},{15,13},... | collective-permute-start | bytes 1572872 | tf_op jit(solution)/shard_map/ppermute | solution.py:46
  135.9 14.3 %collective-permute-start.39 = (bf16[256,1024]{1,0:T(8,128)(2,1)S(1)}, bf16[256,1024]{1,0:T(8,128)(2,1)S(1)}, u32[]{:S(2)}, u32[]{:S(2)}) collective-permute-start(bf16[256,1024]{1,0:T(8,128)(2,1)S(1)} %get-tuple-element.314), channel_id=1, source_target_pairs={{0,4},{1,5},{4,8},{5,9},{8,12},{9,13},{12,14},{13,15},{14,10},{15,... | collective-permute-start | bytes 1572872 | tf_op jit(solution)/shard_map/ppermute | solution.py:46
  137.7 14.0 %collective-permute-start.40 = (bf16[256,1024]{1,0:T(8,128)(2,1)S(1)}, bf16[256,1024]{1,0:T(8,128)(2,1)S(1)}, u32[]{:S(2)}, u32[]{:S(2)}) collective-permute-start(bf16[256,1024]{1,0:T(8,128)(2,1)S(1)} %get-tuple-element.315), channel_id=1, source_target_pairs={{0,2},{1,3},{4,0},{5,1},{8,4},{9,5},{12,8},{13,9},{14,12},{15,13},... | collective-permute-start | bytes 1572872 | tf_op jit(solution)/shard_map/ppermute | solution.py:46
  164.2 12.4 %collective-permute-start.51 = (bf16[128,1024]{1,0:T(8,128)(2,1)S(1)}, bf16[128,1024]{1,0:T(8,128)(2,1)S(1)}, u32[]{:S(2)}, u32[]{:S(2)}) collective-permute-start(bf16[128,1024]{1,0:T(8,128)(2,1)S(1)} %add_convert_fusion.7.refs_0_.refs_8_), channel_id=1, source_target_pairs={{0,1},{1,0},{2,3},{3,2},{4,5},{5,4},{6,7},{7,6},{8,9},{9,8},{10,11... | collective-permute-start | bytes 786440 | tf_op jit(solution)/shard_map/ppermute | solution.py:50
  164.8 11.9 %collective-permute-start.47 = (bf16[128,1024]{1,0:T(8,128)(2,1)S(1)}, bf16[128,1024]{1,0:T(8,128)(2,1)S(1)}, u32[]{:S(2)}, u32[]{:S(2)}) collective-permute-start(bf16[128,1024]{1,0:T(8,128)(2,1)S(1)} %slice.292), channel_id=1, source_target_pairs={{0,2},{1,3},{4,0},{5,1},{8,4},{9,5},{12,8},{13,9},{14,12},{15,13},... | collective-permute-start | bytes 786440 | tf_op jit(solution)/shard_map/ppermute | solution.py:46
  176.7 11.1 %collective-permute-start.55 = (bf16[256,1024]{1,0:T(8,128)(2,1)}, bf16[256,1024]{1,0:T(8,128)(2,1)S(1)}, u32[]{:S(2)}, u32[]{:S(2)}) collective-permute-start(bf16[256,1024]{1,0:T(8,128)(2,1)} %get-tuple-element.254), channel_id=1, source_target_pairs={{0,1},{1,0},{2,3},{3,2},{4,5},{5,4},{6,7},{7,6},{8,9},{9,8},{10,11... | collective-permute-start | bytes 1572872 | tf_op jit(solution)/shard_map/ppermute | solution.py:50
  179.5 11.2 %collective-permute-start.53 = (bf16[192,1024]{1,0:T(8,128)(2,1)S(1)}, bf16[192,1024]{1,0:T(8,128)(2,1)S(1)}, u32[]{:S(2)}, u32[]{:S(2)}) collective-permute-start(bf16[192,1024]{1,0:T(8,128)(2,1)S(1)} %pad_maximum_fusion.20), channel_id=1, source_target_pairs={{0,4},{1,5},{4,8},{5,9},{8,12},{9,13},{12,14},{13,15},{14,10},{15,... | collective-permute-start | bytes 1179656 | tf_op jit(solution)/shard_map/ppermute | solution.py:46
  180.7 10.9 %collective-permute-start.54 = (bf16[192,1024]{1,0:T(8,128)(2,1)S(1)}, bf16[192,1024]{1,0:T(8,128)(2,1)S(1)}, u32[]{:S(2)}, u32[]{:S(2)}) collective-permute-start(bf16[192,1024]{1,0:T(8,128)(2,1)S(1)} %pad_maximum_fusion.21), channel_id=1, source_target_pairs={{0,2},{1,3},{4,0},{5,1},{8,4},{9,5},{12,8},{13,9},{14,12},{15,13},... | collective-permute-start | bytes 1179656 | tf_op jit(solution)/shard_map/ppermute | solution.py:46
  181.8 23.1 %collective-permute-start.42 = (bf16[256,1024]{1,0:T(8,128)(2,1)}, bf16[256,1024]{1,0:T(8,128)(2,1)S(1)}, u32[]{:S(2)}, u32[]{:S(2)}) collective-permute-start(bf16[256,1024]{1,0:T(8,128)(2,1)} %get-tuple-element.228), channel_id=1, source_target_pairs={{0,1},{1,0},{2,3},{3,2},{4,5},{5,4},{6,7},{7,6},{8,9},{9,8},{10,11... | collective-permute-start | bytes 1572872 | tf_op jit(solution)/shard_map/ppermute | solution.py:50
  191.8 13.1 %collective-permute-start.58 = (bf16[128,2048]{1,0:T(8,128)(2,1)S(1)}, bf16[128,2048]{1,0:T(8,128)(2,1)S(1)}, u32[]{:S(2)}, u32[]{:S(2)}) collective-permute-start(bf16[128,2048]{1,0:T(8,128)(2,1)S(1)} %copy-done.66), channel_id=1, source_target_pairs={{0,1},{1,0},{2,3},{3,2},{4,5},{5,4},{6,7},{7,6},{8,9},{9,8},{10,11... | collective-permute-start | bytes 1572872 | tf_op jit(solution)/shard_map/ppermute | solution.py:50
  192.4 11.1 %collective-permute-start.56 = (bf16[192,1024]{1,0:T(8,128)(2,1)S(1)}, bf16[192,1024]{1,0:T(8,128)(2,1)S(1)}, u32[]{:S(2)}, u32[]{:S(2)}) collective-permute-start(bf16[192,1024]{1,0:T(8,128)(2,1)S(1)} %pad_maximum_fusion.22), channel_id=1, source_target_pairs={{0,4},{1,5},{4,8},{5,9},{8,12},{9,13},{12,14},{13,15},{14,10},{15,... | collective-permute-start | bytes 1179656 | tf_op jit(solution)/shard_map/ppermute | solution.py:46
  216.7 14.0 %collective-permute-start.64 = (bf16[256,1024]{1,0:T(8,128)(2,1)S(1)}, bf16[256,1024]{1,0:T(8,128)(2,1)S(1)}, u32[]{:S(2)}, u32[]{:S(2)}) collective-permute-start(bf16[256,1024]{1,0:T(8,128)(2,1)S(1)} %add_convert_fusion), channel_id=1, source_target_pairs={{0,16},{16,0},{1,17},{17,1},{2,18},{18,2},{3,19},{19,3},{4,20},{20... | collective-permute-start | bytes 1572872 | tf_op jit(solution)/shard_map/ppermute | solution.py:683
  (107 other events, 589.8 us)

commit v4 on v3

--- a/solution.py
+++ b/solution.py
@@ -720,14 +720,15 @@
             other_half[d] = got[i * piece : (i + 1) * piece]
 
     blocks = column_blocks(chip_there, grad_out, 2 * shard)
-    grad_sib, block_sib, blocks, shard_rows = ring_step(
+    half_mine, half_other = half_rows(w_out_t, replica), half_rows(w_out_t, 1 - replica)
+    grad_sib, block_sib, blocks, half_mine, half_other = ring_step(
         chips,
         [ring],
-        (swap(grad_out, chips), swap(block, chips), blocks, w_out_t),
+        (swap(grad_out, chips), swap(block, chips), blocks, half_mine, half_other),
     )
     grads = (grad_out, grad_sib)
-    proj = Gather(half_rows(shard_rows, replica), chips, piece // 32 * 16)
-    other_half = {0: half_rows(shard_rows, 1 - replica)}
+    proj = Gather(half_mine, chips, piece // 32 * 16)
+    other_half = {0: half_other}
     for s in range(2, half + 1):
         ds = [2 - s, s - 2] if s > 2 else []
         out, got = ring_step(

time: 233 us -> 232 us (level)
    unnamed x148 -> x150, local copies, waits for them, and re-layouts: 7.35 us -> 8.21 us
where the time goes in v4:
time: 232 us; the launch traced here: 231 us
  Pallas kernels  80.6 us (35%)
  waiting for transfers between devices  67.8 us (29%)
  starting transfers between devices  54.9 us (24%)
  other arithmetic  13.9 us (6%)
  local copies, waits for them, and re-layouts  12 us (5%)
    pallas_call x12, Pallas kernels, local_call(): pl.pallas_call(kernel, in_specs=[SMEM] * len(scalars) + [ANY] * len(array...  78.2 us
    ppermute x37, waiting for transfers between devices, shift(): return lax.ppermute(x, 'expert', pairs)  50.6 us
    ppermute x37, starting transfers between devices, shift(): return lax.ppermute(x, 'expert', pairs)  44 us
    ppermute x5, waiting for transfers between devices, partner(): return lax.ppermute(x, 'dp', [(i, (i + 1) % dp) for i in range(dp)])  10.1 us
    unnamed x150, local copies, waits for them, and re-layouts  8.21 us
    ppermute x23, waiting for transfers between devices, swap(): return lax.ppermute(x, 'expert', [(i, i ^ 1) for i in range(2 * chips)])  7.12 us
    ppermute x5, starting transfers between devices, partner(): return lax.ppermute(x, 'dp', [(i, (i + 1) % dp) for i in range(dp)])  6.85 us
  transfers between devices with their start and end apart: 65, of which 32 were waited for; matrix products, arithmetic and copies ran while one was open for 6% of the time, Pallas kernels for 35%

profile of v4, /device:TPU:0, one launch (start us, length us, event | category | flops | bytes accessed | tf_op | source)
XLA Modules:
  0.0 231.2 jit_solution(13144575263957105856)
XLA Ops:
  3.1 2.9 %collective-permute-start.1 = (bf16[144,1024]{1,0:T(8,128)(2,1)S(1)}, bf16[144,1024]{1,0:T(8,128)(2,1)S(1)}, u32[]{:S(2)}, u32[]{:S(2)}) collective-permute-start(bf16[144,1024]{1,0:T(8,128)(2,1)S(1)} %pad_maximum_fusion.24.refs_0_.refs_5_), channel_id=1, source_target_pairs={{0,2},{1,3},{4,0},{5,1},{8,4},{9,5},{12,8},{13,9},{14,12},{15,13},... | collective-permute-start | bytes 884744 | tf_op jit(solution)/shard_map/ppermute | solution.py:46
  7.2 3.0 %column_blocks.1 = (bf16[128,512]{1,0:T(8,128)(2,1)}, bf16[128,512]{1,0:T(8,128)(2,1)}, bf16[128,512]{1,0:T(8,128)(2,1)}, bf16[128,512]{1,0:T(8,128)(2,1)}, bf16...) custom-call(s32[8]{0:T(128)} %get-tuple-element.288.chip_ref, ...), custom_call_target="tpu_custom_call" | custom-call | bytes 2097152 | tf_op jit(solution)/shard_map/column_blocks/pallas_call | solution.py:157
  11.0 2.3 %collective-permute-done.1.refs_4_.refs_9_ = bf16[144,1024]{1,0:T(8,128)(2,1)S(1)} collective-permute-done((bf16[144,1024]{1,0:T(8,128)(2,1)S(1)}, bf16[144,1024]{1,0:T(8,128)(2,1)S(1)}, u32[]{:S(2)}, u32[]{:S(2)}) %collective-permute-start.1) | collective-permute-done | bytes 294944 | tf_op jit(solution)/shard_map/ppermute | solution.py:46
  18.9 8.8 %expert_forward.4 = (bf16[480,2048]{1,0:T(8,128)(2,1)}, f32[480,128]{1,0:T(8,128)}, bf16[128,1024]{1,0:T(8,128)(2,1)}, bf16[128,1024]{1,0:T(8,128)(2,1)}, bf16[1...) custom-call(s32[1]{0:T(128)} %bitcast.2.me_ref, bf16[144,1024]{1,0:T(8,128)(2,1)} %copy-done.37, ...), custom_call_target="tpu_custom_call" | custom-call | flops 4026531840 | bytes 8388608 | tf_op jit(solution)/shard_map/expert_forward/pallas_call | solution.py:157
  27.7 3.4 %collective-permute-done.5.refs_2_.refs_5_.refs_6_ = bf16[272,1024]{1,0:T(8,128)(2,1)S(1)} collective-permute-done((bf16[272,1024]{1,0:T(8,128)(2,1)}, bf16[272,1024]{1,0:T(8,128)(2,1)S(1)}, u32[]{:S(2)}, u32[]{:S(2)}) %collective-permute-start.5) | collective-permute-done | bytes 557088 | tf_op jit(solution)/shard_map/ppermute | solution.py:46
  37.5 7.3 %expert_forward.5 = (bf16[320,2048]{1,0:T(8,128)(2,1)}, f32[320,128]{1,0:T(8,128)}, bf16[128,1024]{1,0:T(8,128)(2,1)}, bf16[128,1024]{1,0:T(8,128)(2,1)}, bf16[256,1024]{1,0:T(8,128)(2,1)}) custom-call(s32[1]{0:T(128)} %bitcast.2.me_ref, bf16[272,1024]{1,0:T(8,128)(2,1)} %copy-done.3, bf16[288,1024]{1,0:T(8,128)(2,1)} %copy-done.13, ...), custom_call_target="tpu_custom_call" | custom-call | flops 2684354560 | bytes 8388608 | tf_op jit(solution)/shard_map/expert_forward/pallas_call | solution.py:157
  44.8 3.6 %collective-permute-done.10 = bf16[256,1024]{1,0:T(8,128)(2,1)S(1)} collective-permute-done((bf16[256,1024]{1,0:T(8,128)(2,1)S(1)}, bf16[256,1024]{1,0:T(8,128)(2,1)S(1)}, u32[]{:S(2)}, u32[]{:S(2)}) %collective-permute-start.10) | collective-permute-done | bytes 524320 | tf_op jit(solution)/shard_map/ppermute | solution.py:683
  53.1 2.8 %collective-permute-start.21 = (bf16[128,512]{1,0:T(8,128)(2,1)}, bf16[128,512]{1,0:T(8,128)(2,1)S(1)}, u32[]{:S(2)}, u32[]{:S(2)}) collective-permute-start(bf16[128,512]{1,0:T(8,128)(2,1)} %get-tuple-element.187), channel_id=1, source_target_pairs={{0,14},{1,15},{4,10},{5,11},{8,6},{9,7},{12,2},{13,3},{14,0},{15,1... | collective-permute-start | bytes 393224 | tf_op jit(solution)/shard_map/ppermute | solution.py:46
  56.8 7.3 %expert_forward.6 = (bf16[320,2048]{1,0:T(8,128)(2,1)}, f32[320,128]{1,0:T(8,128)}, bf16[128,1024]{1,0:T(8,128)(2,1)}, bf16[128,1024]{1,0:T(8,128)(2,1)}, bf16[256,1024]{1,0:T(8,128)(2,1)}) custom-call(s32[1]{0:T(128)} %bitcast.2.me_ref, bf16[272,1024]{1,0:T(8,128)(2,1)} %copy-done.1, bf16[288,1024]{1,0:T(8,128)(2,1)} %copy-done.12, ...), custom_call_target="tpu_custom_call" | custom-call | flops 2684354560 | bytes 8388608 | tf_op jit(solution)/shard_map/expert_forward/pallas_call | solution.py:157
  66.3 4.6 %collective-permute-start.22 = (bf16[128,512]{1,0:T(8,128)(2,1)}, bf16[128,512]{1,0:T(8,128)(2,1)S(1)}, u32[]{:S(2)}, u32[]{:S(2)}) collective-permute-start(bf16[128,512]{1,0:T(8,128)(2,1)} %get-tuple-element.188), channel_id=1, source_target_pairs={{0,10},{1,11},{4,6},{5,7},{8,2},{9,3},{12,0},{13,1},{14,4},{15,5},... | collective-permute-start | bytes 393224 | tf_op jit(solution)/shard_map/ppermute | solution.py:46
  73.8 5.7 %expert_forward.7 = (bf16[160,2048]{1,0:T(8,128)(2,1)}, f32[160,128]{1,0:T(8,128)}, bf16[128,1024]{1,0:T(8,128)(2,1)}, bf16[128,1024]{1,0:T(8,128)(2,1)}) custom-call(s32[1]{0:T(128)} %bitcast.2.me_ref, bf16[192,1024]{1,0:T(8,128)(2,1)} %copy-done.5, bf16[208,1024]{1,0:T(8,128)(2,1)} %copy-done.4, bf16[144,1024]{1,0:T(8,128)(2,1)} %copy-done.18, ...), custom_call_target="tpu_custom_call" | custom-call | flops 1342177280 | bytes 8388608 | tf_op jit(solution)/shard_map/expert_forward/pallas_call | solution.py:157
  79.6 3.0 %collective-permute-start.28 = (bf16[128,512]{1,0:T(8,128)(2,1)S(1)}, bf16[128,512]{1,0:T(8,128)(2,1)S(1)}, u32[]{:S(2)}, u32[]{:S(2)}) collective-permute-start(bf16[128,512]{1,0:T(8,128)(2,1)S(1)} %copy-done.73), channel_id=1, source_target_pairs={{0,6},{1,7},{4,2},{5,3},{8,0},{9,1},{12,4},{13,5},{14,8},{15,9},{1... | collective-permute-start | bytes 393224 | tf_op jit(solution)/shard_map/ppermute | solution.py:46
  89.2 3.2 %collective-permute-done.27.refs_18_ = bf16[128,1024]{1,0:T(8,128)(2,1)S(1)} collective-permute-done((bf16[128,1024]{1,0:T(8,128)(2,1)S(1)}, bf16[128,1024]{1,0:T(8,128)(2,1)S(1)}, u32[]{:S(2)}, u32[]{:S(2)}) %collective-permute-start.27) | collective-permute-done | bytes 262176 | tf_op jit(solution)/shard_map/ppermute | solution.py:683
  93.2 5.3 %grad_combined.1 = (f32[128,1024]{1,0:T(8,128)}, f32[128,1024]{1,0:T(8,128)}) custom-call(s32[16]{0:T(128)} %pad_add_fusion.offsets, bf16[128,4096]{1,0:T(8,128)(2,1)} %refs_0_.1, bf16[128,4096]{1,0:T(8,128)(2,1)} %copy-done.25, bf16[128,1024]{1,0:T(8,128)(2,1)} %copy-done.6, bf16[128,1024]{1,0:T(8,128)(2,1)} %get-tuple-element.198.refs_3_, ...), custom_call_target="tpu_custom_call" | custom-call | flops 1073741824 | bytes 4194304 | tf_op jit(solution)/shard_map/grad_combined/pallas_call | solution.py:157
  99.0 1.8 collective-permute-done.30
  103.6 1.8 collective-permute-done.33.refs_1_
  105.3 9.6 %collective-permute-done.32.refs_4_ = bf16[256,1024]{1,0:T(8,128)(2,1)S(1)} collective-permute-done((bf16[256,1024]{1,0:T(8,128)(2,1)S(1)}, bf16[256,1024]{1,0:T(8,128)(2,1)S(1)}, u32[]{:S(2)}, u32[]{:S(2)}) %collective-permute-start.32) | collective-permute-done | bytes 524320 | tf_op jit(solution)/shard_map/ppermute | solution.py:46
  120.3 8.9 %expert_backward.4 = (bf16[128,1024]{1,0:T(8,128)(2,1)}, bf16[128,1024]{1,0:T(8,128)(2,1)}, bf16[128,1024]{1,0:T(8,128)(2,1)}, bf16[384,1024]{1,0:T(8,128)(2,1)}) custom-call(bf16[128,1024]{1,0:T(8,128)(2,1)} %copy-done.29, bf16[128,1024]{1,0:T(8,128)(2,1)} %copy-done.69, bf16[256,1024]{1,0:T(8,128)(2,1)} %copy-done.36, ...), custom_call_target="tpu_custom_call" | custom-call | flops 4026531840 | bytes 8388608 | tf_op jit(solution)/shard_map/expert_backward/pallas_call | solution.py:157
  129.2 3.4 %collective-permute-done.34.refs_0_ = bf16[256,1024]{1,0:T(8,128)(2,1)S(1)} collective-permute-done((bf16[256,1024]{1,0:T(8,128)(2,1)S(1)}, bf16[256,1024]{1,0:T(8,128)(2,1)S(1)}, u32[]{:S(2)}, u32[]{:S(2)}) %collective-permute-start.34) | collective-permute-done | bytes 524320 | tf_op jit(solution)/shard_map/ppermute | solution.py:46
  134.3 1.8 collective-permute-start.39
  137.2 7.3 %expert_backward.5 = (bf16[128,1024]{1,0:T(8,128)(2,1)}, bf16[128,1024]{1,0:T(8,128)(2,1)}, bf16[256,1024]{1,0:T(8,128)(2,1)}) custom-call(bf16[256,1024]{1,0:T(8,128)(2,1)} %copy-done.14, bf16[256,1024]{1,0:T(8,128)(2,1)} %copy-done.32, bf16[256,1024]{1,0:T(8,128)(2,1)} %copy-done.15, bf16[320,2048]{1,0:T(8,128)(2,1)} %get-tuple-element.224.refs_3_, ...), custom_call_target="tpu_custom_call" | custom-call | flops 2684354560 | bytes 8388608 | tf_op jit(solution)/shard_map/expert_backward/pallas_call | solution.py:157
  144.5 4.1 %collective-permute-done.39.refs_0_ = bf16[256,1024]{1,0:T(8,128)(2,1)S(1)} collective-permute-done((bf16[256,1024]{1,0:T(8,128)(2,1)S(1)}, bf16[256,1024]{1,0:T(8,128)(2,1)S(1)}, u32[]{:S(2)}, u32[]{:S(2)}) %collective-permute-start.39) | collective-permute-done | bytes 524320 | tf_op jit(solution)/shard_map/ppermute | solution.py:46
  154.5 7.3 %expert_backward.6 = (bf16[128,1024]{1,0:T(8,128)(2,1)}, bf16[128,1024]{1,0:T(8,128)(2,1)}, bf16[256,1024]{1,0:T(8,128)(2,1)}) custom-call(bf16[256,1024]{1,0:T(8,128)(2,1)} %copy-done.10, bf16[256,1024]{1,0:T(8,128)(2,1)} %copy-done.31, bf16[256,1024]{1,0:T(8,128)(2,1)} %copy-done.11, bf16[320,2048]{1,0:T(8,128)(2,1)} %get-tuple-element.234.refs_3_, ...), custom_call_target="tpu_custom_call" | custom-call | flops 2684354560 | bytes 8388608 | tf_op jit(solution)/shard_map/expert_backward/pallas_call | solution.py:157
  167.3 6.7 %expert_backward.7 = (bf16[128,1024]{1,0:T(8,128)(2,1)}, bf16[128,1024]{1,0:T(8,128)(2,1)}) custom-call(bf16[192,1024]{1,0:T(8,128)(2,1)} %copy-done.9, bf16[192,1024]{1,0:T(8,128)(2,1)} %copy-done.8, bf16[128,1024]{1,0:T(8,128)(2,1)} %copy-done.42, bf16[160,2048]{1,0:T(8,128)(2,1)} %get-tuple-element.241.refs_3_, f32[160,128]{1,0:T(8,128)} %get-tuple-element.242.refs_4_, ...), custom_call_target="tpu_custom_call" | custom-call | flops 1342177280 | bytes 8388608 | tf_op jit(solution)/shard_map/expert_backward/pallas_call | solution.py:157
  180.2 6.0 %mixed.1 = (bf16[128,2048]{1,0:T(8,128)(2,1)}, bf16[128,2048]{1,0:T(8,128)(2,1)}) custom-call(bf16[128,1024]{1,0:T(8,128)(2,1)} %copy-done.7, bf16[128,1024]{1,0:T(8,128)(2,1)} %copy-done.40, bf16[128,1024]{1,0:T(8,128)(2,1)} %copy-done.6, bf16[128,1024]{1,0:T(8,128)(2,1)} %get-tuple-element.198.refs_3_, bf16[272,1024]{1,0:T(8,128)(2,1)} %copy-done.3, ...), custom_call_target="tpu_custom_call" | custom-call | flops 1073741824 | bytes 4194304 | tf_op jit(solution)/shard_map/mixed/pallas_call | solution.py:157
  186.5 2.7 %collective-permute-done.53.refs_13_ = bf16[192,1024]{1,0:T(8,128)(2,1)S(1)} collective-permute-done((bf16[192,1024]{1,0:T(8,128)(2,1)S(1)}, bf16[192,1024]{1,0:T(8,128)(2,1)S(1)}, u32[]{:S(2)}, u32[]{:S(2)}) %collective-permute-start.53) | collective-permute-done | bytes 393248 | tf_op jit(solution)/shard_map/ppermute | solution.py:46
  193.0 9.0 %collective-permute-done.56.refs_15_ = bf16[192,1024]{1,0:T(8,128)(2,1)S(1)} collective-permute-done((bf16[192,1024]{1,0:T(8,128)(2,1)S(1)}, bf16[192,1024]{1,0:T(8,128)(2,1)S(1)}, u32[]{:S(2)}, u32[]{:S(2)}) %collective-permute-start.56) | collective-permute-done | bytes 393248 | tf_op jit(solution)/shard_map/ppermute | solution.py:46
  205.7 4.6 %weight_grad.1 = (f32[256,1024]{1,0:T(8,128)}, bf16[256,1024]{1,0:T(8,128)(2,1)}) custom-call(s32[1]{0:T(128)} %bitcast.5.core_ref, bf16[128,512]{1,0:T(8,128)(2,1)} %get-tuple-element.263.refs_0_, bf16[128,512]{1,0:T(8,128)(2,1)} %copy-done.61, bf16[128,512]{1,0:T(8,128)(2,1)} %copy-done.60, bf16[128,512]{1,0:T(8,128)(2,1)} %copy-done.59, ...), custom_call_target="tpu_custom_call" | custom-call | flops 1073741824 | bytes 3145728 | tf_op jit(solution)/shard_map/weight_grad/pallas_call | solution.py:157
  211.4 2.3 collective-permute-done.63
  219.6 2.4 %place_columns.1 = bf16[128,4096]{1,0:T(8,128)(2,1)} custom-call(s32[32]{0:T(128)} %pad_add_fusion.1.offsets, bf16[128,2048]{1,0:T(8,128)(2,1)} %get-tuple-element.279.own_ref, bf16[128,2048]{1,0:T(8,128)(2,1)} %copy-done.30), custom_call_target="tpu_custom_call" | custom-call | bytes 2097152 | tf_op jit(solution)/shard_map/place_columns/pallas_call | solution.py:591
  222.0 3.0 %collective-permute-done.62 = bf16[128,1024]{1,0:T(8,128)(2,1)S(1)} collective-permute-done((bf16[128,1024]{1,0:T(8,128)(2,1)S(1)}, bf16[128,1024]{1,0:T(8,128)(2,1)S(1)}, u32[]{:S(2)}, u32[]{:S(2)}) %collective-permute-start.62) | collective-permute-done | bytes 262176 | tf_op jit(solution)/shard_map/ppermute | solution.py:46
  225.8 3.3 %collective-permute-done.64 = bf16[256,1024]{1,0:T(8,128)(2,1)S(1)} collective-permute-done((bf16[256,1024]{1,0:T(8,128)(2,1)S(1)}, bf16[256,1024]{1,0:T(8,128)(2,1)S(1)}, u32[]{:S(2)}, u32[]{:S(2)}) %collective-permute-start.64) | collective-permute-done | bytes 524320 | tf_op jit(solution)/shard_map/ppermute | solution.py:683
  (344 shorter events, 79.9 us)
Async XLA Ops:
  0.6 14.1 %collective-permute-start.2 = (bf16[128,4096]{1,0:T(8,128)(2,1)}, bf16[128,4096]{1,0:T(8,128)(2,1)S(1)}, u32[]{:S(2)}, u32[]{:S(2)}) collective-permute-start(bf16[128,4096]{1,0:T(8,128)(2,1)} %refs_0_.1), channel_id=1, source_target_pairs={{0,1},{1,0},{2,3},{3,2},{4,5},{5,4},{6,7},{7,6},{8,9},{9,8},{10,11... | collective-permute-start | bytes 3145736 | tf_op jit(solution)/shard_map/ppermute | solution.py:50
  16.0 15.1 %collective-permute-start.5 = (bf16[272,1024]{1,0:T(8,128)(2,1)}, bf16[272,1024]{1,0:T(8,128)(2,1)S(1)}, u32[]{:S(2)}, u32[]{:S(2)}) collective-permute-start(bf16[272,1024]{1,0:T(8,128)(2,1)} %get-tuple-element.325), channel_id=1, source_target_pairs={{0,2},{1,3},{4,0},{5,1},{8,4},{9,5},{12,8},{13,9},{14,12},{15,13},... | collective-permute-start | bytes 1671176 | tf_op jit(solution)/shard_map/ppermute | solution.py:46
  17.6 14.6 %collective-permute-start.4 = (bf16[272,1024]{1,0:T(8,128)(2,1)S(1)}, bf16[272,1024]{1,0:T(8,128)(2,1)S(1)}, u32[]{:S(2)}, u32[]{:S(2)}) collective-permute-start(bf16[272,1024]{1,0:T(8,128)(2,1)S(1)} %get-tuple-element.326), channel_id=1, source_target_pairs={{0,4},{1,5},{4,8},{5,9},{8,12},{9,13},{12,14},{13,15},{14,10},{15,... | collective-permute-start | bytes 1671176 | tf_op jit(solution)/shard_map/ppermute | solution.py:46
  33.0 15.3 %collective-permute-start.7 = (bf16[272,1024]{1,0:T(8,128)(2,1)S(1)}, bf16[272,1024]{1,0:T(8,128)(2,1)S(1)}, u32[]{:S(2)}, u32[]{:S(2)}) collective-permute-start(bf16[272,1024]{1,0:T(8,128)(2,1)S(1)} %collective-permute-done.4.refs_0_.refs_3_.refs_4_), channel_id=1, source_target_pairs={{0,4},{1,5},{4,8},{5,9},{8,12},{9,13},{12,14},{13,15},{14,10},{15,... | collective-permute-start | bytes 1671176 | tf_op jit(solution)/shard_map/ppermute | solution.py:46
  33.5 14.9 %collective-permute-start.8 = (bf16[272,1024]{1,0:T(8,128)(2,1)S(1)}, bf16[272,1024]{1,0:T(8,128)(2,1)S(1)}, u32[]{:S(2)}, u32[]{:S(2)}) collective-permute-start(bf16[272,1024]{1,0:T(8,128)(2,1)S(1)} %collective-permute-done.5.refs_2_.refs_5_.refs_6_), channel_id=1, source_target_pairs={{0,2},{1,3},{4,0},{5,1},{8,4},{9,5},{12,8},{13,9},{14,12},{15,13},... | collective-permute-start | bytes 1671176 | tf_op jit(solution)/shard_map/ppermute | solution.py:46
  35.1 13.3 %collective-permute-start.10 = (bf16[256,1024]{1,0:T(8,128)(2,1)S(1)}, bf16[256,1024]{1,0:T(8,128)(2,1)S(1)}, u32[]{:S(2)}, u32[]{:S(2)}) collective-permute-start(bf16[256,1024]{1,0:T(8,128)(2,1)S(1)} %pad_maximum_fusion.11), channel_id=1, source_target_pairs={{0,16},{16,0},{1,17},{17,1},{2,18},{18,2},{3,19},{19,3},{4,20},{20... | collective-permute-start | bytes 1572872 | tf_op jit(solution)/shard_map/ppermute | solution.py:683
  48.7 15.4 %collective-permute-start.15 = (bf16[256,1024]{1,0:T(8,128)(2,1)S(1)}, bf16[256,1024]{1,0:T(8,128)(2,1)S(1)}, u32[]{:S(2)}, u32[]{:S(2)}) collective-permute-start(bf16[256,1024]{1,0:T(8,128)(2,1)S(1)} %pad_maximum_fusion.12), channel_id=1, source_target_pairs={{0,16},{16,0},{1,17},{17,1},{2,18},{18,2},{3,19},{19,3},{4,20},{20... | collective-permute-start | bytes 1572872 | tf_op jit(solution)/shard_map/ppermute | solution.py:683
  50.3 13.8 %collective-permute-start.13 = (bf16[208,1024]{1,0:T(8,128)(2,1)S(1)}, bf16[208,1024]{1,0:T(8,128)(2,1)S(1)}, u32[]{:S(2)}, u32[]{:S(2)}) collective-permute-start(bf16[208,1024]{1,0:T(8,128)(2,1)S(1)} %concatenate.120), channel_id=1, source_target_pairs={{0,2},{1,3},{4,0},{5,1},{8,4},{9,5},{12,8},{13,9},{14,12},{15,13},... | collective-permute-start | bytes 1277960 | tf_op jit(solution)/shard_map/ppermute | solution.py:46
  52.7 11.4 %collective-permute-start.12 = (bf16[192,1024]{1,0:T(8,128)(2,1)}, bf16[192,1024]{1,0:T(8,128)(2,1)S(1)}, u32[]{:S(2)}, u32[]{:S(2)}) collective-permute-start(bf16[192,1024]{1,0:T(8,128)(2,1)} %pad_maximum_fusion.19), channel_id=1, source_target_pairs={{0,4},{1,5},{4,8},{5,9},{8,12},{9,13},{12,14},{13,15},{14,10},{15,... | collective-permute-start | bytes 1179656 | tf_op jit(solution)/shard_map/ppermute | solution.py:46
  53.1 17.7 %collective-permute-start.21 = (bf16[128,512]{1,0:T(8,128)(2,1)}, bf16[128,512]{1,0:T(8,128)(2,1)S(1)}, u32[]{:S(2)}, u32[]{:S(2)}) collective-permute-start(bf16[128,512]{1,0:T(8,128)(2,1)} %get-tuple-element.187), channel_id=1, source_target_pairs={{0,14},{1,15},{4,10},{5,11},{8,6},{9,7},{12,2},{13,3},{14,0},{15,1... | collective-permute-start | bytes 393224 | tf_op jit(solution)/shard_map/ppermute | solution.py:46
  65.0 17.7 %collective-permute-start.20 = (bf16[256,1024]{1,0:T(8,128)(2,1)S(1)}, bf16[256,1024]{1,0:T(8,128)(2,1)S(1)}, u32[]{:S(2)}, u32[]{:S(2)}) collective-permute-start(bf16[256,1024]{1,0:T(8,128)(2,1)S(1)} %pad_maximum_fusion.13), channel_id=1, source_target_pairs={{0,16},{16,0},{1,17},{17,1},{2,18},{18,2},{3,19},{19,3},{4,20},{20... | collective-permute-start | bytes 1572872 | tf_op jit(solution)/shard_map/ppermute | solution.py:683
  66.3 13.3 %collective-permute-start.22 = (bf16[128,512]{1,0:T(8,128)(2,1)}, bf16[128,512]{1,0:T(8,128)(2,1)S(1)}, u32[]{:S(2)}, u32[]{:S(2)}) collective-permute-start(bf16[128,512]{1,0:T(8,128)(2,1)} %get-tuple-element.188), channel_id=1, source_target_pairs={{0,10},{1,11},{4,6},{5,7},{8,2},{9,3},{12,0},{13,1},{14,4},{15,5},... | collective-permute-start | bytes 393224 | tf_op jit(solution)/shard_map/ppermute | solution.py:46
  70.8 11.7 %collective-permute-start.23 = (bf16[128,512]{1,0:T(8,128)(2,1)S(1)}, bf16[128,512]{1,0:T(8,128)(2,1)S(1)}, u32[]{:S(2)}, u32[]{:S(2)}) collective-permute-start(bf16[128,512]{1,0:T(8,128)(2,1)S(1)} %copy-done.74), channel_id=1, source_target_pairs={{0,12},{1,13},{4,14},{5,15},{8,10},{9,11},{12,6},{13,7},{14,2},{15... | collective-permute-start | bytes 393224 | tf_op jit(solution)/shard_map/ppermute | solution.py:46
  70.9 11.7 %collective-permute-start.18 = (bf16[64,1024]{1,0:T(8,128)(2,1)S(1)}, bf16[64,1024]{1,0:T(8,128)(2,1)S(1)}, u32[]{:S(2)}, u32[]{:S(2)}) collective-permute-start(bf16[64,1024]{1,0:T(8,128)(2,1)S(1)} %slice.254), channel_id=1, source_target_pairs={{0,2},{1,3},{4,0},{5,1},{8,4},{9,5},{12,8},{13,9},{14,12},{15,13},... | collective-permute-start | bytes 393224 | tf_op jit(solution)/shard_map/ppermute | solution.py:46
  82.6 16.0 %collective-permute-start.16 = (bf16[256,1024]{1,0:T(8,128)(2,1)}, bf16[256,1024]{1,0:T(8,128)(2,1)S(1)}, u32[]{:S(2)}, u32[]{:S(2)}) collective-permute-start(bf16[256,1024]{1,0:T(8,128)(2,1)} %get-tuple-element.180), channel_id=1, source_target_pairs={{0,1},{1,0},{2,3},{3,2},{4,5},{5,4},{6,7},{7,6},{8,9},{9,8},{10,11... | collective-permute-start | bytes 1572872 | tf_op jit(solution)/shard_map/ppermute | solution.py:50
  101.0 14.0 %collective-permute-start.32 = (bf16[256,1024]{1,0:T(8,128)(2,1)S(1)}, bf16[256,1024]{1,0:T(8,128)(2,1)S(1)}, u32[]{:S(2)}, u32[]{:S(2)}) collective-permute-start(bf16[256,1024]{1,0:T(8,128)(2,1)S(1)} %get-tuple-element.321), channel_id=1, source_target_pairs={{0,2},{1,3},{4,0},{5,1},{8,4},{9,5},{12,8},{13,9},{14,12},{15,13},... | collective-permute-start | bytes 1572872 | tf_op jit(solution)/shard_map/ppermute | solution.py:46
  102.7 13.7 %collective-permute-start.31 = (bf16[256,1024]{1,0:T(8,128)(2,1)S(1)}, bf16[256,1024]{1,0:T(8,128)(2,1)S(1)}, u32[]{:S(2)}, u32[]{:S(2)}) collective-permute-start(bf16[256,1024]{1,0:T(8,128)(2,1)S(1)} %get-tuple-element.322), channel_id=1, source_target_pairs={{0,4},{1,5},{4,8},{5,9},{8,12},{9,13},{12,14},{13,15},{14,10},{15,... | collective-permute-start | bytes 1572872 | tf_op jit(solution)/shard_map/ppermute | solution.py:46
  103.0 13.4 %collective-permute-start.11 = (bf16[256,1024]{1,0:T(8,128)(2,1)S(1)}, bf16[256,1024]{1,0:T(8,128)(2,1)S(1)}, u32[]{:S(2)}, u32[]{:S(2)}) collective-permute-start(bf16[256,1024]{1,0:T(8,128)(2,1)S(1)} %copy-done.66), channel_id=1, source_target_pairs={{0,1},{1,0},{2,3},{3,2},{4,5},{5,4},{6,7},{7,6},{8,9},{9,8},{10,11... | collective-permute-start | bytes 1572872 | tf_op jit(solution)/shard_map/ppermute | solution.py:50
  118.3 15.1 %collective-permute-start.38 = (bf16[384,1024]{1,0:T(8,128)(2,1)S(1)}, bf16[384,1024]{1,0:T(8,128)(2,1)S(1)}, u32[]{:S(2)}, u32[]{:S(2)}) collective-permute-start(bf16[384,1024]{1,0:T(8,128)(2,1)S(1)} %copy-done.63), channel_id=1, source_target_pairs={{0,1},{1,0},{2,3},{3,2},{4,5},{5,4},{6,7},{7,6},{8,9},{9,8},{10,11... | collective-permute-start | bytes 2359304 | tf_op jit(solution)/shard_map/ppermute | solution.py:50
  118.3 14.3 %collective-permute-start.34 = (bf16[256,1024]{1,0:T(8,128)(2,1)S(1)}, bf16[256,1024]{1,0:T(8,128)(2,1)S(1)}, u32[]{:S(2)}, u32[]{:S(2)}) collective-permute-start(bf16[256,1024]{1,0:T(8,128)(2,1)S(1)} %get-tuple-element.319), channel_id=1, source_target_pairs={{0,4},{1,5},{4,8},{5,9},{8,12},{9,13},{12,14},{13,15},{14,10},{15,... | collective-permute-start | bytes 1572872 | tf_op jit(solution)/shard_map/ppermute | solution.py:46
  119.2 14.1 %collective-permute-start.35 = (bf16[256,1024]{1,0:T(8,128)(2,1)S(1)}, bf16[256,1024]{1,0:T(8,128)(2,1)S(1)}, u32[]{:S(2)}, u32[]{:S(2)}) collective-permute-start(bf16[256,1024]{1,0:T(8,128)(2,1)S(1)} %get-tuple-element.320), channel_id=1, source_target_pairs={{0,2},{1,3},{4,0},{5,1},{8,4},{9,5},{12,8},{13,9},{14,12},{15,13},... | collective-permute-start | bytes 1572872 | tf_op jit(solution)/shard_map/ppermute | solution.py:46
  134.3 14.3 %collective-permute-start.39 = (bf16[256,1024]{1,0:T(8,128)(2,1)S(1)}, bf16[256,1024]{1,0:T(8,128)(2,1)S(1)}, u32[]{:S(2)}, u32[]{:S(2)}) collective-permute-start(bf16[256,1024]{1,0:T(8,128)(2,1)S(1)} %get-tuple-element.316), channel_id=1, source_target_pairs={{0,4},{1,5},{4,8},{5,9},{8,12},{9,13},{12,14},{13,15},{14,10},{15,... | collective-permute-start | bytes 1572872 | tf_op jit(solution)/shard_map/ppermute | solution.py:46
  136.1 14.0 %collective-permute-start.40 = (bf16[256,1024]{1,0:T(8,128)(2,1)S(1)}, bf16[256,1024]{1,0:T(8,128)(2,1)S(1)}, u32[]{:S(2)}, u32[]{:S(2)}) collective-permute-start(bf16[256,1024]{1,0:T(8,128)(2,1)S(1)} %get-tuple-element.317), channel_id=1, source_target_pairs={{0,2},{1,3},{4,0},{5,1},{8,4},{9,5},{12,8},{13,9},{14,12},{15,13},... | collective-permute-start | bytes 1572872 | tf_op jit(solution)/shard_map/ppermute | solution.py:46
  162.6 12.4 %collective-permute-start.51 = (bf16[128,1024]{1,0:T(8,128)(2,1)S(1)}, bf16[128,1024]{1,0:T(8,128)(2,1)S(1)}, u32[]{:S(2)}, u32[]{:S(2)}) collective-permute-start(bf16[128,1024]{1,0:T(8,128)(2,1)S(1)} %add_convert_fusion.7.refs_0_.refs_8_), channel_id=1, source_target_pairs={{0,1},{1,0},{2,3},{3,2},{4,5},{5,4},{6,7},{7,6},{8,9},{9,8},{10,11... | collective-permute-start | bytes 786440 | tf_op jit(solution)/shard_map/ppermute | solution.py:50
  163.2 11.9 %collective-permute-start.47 = (bf16[128,1024]{1,0:T(8,128)(2,1)S(1)}, bf16[128,1024]{1,0:T(8,128)(2,1)S(1)}, u32[]{:S(2)}, u32[]{:S(2)}) collective-permute-start(bf16[128,1024]{1,0:T(8,128)(2,1)S(1)} %slice.292), channel_id=1, source_target_pairs={{0,2},{1,3},{4,0},{5,1},{8,4},{9,5},{12,8},{13,9},{14,12},{15,13},... | collective-permute-start | bytes 786440 | tf_op jit(solution)/shard_map/ppermute | solution.py:46
  175.1 11.1 %collective-permute-start.55 = (bf16[256,1024]{1,0:T(8,128)(2,1)}, bf16[256,1024]{1,0:T(8,128)(2,1)S(1)}, u32[]{:S(2)}, u32[]{:S(2)}) collective-permute-start(bf16[256,1024]{1,0:T(8,128)(2,1)} %get-tuple-element.256), channel_id=1, source_target_pairs={{0,1},{1,0},{2,3},{3,2},{4,5},{5,4},{6,7},{7,6},{8,9},{9,8},{10,11... | collective-permute-start | bytes 1572872 | tf_op jit(solution)/shard_map/ppermute | solution.py:50
  178.0 11.2 %collective-permute-start.53 = (bf16[192,1024]{1,0:T(8,128)(2,1)S(1)}, bf16[192,1024]{1,0:T(8,128)(2,1)S(1)}, u32[]{:S(2)}, u32[]{:S(2)}) collective-permute-start(bf16[192,1024]{1,0:T(8,128)(2,1)S(1)} %pad_maximum_fusion.20), channel_id=1, source_target_pairs={{0,4},{1,5},{4,8},{5,9},{8,12},{9,13},{12,14},{13,15},{14,10},{15,... | collective-permute-start | bytes 1179656 | tf_op jit(solution)/shard_map/ppermute | solution.py:46
  179.2 10.9 %collective-permute-start.54 = (bf16[192,1024]{1,0:T(8,128)(2,1)S(1)}, bf16[192,1024]{1,0:T(8,128)(2,1)S(1)}, u32[]{:S(2)}, u32[]{:S(2)}) collective-permute-start(bf16[192,1024]{1,0:T(8,128)(2,1)S(1)} %pad_maximum_fusion.21), channel_id=1, source_target_pairs={{0,2},{1,3},{4,0},{5,1},{8,4},{9,5},{12,8},{13,9},{14,12},{15,13},... | collective-permute-start | bytes 1179656 | tf_op jit(solution)/shard_map/ppermute | solution.py:46
  180.2 23.1 %collective-permute-start.42 = (bf16[256,1024]{1,0:T(8,128)(2,1)}, bf16[256,1024]{1,0:T(8,128)(2,1)S(1)}, u32[]{:S(2)}, u32[]{:S(2)}) collective-permute-start(bf16[256,1024]{1,0:T(8,128)(2,1)} %get-tuple-element.230), channel_id=1, source_target_pairs={{0,1},{1,0},{2,3},{3,2},{4,5},{5,4},{6,7},{7,6},{8,9},{9,8},{10,11... | collective-permute-start | bytes 1572872 | tf_op jit(solution)/shard_map/ppermute | solution.py:50
  190.2 13.1 %collective-permute-start.58 = (bf16[128,2048]{1,0:T(8,128)(2,1)S(1)}, bf16[128,2048]{1,0:T(8,128)(2,1)S(1)}, u32[]{:S(2)}, u32[]{:S(2)}) collective-permute-start(bf16[128,2048]{1,0:T(8,128)(2,1)S(1)} %copy-done.67), channel_id=1, source_target_pairs={{0,1},{1,0},{2,3},{3,2},{4,5},{5,4},{6,7},{7,6},{8,9},{9,8},{10,11... | collective-permute-start | bytes 1572872 | tf_op jit(solution)/shard_map/ppermute | solution.py:50
  190.8 11.1 %collective-permute-start.56 = (bf16[192,1024]{1,0:T(8,128)(2,1)S(1)}, bf16[192,1024]{1,0:T(8,128)(2,1)S(1)}, u32[]{:S(2)}, u32[]{:S(2)}) collective-permute-start(bf16[192,1024]{1,0:T(8,128)(2,1)S(1)} %pad_maximum_fusion.22), channel_id=1, source_target_pairs={{0,4},{1,5},{4,8},{5,9},{8,12},{9,13},{12,14},{13,15},{14,10},{15,... | collective-permute-start | bytes 1179656 | tf_op jit(solution)/shard_map/ppermute | solution.py:46
  215.1 14.0 %collective-permute-start.64 = (bf16[256,1024]{1,0:T(8,128)(2,1)S(1)}, bf16[256,1024]{1,0:T(8,128)(2,1)S(1)}, u32[]{:S(2)}, u32[]{:S(2)}) collective-permute-start(bf16[256,1024]{1,0:T(8,128)(2,1)S(1)} %add_convert_fusion), channel_id=1, source_target_pairs={{0,16},{16,0},{1,17},{17,1},{2,18},{18,2},{3,19},{19,3},{4,20},{20... | collective-permute-start | bytes 1572872 | tf_op jit(solution)/shard_map/ppermute | solution.py:683
  (108 other events, 572.8 us)
